TPU v7x, 32 devices: a whole 2x2x4 slice. The times are simulated.
32 devices in a mesh: blk: 8 (over z, x), uly: 4 (over y, core).
Axes of the slice: x: 2, y: 2, z: 4, core: 2. Of those that a mesh axis runs over, the one named last changes fastest.
Arguments:
- tokens: bfloat16 [768, 2560], P(('blk', 'uly')), may hold values from -6 to 6
- in_bits: int32 [768, 2560], P(('blk', 'uly')), may hold values from 0 to 1
- qkv_weights: bfloat16 [2, 3, 2560, 2560], P(None, None, 'blk', 'uly'), may hold values from -0.125 to 0.125
- qkv_bits: int32 [768, 3, 2560], P('blk', None, 'uly'), may hold values from 0 to 1
- gain_query: float32 [2560], P('uly'), may hold values from 0.7 to 1.8
- gain_key: float32 [2560], P('uly'), may hold values from 0.7 to 1.8
- out_weights: bfloat16 [2, 2560, 2560], P(None, 'uly', 'blk'), may hold values from -0.5 to 0.5
- mix_bits: int32 [768, 2560], P('blk', 'uly'), may hold values from 0 to 1
- out_bits: int32 [768, 2560], P('blk'), may hold values from 0 to 1
Outputs:
- layer_output: bfloat16 [768, 2560], P(('blk', 'uly'))
Inputs may be any that keep to these rules, and one draw needn't show every extreme that they name: `in_bits`: a bit of 1 stands for the sign +1, a bit of 0 for -1. `qkv_bits`: a bit of 1 stands for the sign +1, a bit of 0 for -1. `mix_bits`: a bit of 1 stands for the sign +1, a bit of 0 for -1. `out_bits`: a bit of 1 stands for the sign +1, a bit of 0 for -1.
All inputs are finite; a program needn't handle non-finite values.
Results may differ from a plain program's by a relative error of at most 0.018.
Values may be sent and summed in bfloat16 or wider, within the bound.
No kernel may reach another device: no remote copies, remote signals or barrier semaphores. Data moves between devices by JAX's collectives and lax.ppermute only.
A program may use at most 128 MiB of HBM per device.

v0:
```python
import functools
import math

import jax
import jax.numpy as jnp
from jax import lax
from jax.experimental import pallas as pl
from jax.experimental.pallas import tpu as pltpu
from jax.sharding import PartitionSpec as P

HEAD = 128


epsilon = 1e-06


def signed(bit_values):
    return (2 * bit_values - 1).astype(jnp.float32)


def normalize(values, gain_vector):
    row_count = values.shape[0]
    by_head = values.astype(jnp.float32).reshape(row_count, -1, HEAD)
    inverse_rms = lax.rsqrt(jnp.mean(by_head * by_head, axis=-1, keepdims=True) + epsilon)
    return (by_head * inverse_rms * gain_vector.reshape(-1, HEAD)).astype(jnp.bfloat16)


def gather_plan(
    tokens, in_bits, qkv_weights, qkv_bits, gain_query, gain_key, out_weights, mix_bits, out_bits
):
    flipped = (tokens.astype(jnp.float32) * signed(in_bits)).astype(jnp.bfloat16)
    group_rows = lax.all_gather(jnp.stack([tokens, flipped]), "uly", axis=1, tiled=True)
    row_total = group_rows.shape[1]
    projections = jnp.einsum(
        "mrd,mkdc->rmkc",
        group_rows,
        lax.all_gather(qkv_weights, "blk", axis=2, tiled=True),
        preferred_element_type=jnp.float32,
    )
    projected = (projections[:, 0] + signed(qkv_bits) * projections[:, 1]).astype(jnp.bfloat16)
    queries = normalize(projected[:, 0], gain_query)
    head_count = queries.shape[1]
    keys_normed = normalize(projected[:, 1], gain_key).reshape(row_total, -1)
    values_block = projected[:, 2]
    score_scale = 1.0 / math.sqrt(HEAD)

    def attend(running, shard_piece):
        numerator, denominator = running
        key_rows = shard_piece[0].reshape(shard_piece[0].shape[0], head_count, HEAD)
        value_rows = shard_piece[1].reshape(shard_piece[1].shape[0], head_count, HEAD)
        scores = (
            jnp.einsum("rhd,nhd->hrn", queries, key_rows, preferred_element_type=jnp.float32)
            * score_scale
        )
        weights = jnp.exp(scores).astype(jnp.bfloat16)
        numerator = numerator + jnp.einsum(
            "hrn,nhd->rhd", weights, value_rows, preferred_element_type=jnp.float32
        )
        denominator = denominator + jnp.sum(weights.astype(jnp.float32), axis=2).T
        return (numerator, denominator)

    start_state = (
        jnp.zeros((row_total, head_count, HEAD), jnp.float32),
        jnp.zeros((row_total, head_count), jnp.float32),
    )
    all_keys, all_values = (
        lax.all_gather(keys_normed, "blk", axis=0, tiled=True),
        lax.all_gather(values_block, "blk", axis=0, tiled=True),
    )
    group_count = lax.axis_size("blk")
    per_block = 1
    while per_block * row_total < 512 and group_count % (per_block * 2) == 0:
        per_block = per_block * 2
    block_rows = per_block * row_total
    block_count = group_count // per_block
    key_blocks = all_keys.reshape(block_count, block_rows, all_keys.shape[1])
    value_blocks = all_values.reshape(block_count, block_rows, all_values.shape[1])

    def scan_step(running, block_pair):
        return (attend(running, block_pair), None)

    (numerator, denominator), unused = lax.scan(scan_step, start_state, (key_blocks, value_blocks))
    attended = (numerator / denominator[:, :, None]).astype(jnp.bfloat16).reshape(row_total, -1)
    attended_flipped = (attended.astype(jnp.float32) * signed(mix_bits)).astype(jnp.bfloat16)
    attended_pair = jnp.stack([attended, attended_flipped])
    out_signs = signed(out_bits)
    partial_out = jnp.einsum(
        "mrc,mcn->rmn",
        attended_pair,
        lax.all_gather(out_weights, "blk", axis=2, tiled=True),
        preferred_element_type=jnp.float32,
    )
    summed = lax.psum_scatter(
        partial_out.astype(jnp.bfloat16), "uly", scatter_dimension=0, tiled=True
    ).astype(jnp.float32)
    own_rows = summed.shape[0]
    own_signs = lax.dynamic_slice_in_dim(out_signs, lax.axis_index("uly") * own_rows, own_rows, 0)
    result_rows = summed[:, 0] + own_signs * summed[:, 1]
    return result_rows.astype(jnp.bfloat16)


def dot32(a, b):
    return lax.dot_general(
        a, b, (((1,), (0,)), ((), ())), preferred_element_type=jnp.float32
    )


def dot32_t(a, b):
    return lax.dot_general(
        a, b, (((1,), (1,)), ((), ())), preferred_element_type=jnp.float32
    )


bf = jnp.bfloat16
VMEM = pl.BlockSpec(memory_space=pltpu.VMEM)
SMEM = pl.BlockSpec(memory_space=pltpu.SMEM)
ANY = pl.BlockSpec(memory_space=pl.ANY)


def call(kernel, outs, out_specs, in_specs, scratch=(), flops=0, moved=0):
    return pl.pallas_call(
        kernel,
        out_shape=outs,
        in_specs=in_specs,
        out_specs=out_specs,
        scratch_shapes=list(scratch),
        compiler_params=pltpu.CompilerParams(vmem_limit_bytes=40 * 1024 * 1024),
        cost_estimate=pl.CostEstimate(flops=flops, bytes_accessed=moved, transcendentals=0),
    )


def shape(*dims, dtype=bf):
    return jax.ShapeDtypeStruct(dims, dtype)


def lanes(index, size):
    return pl.ds(pl.multiple_of(index * size, 128), size)


def copy_kernel(first, count, weights, out, sems):
    copies = [
        pltpu.make_async_copy(weights.at[m, pl.ds(first, count)], out.at[m], sems.at[m])
        for m in (0, 1)
    ]
    for copy in copies:
        copy.start()
    for copy in copies:
        copy.wait()


def sign_pieces(bits, u, team):
    piece = bits.shape[0] // team
    parts = [bits[pl.ds(pl.multiple_of((u ^ r) * piece, 8), piece), :] for r in range(team)]
    return [(2 * part - 1).astype(jnp.float32) for part in parts]


def prepare_kernel(team, place, tokens, in_bits, sign_bits, *blocks):
    wide = tokens.shape[1] // len(blocks)
    for k, block in enumerate(blocks):
        cut = lanes(place[0] ^ k, wide)
        plain = tokens[:, cut]
        sign = (2 * in_bits[:, cut] - 1).astype(jnp.float32)
        block[0] = plain
        block[1] = (plain.astype(jnp.float32) * sign).astype(bf)
    for i, part in enumerate((1, 2, 0)):
        for r, piece in enumerate(sign_pieces(sign_bits.at[part], place[2], team)):
            blocks[2][2 + team * i + r] = piece.astype(bf)


def late_signs_kernel(team, place, out_bits, mix_bits, weights, query_weights, out, near, far, sems):
    copies = [
        pltpu.make_async_copy(weights.at[m, 0], query_weights.at[m], sems.at[m]) for m in (0, 1)
    ]
    for copy in copies:
        copy.start()
    z, u = place[0], place[2]
    own_rows, wide = out.shape[1:]

    def fill(target, start, k):
        for i, r in enumerate((0, 2)):
            rows = pl.ds(pl.multiple_of((u ^ r) * own_rows, 8), own_rows)
            bits = out_bits[rows, lanes(z ^ k, wide)]
            target[start + i] = (2 * bits - 1).astype(jnp.float32).astype(bf)

    fill(out, 0, 0)
    for r, part in enumerate(sign_pieces(mix_bits, u, team)):
        near[r] = part.astype(bf)
        far[r] = part.astype(bf)
    fill(near, team, 1)
    fill(far, team, 2)
    fill(far, team + 2, 3)
    for copy in copies:
        copy.wait()


def near_kernel(near, far, out):
    team = near.shape[0] - 2
    out[:team] = near[:team]
    out[team : 2 * team] = far[:team]
    out[2 * team : 2 * team + 2] = near[team:]
    out[2 * team + 2 :] = far[team + 2 :]


def late_kernel(place, own, near, far, got, mix, out):
    team, own_rows = near.shape[0] - 2, near.shape[1]
    size = team * own_rows
    out[0] = own[...]
    out[1] = got[2 * team : 2 * team + 2]
    out[2] = far[team : team + 2]
    out[3] = got[2 * team + 2 :]
    for j, (ref, start) in enumerate(((near, 0), (got, 0), (far, 0), (got, team))):
        cut = slice(j * size, (j + 1) * size)
        for k in range(5):
            head = lanes(place[0] ^ k, HEAD) if k < 4 else slice(4 * HEAD, None)
            parts = [ref[start + r, :, head].astype(jnp.float32) for r in range(team)]
            mix[cut, k * HEAD : (k + 1) * HEAD] = jnp.concatenate(parts, axis=0).astype(bf)


def stack_kernel(*refs):
    for k, ref in enumerate(refs[:-1]):
        refs[-1][k] = ref[: refs[-1].shape[1]]


def pair_kernel(own, taken, out):
    out[0] = own[...]
    out[1] = taken[...]


def sign_pair_kernel(first, own, taken, out):
    team = (own.shape[0] - 2) // 3
    for b, ref in enumerate((own, taken)):
        for i in range(out.shape[1]):
            at = 2 + team * (first + i)
            pieces = [ref[at + r].astype(jnp.float32) for r in range(team)]
            out[b, i] = jnp.concatenate(pieces, axis=0).astype(bf)


def rows_kernel(own, taken, rows):
    depth, kinds, piece = own.shape[1:4]
    for m in range(kinds):
        for j in range(depth):
            parts = [ref[y, j, m].astype(jnp.float32) for y in (0, 1) for ref in (own, taken)]
            at = j * 4 * piece
            rows[m, at : at + 4 * piece] = jnp.concatenate(parts, axis=0).astype(bf)


def project_kernel(
    parts, size, place, rows, weights, partner, signs_02, signs_13,
    send, keep_own, keep_two, held, total, sems,
):
    z, x = place[0], place[1]
    slab = weights.shape[2]
    own = pl.ds(pl.multiple_of(x * slab, 64), slab)
    other = pl.ds(pl.multiple_of((1 - x) * slab, 64), slab)
    depth = rows.shape[1] // size
    half = depth * size
    copies = []
    for i, part in enumerate(parts):
        for m in (0, 1):
            near, far = weights.at[m, part], partner.at[m, i]
            copies.append(pltpu.make_async_copy(near, held.at[i, m, own], sems.at[i, m, 0]))
            copies.append(pltpu.make_async_copy(far, held.at[i, m, other], sems.at[i, m, 1]))
    for copy in copies:
        copy.start()

    def block(j, head):
        return total[j * size : (j + 1) * size, lanes(head, HEAD)]

    def main(target, start, k):
        for j in range(depth):
            at = start + (j ^ k) * size
            target[at : at + size] = block(j, z ^ k).astype(target.dtype)

    def rest(target, start, j):
        target[start : start + size] = block(j, depth).astype(target.dtype)

    for i, part in enumerate(parts):
        for copy in copies[4 * i : 4 * i + 4]:
            copy.wait()
        total[...] = dot32(rows[1], held[i, 1])
        plain = dot32(rows[0], held[i, 0])
        signs = (signs_02[0, i], signs_13[0, i], signs_02[1, i], signs_13[1, i])
        for j in range(depth):
            cut = slice(j * size, (j + 1) * size)
            total[cut] = plain[cut] + signs[j].astype(jnp.float32) * total[cut]
        if part:
            main(send, 3 * half * i, 1)
            main(send, 3 * half * i + half, 3)
            main(keep_own, 2 * half * i, 0)
            main(keep_two, half * i, 2)
            for j in range(depth):
                rest(send, 3 * half * i + 2 * half + (j ^ 1) * size, j)
                rest(keep_own, 2 * half * i + half + j * size, j)
        else:
            main(send, 0, 1)
            rest(send, half, 1)
            main(send, half + size, 3)
            rest(send, 2 * half + size, 3)
            main(keep_own, 0, 0)
            rest(keep_own, half, 0)
            main(keep_two, 0, 2)
            rest(keep_two, half, 2)


def middle_kernel(size, keep_own, keep_two, taken, send, total):
    count = keep_two.shape[0]
    if keep_own.shape[0] == count:
        total[...] = keep_own[...] + taken[:count].astype(jnp.float32)
        send[...] = (keep_two[...] + taken[count:].astype(jnp.float32)).astype(bf)
        return
    half = count // 2
    for i in (0, 1):
        base, got = 2 * half * i, 3 * half * i
        first = slice(base, base + half)
        total[first] = keep_own[first] + taken[got : got + half].astype(jnp.float32)
        far = keep_two[half * i : half * i + half]
        send[first] = (far + taken[got + half : got + 2 * half].astype(jnp.float32)).astype(bf)
        for j in range(half // size):
            cut = slice(base + half + j * size, base + half + (j + 1) * size)
            at = got + 2 * half + j * size
            value = keep_own[cut] + taken[at : at + size].astype(jnp.float32)
            total[cut] = value
            at = base + half + (j ^ 2) * size
            send[at : at + size] = value.astype(bf)


def norm_rows(values, gain_row):
    wide = values.astype(jnp.float32)
    inverse_rms = lax.rsqrt(jnp.mean(wide * wide, axis=-1, keepdims=True) + epsilon)
    return (wide * inverse_rms * gain_row).astype(bf)


def key_value_kernel(half, place, total, taken, gain, out):
    keep = (total[...] + taken[...].astype(jnp.float32)).astype(bf)
    heads = gain.shape[0]
    out[:half] = norm_rows(keep[:half], gain[pl.ds(place[0], 1), :])
    out[half : 2 * half] = norm_rows(keep[half : 2 * half], gain[heads - 1 : heads, :])
    out[2 * half :] = keep[2 * half :]


def attend_kernel(half, place, total, taken, gain, own, partner, out):
    keep = (total[...] + taken[...].astype(jnp.float32)).astype(bf)
    heads = gain.shape[0]

    def attend(queries, cut):
        score_scale = 1.0 / math.sqrt(HEAD)
        totals, sums = 0.0, 0.0
        for both in (own, partner):
            scores = dot32_t(queries, both[cut]) * score_scale
            weights = jnp.exp(scores).astype(bf)
            totals = totals + jnp.sum(weights.astype(jnp.float32), axis=1, keepdims=True)
            sums = sums + dot32(weights, both[2 * half + cut.start : 2 * half + cut.stop])
        return (sums / totals).astype(bf)

    first = norm_rows(keep[:half], gain[pl.ds(place[0], 1), :])
    out[:half] = attend(first, slice(0, half))
    last = norm_rows(keep[half:], gain[heads - 1 : heads, :])
    out[half:] = attend(last, slice(half, 2 * half))


def core_kernel(own, taken, signs, kept, sent):
    for i, target in enumerate((kept, sent)):
        for j in range(kept.shape[0]):
            parts = [own[m, j, i].astype(jnp.float32) + taken[m, j, i].astype(jnp.float32) for m in (0, 1)]
            value = parts[0] + signs[j, i].astype(jnp.float32) * parts[1]
            target[j] = value.astype(target.dtype)


def team_kernel(kept, taken, *blocks):
    for j, block in enumerate(blocks):
        block[...] = (kept[j] + taken[j].astype(jnp.float32)).astype(bf)


def final_kernel(place, *refs):
    out = refs[-1]
    for k, block in enumerate(refs[:-1]):
        out[:, lanes(place[0] ^ k, block.shape[1])] = block[...]


def stationary_plan(
    tokens, in_bits, qkv_weights, qkv_bits, gain_query, gain_key, out_weights, mix_bits, out_bits
):
    groups = lax.axis_size("blk")
    team = lax.axis_size("uly")
    depth = groups // 2
    z = lax.axis_index("blk") // 2
    x = lax.axis_index("blk") % 2
    u = lax.axis_index("uly")
    own_rows, width = tokens.shape
    slab = qkv_weights.shape[2]
    columns = qkv_weights.shape[3]
    size = own_rows * team
    heads = columns // HEAD
    half = depth * size
    steps = range(depth)
    f32 = jnp.float32
    place = jnp.stack([z, x, u]).astype(jnp.int32)

    def swap_x(value):
        return lax.ppermute(value, "blk", [(i, i ^ 1) for i in range(groups)])

    def swap_z(value, step):
        return lax.ppermute(value, "blk", [(i, i ^ (2 * step)) for i in range(groups)])

    def swap_u(value, bit):
        return lax.ppermute(value, "uly", [(i, i ^ bit) for i in range(team)])

    def after(value, *earlier):
        return lax.optimization_barrier((value,) + earlier)[0]

    early = call(
        functools.partial(copy_kernel, 1, 2),
        shape(2, 2, slab, columns), ANY, [ANY], [pltpu.SemaphoreType.DMA((2,))],
    )(qkv_weights)
    partner_early = swap_x(early)

    sign_bits = jnp.transpose(qkv_bits, (1, 0, 2))
    counts = [2 + 3 * team if k == 2 else 2 for k in steps]
    blocks = call(
        functools.partial(prepare_kernel, team),
        [shape(count, own_rows, 2 * slab) for count in counts],
        [VMEM] * depth, [SMEM] + [VMEM] * 3,
    )(place, after(tokens, early), in_bits, sign_bits)
    got = [blocks[0]] + [swap_z(blocks[k], k) for k in steps if k]

    def pair(first, second):
        return call(pair_kernel, shape(2, *first.shape), VMEM, [VMEM] * 2)(first, second)

    def sign_pair(first, count):
        return call(
            functools.partial(sign_pair_kernel, first),
            shape(2, count, size, columns), VMEM, [VMEM] * 2,
        )(blocks[2], got[2])

    held_shape = (depth, 2, own_rows, 2 * slab)
    held = call(stack_kernel, shape(*held_shape), VMEM, [VMEM] * depth)(*got)
    both_pair = sign_pair(0, 2)
    both_near = swap_z(after(both_pair, held), 1)
    held = pair(held, swap_u(held, 2))
    rows = call(rows_kernel, shape(2, half, 2 * slab), VMEM, [VMEM] * 2)(
        held, swap_u(after(held, both_near), 1)
    )

    query_weights, late_own, late_near, late_far = call(
        functools.partial(late_signs_kernel, team),
        [shape(2, slab, columns)]
        + [shape(count, own_rows, 2 * slab) for count in (2, team + 2, team + 4)],
        [ANY] + [VMEM] * 3,
        [SMEM] + [VMEM] * 2 + [ANY],
        [pltpu.SemaphoreType.DMA((2,))],
    )(place, after(out_bits, blocks[0]), mix_bits, qkv_weights)
    late_far = swap_z(after(late_far, held), 2)
    query_pair = sign_pair(2, 1)
    query_near = swap_z(after(query_pair, both_near, late_far), 1)
    partner_query = swap_x(after(query_weights, partner_early, both_pair))
    out_t = jnp.transpose(out_weights, (0, 2, 1))
    out_partner = swap_x(after(out_t, partner_query))

    def project(parts, rows, partner, pair, near):
        whole = len(parts)
        count = half + size
        counts = (3 * half * whole, 2 * half * whole, half * whole)
        if parts == (0,):
            counts = (2 * count, count, count)
        return call(
            functools.partial(project_kernel, parts, size),
            [shape(counts[0], HEAD)] + [shape(count, HEAD, dtype=f32) for count in counts[1:]],
            [VMEM] * 3,
            [SMEM, VMEM, ANY, ANY] + [VMEM] * 2,
            [
                pltpu.VMEM((whole, 2, 2 * slab, columns), bf),
                pltpu.VMEM((half, columns), f32),
                pltpu.SemaphoreType.DMA((whole, 2, 2)),
            ],
        )(place, rows, qkv_weights, partner, pair, near)

    def middle(keep_own, keep_two, taken):
        count = keep_own.shape[0]
        return call(
            functools.partial(middle_kernel, size),
            [shape(count, HEAD), shape(count, HEAD, dtype=f32)],
            [VMEM] * 2,
            [VMEM] * 3,
        )(keep_own, keep_two, taken)

    both_send, both_own, both_two = project(
        (1, 2), rows, partner_early, both_pair, both_near
    )
    taken = swap_z(both_send, 1)
    query_send, query_own, query_two = project(
        (0,), after(rows, both_send), partner_query.reshape(2, 1, slab, columns),
        query_pair, query_near,
    )
    query_taken = swap_z(query_send, 1)
    send, both_total = middle(both_own, both_two, after(taken, query_send))
    both_last = swap_z(send, 2)
    send, query_total = middle(query_own, query_two, after(query_taken, both_total))
    query_last = swap_z(send, 2)
    both = call(
        functools.partial(key_value_kernel, half),
        shape(4 * half, HEAD), VMEM, [SMEM] + [VMEM] * 3,
    )(place, both_total, after(both_last, query_total), gain_key.reshape(heads, HEAD))
    both_partner = swap_x(both)
    late_got = call(near_kernel, shape(2 * team + 4, own_rows, 2 * slab), VMEM, [VMEM] * 2)(
        late_near, late_far
    )
    late_got = swap_z(after(late_got, both), 1)
    done = call(
        functools.partial(attend_kernel, half),
        shape(half + size, HEAD), VMEM, [SMEM] + [VMEM] * 5,
    )(place, query_total, query_last, gain_query.reshape(heads, HEAD), both, both_partner)

    by_head, last_head = [], []
    for k in steps:
        block = swap_z(done, k) if k else done
        main = block[:half].reshape(depth, size, HEAD)
        by_head.append(jnp.concatenate([main[j ^ k] for j in steps], axis=0))
        last_head.append(block[half:])
    attended = jnp.concatenate(by_head + [jnp.concatenate(last_head, axis=0)], axis=1)

    def relative(value, axis):
        parts = [
            lax.dynamic_slice_in_dim(value, (z ^ k) * HEAD, HEAD, axis) for k in steps
        ] + [lax.slice_in_dim(value, depth * HEAD, heads * HEAD, axis=axis)]
        return jnp.concatenate(parts, axis=axis)

    mix, out_signs = call(
        late_kernel,
        [shape(half, columns), shape(depth, 2, own_rows, 2 * slab)], [VMEM] * 2,
        [SMEM] + [VMEM] * 4,
    )(place, late_own, after(late_near, done), late_far, late_got)
    attended_flipped = attended * mix
    first = jnp.where(x == 0, out_t, out_partner)
    second = jnp.where(x == 0, out_partner, out_t)
    out_full = relative(jnp.concatenate([first, second], axis=1), 2)
    partial = jnp.stack(
        [dot32_t(attended, out_full[0]), dot32_t(attended_flipped, out_full[1])]
    ).astype(bf)
    partial = partial.reshape(2, depth, team, own_rows, 2 * slab)
    kept, sent = call(
        core_kernel,
        [shape(depth, own_rows, 2 * slab, dtype=f32), shape(depth, own_rows, 2 * slab)],
        [VMEM] * 2, [VMEM] * 3,
    )(partial[:, :, 0::2], swap_u(partial[:, :, 1::2], 1), out_signs)
    blocks = call(
        team_kernel, [shape(own_rows, 2 * slab)] * depth, [VMEM] * depth, [VMEM] * 2
    )(kept, swap_u(sent, 2))
    return call(
        final_kernel, shape(own_rows, width), VMEM, [SMEM] + [VMEM] * depth
    )(place, blocks[0], *[swap_z(blocks[k], k) for k in steps if k])


def body(*arrays):
    heads = arrays[2].shape[3] // HEAD
    depth = lax.axis_size("blk") // 2
    if depth == heads - 1 and depth == 4 and lax.axis_size("uly") == 4:
        return stationary_plan(*arrays)
    return gather_plan(*arrays)


def solution(mesh):
    return jax.shard_map(
        body,
        mesh=mesh,
        in_specs=(
            P(("blk", "uly"), None),
            P(("blk", "uly"), None),
            P(None, None, "blk", "uly"),
            P("blk", None, "uly"),
            P("uly"),
            P("uly"),
            P(None, "uly", "blk"),
            P("blk", "uly"),
            P("blk", None),
        ),
        out_specs=P(("blk", "uly"), None),
        check_vma=False,
    )
```

profile of v0, /device:TPU:0, one launch (start us, length us, event | category | flops | bytes accessed | tf_op | source)
XLA Modules:
  0.0 148.4 jit_solution(17293352604434078532)
XLA Ops:
  0.0 1.7 %copy-done = bf16[2,3,320,640]{3,2,1,0:T(8,128)(2,1)S(1)} copy-done((bf16[2,3,320,640]{3,2,1,0:T(8,128)(2,1)S(1)}, bf16[2,3,320,640]{3,2,1,0:T(8,128)(2,1)}, u32[]{:S(2)}) %copy-start) | copy-done | bytes 2457624
  1.9 3.0 %collective-permute-start.6 = (bf16[2,2,320,640]{3,2,1,0:T(8,128)(2,1)S(1)}, bf16[2,2,320,640]{3,2,1,0:T(8,128)(2,1)S(1)}, u32[]{:S(2)}, u32[]{:S(2)}) collective-permute-start(bf16[2,2,320,640]{3,2,1,0:T(8,128)(2,1)S(1)} %shard_map.91), channel_id=1, source_target_pairs={{0,4},{4,0},{8,12},{12,8},{16,20},{20,16},{24,28},{28,24},{1,5},{5... | collective-permute-start | bytes 4915208 | tf_op jit(solution)/shard_map/ppermute | solution.py:400
  5.0 1.1 copy-done.3
  6.1 0.9 copy-done.6
  7.0 0.7 shard_map.92
  7.7 2.7 %collective-permute-start.1 = (bf16[14,24,640]{2,1,0:T(8,128)(2,1)S(1)}, bf16[14,24,640]{2,1,0:T(8,128)(2,1)S(1)}, u32[]{:S(2)}, u32[]{:S(2)}) collective-permute-start(bf16[14,24,640]{2,1,0:T(8,128)(2,1)S(1)} %get-tuple-element.48.own), channel_id=1, source_target_pairs={{0,16},{4,20},{8,24},{12,28},{16,0},{20,4},{24,8},{28,12},{1,17},{... | collective-permute-start | bytes 1290248 | tf_op jit(solution)/shard_map/ppermute | solution.py:403
  10.4 1.6 %collective-permute-start = (bf16[2,24,640]{2,1,0:T(8,128)(2,1)S(1)}, bf16[2,24,640]{2,1,0:T(8,128)(2,1)S(1)}, u32[]{:S(2)}, u32[]{:S(2)}) collective-permute-start(bf16[2,24,640]{2,1,0:T(8,128)(2,1)S(1)} %get-tuple-element.47), channel_id=1, source_target_pairs={{0,8},{4,12},{8,0},{12,4},{16,24},{20,28},{24,16},{28,20},{1,9},{5... | collective-permute-start | bytes 184328 | tf_op jit(solution)/shard_map/ppermute | solution.py:403
  12.0 0.2 collective-permute-start.2
  12.2 19.1 %collective-permute-done.1.refs_2_.taken = bf16[14,24,640]{2,1,0:T(8,128)(2,1)S(1)} collective-permute-done((bf16[14,24,640]{2,1,0:T(8,128)(2,1)S(1)}, bf16[14,24,640]{2,1,0:T(8,128)(2,1)S(1)}, u32[]{:S(2)}, u32[]{:S(2)}) %collective-permute-start.1) | collective-permute-done | bytes 430112 | tf_op jit(solution)/shard_map/ppermute | solution.py:403
  31.3 1.3 collective-permute-start.4
  32.7 1.5 %collective-permute-start.3 = (bf16[4,2,24,640]{3,2,1,0:T(8,128)(2,1)S(1)}, bf16[4,2,24,640]{3,2,1,0:T(8,128)(2,1)S(1)}, u32[]{:S(2)}, u32[]{:S(2)}) collective-permute-start(bf16[4,2,24,640]{3,2,1,0:T(8,128)(2,1)S(1)} %shard_map.93.own), channel_id=1, source_target_pairs={{0,2},{1,3},{2,0},{3,1},{4,6},{5,7},{6,4},{7,5},{8,10},{9,11},{10,... | collective-permute-start | bytes 737288 | tf_op jit(solution)/shard_map/ppermute | solution.py:406
  34.2 6.1 %collective-permute-done.3.taken = bf16[4,2,24,640]{3,2,1,0:T(8,128)(2,1)S(1)} collective-permute-done((bf16[4,2,24,640]{3,2,1,0:T(8,128)(2,1)S(1)}, bf16[4,2,24,640]{3,2,1,0:T(8,128)(2,1)S(1)}, u32[]{:S(2)}, u32[]{:S(2)}) %collective-permute-start.3) | collective-permute-done | bytes 245792 | tf_op jit(solution)/shard_map/ppermute | solution.py:406
  40.3 3.8 %collective-permute-done.4.signs_13 = bf16[2,2,96,640]{3,2,1,0:T(8,128)(2,1)S(1)} collective-permute-done((bf16[2,2,96,640]{3,2,1,0:T(8,128)(2,1)S(1)}, bf16[2,2,96,640]{3,2,1,0:T(8,128)(2,1)S(1)}, u32[]{:S(2)}, u32[]{:S(2)}) %collective-permute-start.4) | collective-permute-done | bytes 491552 | tf_op jit(solution)/shard_map/ppermute | solution.py:403
  44.1 1.1 shard_map.98
  45.2 0.9 collective-permute-start.7
  46.2 4.5 %shard_map.97 = (bf16[2304,128]{1,0:T(8,128)(2,1)S(1)}, f32[1536,128]{1,0:T(8,128)S(1)}, f32[768,128]{1,0:T(8,128)S(1)}) custom-call(s32[3]{0:T(128)S(1)} %pad_add_fusion.place, bf16[2,384,640]{2,1,0:T(8,128)(2,1)S(1)} %shard_map.96.rows, bf16[2,3,320,640]{3,2,1,0:T(8,128)(2,1)S(1)} %copy-done.1, ...), custom_call_target="tpu_custom_call" | custom-call | tf_op jit(solution)/shard_map/pallas_call | solution.py:465
  50.7 1.8 %collective-permute-start.11 = (bf16[2304,128]{1,0:T(8,128)(2,1)S(1)}, bf16[2304,128]{1,0:T(8,128)(2,1)S(1)}, u32[]{:S(2)}, u32[]{:S(2)}) collective-permute-start(bf16[2304,128]{1,0:T(8,128)(2,1)S(1)} %get-tuple-element.52), channel_id=1, source_target_pairs={{0,8},{4,12},{8,0},{12,4},{16,24},{20,28},{24,16},{28,20},{1,9},{5... | collective-permute-start | bytes 1769480 | tf_op jit(solution)/shard_map/ppermute | solution.py:403
  52.5 2.2 %collective-permute-start.8 = (bf16[8,24,640]{2,1,0:T(8,128)(2,1)S(1)}, bf16[8,24,640]{2,1,0:T(8,128)(2,1)S(1)}, u32[]{:S(2)}, u32[]{:S(2)}) collective-permute-start(bf16[8,24,640]{2,1,0:T(8,128)(2,1)S(1)} %get-tuple-element.58), channel_id=1, source_target_pairs={{0,16},{4,20},{8,24},{12,28},{16,0},{20,4},{24,8},{28,12},{1,17},{... | collective-permute-start | bytes 737288 | tf_op jit(solution)/shard_map/ppermute | solution.py:403
  54.7 16.0 %collective-permute-done.8.far = bf16[8,24,640]{2,1,0:T(8,128)(2,1)S(1)} collective-permute-done((bf16[8,24,640]{2,1,0:T(8,128)(2,1)S(1)}, bf16[8,24,640]{2,1,0:T(8,128)(2,1)S(1)}, u32[]{:S(2)}, u32[]{:S(2)}) %collective-permute-start.8) | collective-permute-done | bytes 245792 | tf_op jit(solution)/shard_map/ppermute | solution.py:403
  70.7 4.4 %collective-permute-start.9 = (bf16[2,1,96,640]{3,2,1,0:T(8,128)(2,1)S(1)}, bf16[2,1,96,640]{3,2,1,0:T(8,128)(2,1)S(1)}, u32[]{:S(2)}, u32[]{:S(2)}) collective-permute-start(bf16[2,1,96,640]{3,2,1,0:T(8,128)(2,1)S(1)} %shard_map.99.signs_02), channel_id=1, source_target_pairs={{0,8},{4,12},{8,0},{12,4},{16,24},{20,28},{24,16},{28,20},{1,9},{5... | collective-permute-start | bytes 737288 | tf_op jit(solution)/shard_map/ppermute | solution.py:403
  75.1 5.5 %collective-permute-done.9.signs_13 = bf16[2,1,96,640]{3,2,1,0:T(8,128)(2,1)S(1)} collective-permute-done((bf16[2,1,96,640]{3,2,1,0:T(8,128)(2,1)S(1)}, bf16[2,1,96,640]{3,2,1,0:T(8,128)(2,1)S(1)}, u32[]{:S(2)}, u32[]{:S(2)}) %collective-permute-start.9) | collective-permute-done | bytes 245792 | tf_op jit(solution)/shard_map/ppermute | solution.py:403
  80.7 2.5 %shard_map.100 = (bf16[960,128]{1,0:T(8,128)(2,1)S(1)}, f32[480,128]{1,0:T(8,128)S(1)}, f32[480,128]{1,0:T(8,128)S(1)}) custom-call(s32[3]{0:T(128)S(1)} %pad_add_fusion.place, bf16[2,384,640]{2,1,0:T(8,128)(2,1)S(1)} %shard_map.96.rows, bf16[2,3,320,640]{3,2,1,0:T(8,128)(2,1)S(1)} %copy-done.1, bf16[2,1,320,640]{3,2,1,0:T(8,128)(2,1)S(1)} %bitcast.32, ...), custom_call_target="tpu_custom_call" | custom-call | tf_op jit(solution)/shard_map/pallas_call | solution.py:465
  83.4 0.8 collective-permute-start.13
  84.1 1.1 collective-permute-start.10
  85.2 1.2 collective-permute-start.18
  86.4 10.1 %collective-permute-done.10.taken = bf16[960,128]{1,0:T(8,128)(2,1)S(1)} collective-permute-done((bf16[960,128]{1,0:T(8,128)(2,1)S(1)}, bf16[960,128]{1,0:T(8,128)(2,1)S(1)}, u32[]{:S(2)}, u32[]{:S(2)}) %collective-permute-start.10) | collective-permute-done | bytes 245792 | tf_op jit(solution)/shard_map/ppermute | solution.py:403
  96.5 6.0 %collective-permute-done.13.taken = bf16[1536,128]{1,0:T(8,128)(2,1)S(1)} collective-permute-done((bf16[1536,128]{1,0:T(8,128)(2,1)S(1)}, bf16[1536,128]{1,0:T(8,128)(2,1)S(1)}, u32[]{:S(2)}, u32[]{:S(2)}) %collective-permute-start.13) | collective-permute-done | bytes 393248 | tf_op jit(solution)/shard_map/ppermute | solution.py:403
  102.5 0.8 shard_map.103.own
  103.3 1.2 collective-permute-start.14
  104.7 1.7 %collective-permute-start.12 = (bf16[480,128]{1,0:T(8,128)(2,1)S(1)}, bf16[480,128]{1,0:T(8,128)(2,1)S(1)}, u32[]{:S(2)}, u32[]{:S(2)}) collective-permute-start(bf16[480,128]{1,0:T(8,128)(2,1)S(1)} %get-tuple-element.69), channel_id=1, source_target_pairs={{0,16},{4,20},{8,24},{12,28},{16,0},{20,4},{24,8},{28,12},{1,17},{... | collective-permute-start | bytes 368648 | tf_op jit(solution)/shard_map/ppermute | solution.py:403
  106.4 8.0 %collective-permute-done.12.taken = bf16[480,128]{1,0:T(8,128)(2,1)S(1)} collective-permute-done((bf16[480,128]{1,0:T(8,128)(2,1)S(1)}, bf16[480,128]{1,0:T(8,128)(2,1)S(1)}, u32[]{:S(2)}, u32[]{:S(2)}) %collective-permute-start.12) | collective-permute-done | bytes 122912 | tf_op jit(solution)/shard_map/ppermute | solution.py:403
  114.4 1.4 shard_map.104
  115.8 3.0 %collective-permute-start.15 = (bf16[480,128]{1,0:T(8,128)(2,1)S(1)}, bf16[480,128]{1,0:T(8,128)(2,1)S(1)}, u32[]{:S(2)}, u32[]{:S(2)}) collective-permute-start(bf16[480,128]{1,0:T(8,128)(2,1)S(1)} %shard_map.104), channel_id=1, source_target_pairs={{0,8},{4,12},{8,0},{12,4},{16,24},{20,28},{24,16},{28,20},{1,9},{5... | collective-permute-start | bytes 368648 | tf_op jit(solution)/shard_map/ppermute | solution.py:403
  118.8 0.5 collective-permute-start.16
  119.3 1.9 %collective-permute-start.17 = (bf16[480,128]{1,0:T(8,128)(2,1)S(1)}, bf16[480,128]{1,0:T(8,128)(2,1)S(1)}, u32[]{:S(2)}, u32[]{:S(2)}) collective-permute-start(bf16[480,128]{1,0:T(8,128)(2,1)S(1)} %shard_map.104), channel_id=1, source_target_pairs={{0,24},{4,28},{8,16},{12,20},{16,8},{20,12},{24,0},{28,4},{1,25},{... | collective-permute-start | bytes 368648 | tf_op jit(solution)/shard_map/ppermute | solution.py:403
  121.3 0.6 shard_map.106
  122.0 1.3 broadcast_select_fusion
  123.8 5.5 %collective-permute-done.16 = bf16[480,128]{1,0:T(8,128)(2,1)S(1)} collective-permute-done((bf16[480,128]{1,0:T(8,128)(2,1)S(1)}, bf16[480,128]{1,0:T(8,128)(2,1)S(1)}, u32[]{:S(2)}, u32[]{:S(2)}) %collective-permute-start.16) | collective-permute-done | bytes 122912 | tf_op jit(solution)/shard_map/ppermute | solution.py:403
  129.6 0.7 fusion.1
  130.3 0.7 fusion
  131.3 1.9 %collective-permute-done.20.taken = bf16[2,4,2,24,640]{4,3,2,1,0:T(8,128)(2,1)S(1)} collective-permute-done((bf16[2,4,2,24,640]{4,3,2,1,0:T(8,128)(2,1)S(1)}, bf16[2,4,2,24,640]{4,3,2,1,0:T(8,128)(2,1)S(1)}, u32[]{:S(2)}, u32[]{:S(2)}) %collective-permute-start.20) | collective-permute-done | bytes 491552 | tf_op jit(solution)/shard_map/ppermute | solution.py:406
  133.3 1.6 %collective-permute-start.21 = (bf16[4,24,640]{2,1,0:T(8,128)(2,1)S(1)}, bf16[4,24,640]{2,1,0:T(8,128)(2,1)S(1)}, u32[]{:S(2)}, u32[]{:S(2)}) collective-permute-start(bf16[4,24,640]{2,1,0:T(8,128)(2,1)S(1)} %get-tuple-element.80), channel_id=1, source_target_pairs={{0,2},{1,3},{2,0},{3,1},{4,6},{5,7},{6,4},{7,5},{8,10},{9,11},{10,... | collective-permute-start | bytes 368648 | tf_op jit(solution)/shard_map/ppermute | solution.py:406
  134.8 3.8 %collective-permute-done.21.taken = bf16[4,24,640]{2,1,0:T(8,128)(2,1)S(1)} collective-permute-done((bf16[4,24,640]{2,1,0:T(8,128)(2,1)S(1)}, bf16[4,24,640]{2,1,0:T(8,128)(2,1)S(1)}, u32[]{:S(2)}, u32[]{:S(2)}) %collective-permute-start.21) | collective-permute-done | bytes 122912 | tf_op jit(solution)/shard_map/ppermute | solution.py:406
  138.7 2.6 %collective-permute-start.22 = (bf16[24,640]{1,0:T(8,128)(2,1)S(1)}, bf16[24,640]{1,0:T(8,128)(2,1)S(1)}, u32[]{:S(2)}, u32[]{:S(2)}) collective-permute-start(bf16[24,640]{1,0:T(8,128)(2,1)S(1)} %get-tuple-element.82), channel_id=1, source_target_pairs={{0,8},{4,12},{8,0},{12,4},{16,24},{20,28},{24,16},{28,20},{1,9},{5... | collective-permute-start | bytes 92168 | tf_op jit(solution)/shard_map/ppermute | solution.py:403
  141.5 2.3 %collective-permute-start.24 = (bf16[24,640]{1,0:T(8,128)(2,1)S(1)}, bf16[24,640]{1,0:T(8,128)(2,1)S(1)}, u32[]{:S(2)}, u32[]{:S(2)}) collective-permute-start(bf16[24,640]{1,0:T(8,128)(2,1)S(1)} %get-tuple-element.84), channel_id=1, source_target_pairs={{0,24},{4,28},{8,16},{12,20},{16,8},{20,12},{24,0},{28,4},{1,25},{... | collective-permute-start | bytes 92168 | tf_op jit(solution)/shard_map/ppermute | solution.py:403
  143.8 2.3 %collective-permute-done.23.refs_2_ = bf16[24,640]{1,0:T(8,128)(2,1)S(1)} collective-permute-done((bf16[24,640]{1,0:T(8,128)(2,1)S(1)}, bf16[24,640]{1,0:T(8,128)(2,1)S(1)}, u32[]{:S(2)}, u32[]{:S(2)}) %collective-permute-start.23) | collective-permute-done | bytes 30752 | tf_op jit(solution)/shard_map/ppermute | solution.py:403
  146.1 1.1 collective-permute-done.24.refs_3_
  147.2 1.2 shard_map.109
  (63 shorter events, 2.1 us)
Async XLA Ops:
  0.0 1.7 %copy-start = (bf16[2,3,320,640]{3,2,1,0:T(8,128)(2,1)S(1)}, bf16[2,3,320,640]{3,2,1,0:T(8,128)(2,1)}, u32[]{:S(2)}) copy-start(bf16[2,3,320,640]{3,2,1,0:T(8,128)(2,1)} %weights.7) | copy-start | bytes 7372804
  1.7 3.3 %copy-start.4 = (s32[24,2560]{1,0:T(8,128)S(1)}, s32[24,2560]{1,0:T(8,128)}, u32[]{:S(2)}) copy-start(s32[24,2560]{1,0:T(8,128)} %in_bits.1) | copy-start | bytes 737284
  1.9 43.3 %collective-permute-start.6 = (bf16[2,2,320,640]{3,2,1,0:T(8,128)(2,1)S(1)}, bf16[2,2,320,640]{3,2,1,0:T(8,128)(2,1)S(1)}, u32[]{:S(2)}, u32[]{:S(2)}) collective-permute-start(bf16[2,2,320,640]{3,2,1,0:T(8,128)(2,1)S(1)} %shard_map.91), channel_id=1, source_target_pairs={{0,4},{4,0},{8,12},{12,8},{16,20},{20,16},{24,28},{28,24},{1,5},{5... | collective-permute-start | bytes 4915208 | tf_op jit(solution)/shard_map/ppermute | solution.py:400
  5.0 1.1 copy-start.3
  6.1 0.9 copy-start.6
  7.0 37.1 %copy-start.2 = (s32[96,2560]{1,0:T(8,128)S(1)}, s32[96,2560]{1,0:T(8,128)}, u32[]{:S(2)}) copy-start(s32[96,2560]{1,0:T(8,128)} %out_bits) | copy-start | bytes 2949124
  7.7 36.4 %copy-start.1 = (bf16[2,3,320,640]{3,2,1,0:T(8,128)(2,1)S(1)}, bf16[2,3,320,640]{3,2,1,0:T(8,128)(2,1)}, u32[]{:S(2)}) copy-start(bf16[2,3,320,640]{3,2,1,0:T(8,128)(2,1)} %weights.7) | copy-start | bytes 7372804
  7.7 36.4 %copy-start.5 = (s32[96,640]{1,0:T(8,128)S(1)}, s32[96,640]{1,0:T(8,128)}, u32[]{:S(2)}) copy-start(s32[96,640]{1,0:T(8,128)} %mix_bits.1) | copy-start | bytes 737284
  7.7 23.5 %collective-permute-start.1 = (bf16[14,24,640]{2,1,0:T(8,128)(2,1)S(1)}, bf16[14,24,640]{2,1,0:T(8,128)(2,1)S(1)}, u32[]{:S(2)}, u32[]{:S(2)}) collective-permute-start(bf16[14,24,640]{2,1,0:T(8,128)(2,1)S(1)} %get-tuple-element.48.own), channel_id=1, source_target_pairs={{0,16},{4,20},{8,24},{12,28},{16,0},{20,4},{24,8},{28,12},{1,17},{... | collective-permute-start | bytes 1290248 | tf_op jit(solution)/shard_map/ppermute | solution.py:403
  10.4 20.9 %collective-permute-start = (bf16[2,24,640]{2,1,0:T(8,128)(2,1)S(1)}, bf16[2,24,640]{2,1,0:T(8,128)(2,1)S(1)}, u32[]{:S(2)}, u32[]{:S(2)}) collective-permute-start(bf16[2,24,640]{2,1,0:T(8,128)(2,1)S(1)} %get-tuple-element.47), channel_id=1, source_target_pairs={{0,8},{4,12},{8,0},{12,4},{16,24},{20,28},{24,16},{28,20},{1,9},{5... | collective-permute-start | bytes 184328 | tf_op jit(solution)/shard_map/ppermute | solution.py:403
  12.0 19.3 %collective-permute-start.2 = (bf16[2,24,640]{2,1,0:T(8,128)(2,1)S(1)}, bf16[2,24,640]{2,1,0:T(8,128)(2,1)S(1)}, u32[]{:S(2)}, u32[]{:S(2)}) collective-permute-start(bf16[2,24,640]{2,1,0:T(8,128)(2,1)S(1)} %get-tuple-element.49), channel_id=1, source_target_pairs={{0,24},{4,28},{8,16},{12,20},{16,8},{20,12},{24,0},{28,4},{1,25},{... | collective-permute-start | bytes 184328 | tf_op jit(solution)/shard_map/ppermute | solution.py:403
  31.3 12.7 %collective-permute-start.4 = (bf16[2,2,96,640]{3,2,1,0:T(8,128)(2,1)S(1)}, bf16[2,2,96,640]{3,2,1,0:T(8,128)(2,1)S(1)}, u32[]{:S(2)}, u32[]{:S(2)}) collective-permute-start(bf16[2,2,96,640]{3,2,1,0:T(8,128)(2,1)S(1)} %shard_map.95.signs_02), channel_id=1, source_target_pairs={{0,8},{4,12},{8,0},{12,4},{16,24},{20,28},{24,16},{28,20},{1,9},{5... | collective-permute-start | bytes 1474568 | tf_op jit(solution)/shard_map/ppermute | solution.py:403
  32.7 7.6 %collective-permute-start.3 = (bf16[4,2,24,640]{3,2,1,0:T(8,128)(2,1)S(1)}, bf16[4,2,24,640]{3,2,1,0:T(8,128)(2,1)S(1)}, u32[]{:S(2)}, u32[]{:S(2)}) collective-permute-start(bf16[4,2,24,640]{3,2,1,0:T(8,128)(2,1)S(1)} %shard_map.93.own), channel_id=1, source_target_pairs={{0,2},{1,3},{2,0},{3,1},{4,6},{5,7},{6,4},{7,5},{8,10},{9,11},{10,... | collective-permute-start | bytes 737288 | tf_op jit(solution)/shard_map/ppermute | solution.py:406
  44.1 2.0 %collective-permute-start.5 = (bf16[2,4,2,24,640]{4,3,2,1,0:T(8,128)(2,1)S(1)}, bf16[2,4,2,24,640]{4,3,2,1,0:T(8,128)(2,1)S(1)}, u32[]{:S(2)}, u32[]{:S(2)}) collective-permute-start(bf16[2,4,2,24,640]{4,3,2,1,0:T(8,128)(2,1)S(1)} %shard_map.94.own), channel_id=1, source_target_pairs={{0,1},{1,0},{2,3},{3,2},{4,5},{5,4},{6,7},{7,6},{8,9},{9,8},{10,11... | collective-permute-start | bytes 1474568 | tf_op jit(solution)/shard_map/ppermute | solution.py:406
  45.2 35.5 %collective-permute-start.7 = (bf16[2,320,640]{2,1,0:T(8,128)(2,1)S(1)}, bf16[2,320,640]{2,1,0:T(8,128)(2,1)S(1)}, u32[]{:S(2)}, u32[]{:S(2)}) collective-permute-start(bf16[2,320,640]{2,1,0:T(8,128)(2,1)S(1)} %get-tuple-element.56), channel_id=1, source_target_pairs={{0,4},{4,0},{8,12},{12,8},{16,20},{20,16},{24,28},{28,24},{1,5},{5... | collective-permute-start | bytes 2457608 | tf_op jit(solution)/shard_map/ppermute | solution.py:400
  50.7 32.5 %collective-permute-start.11 = (bf16[2304,128]{1,0:T(8,128)(2,1)S(1)}, bf16[2304,128]{1,0:T(8,128)(2,1)S(1)}, u32[]{:S(2)}, u32[]{:S(2)}) collective-permute-start(bf16[2304,128]{1,0:T(8,128)(2,1)S(1)} %get-tuple-element.52), channel_id=1, source_target_pairs={{0,8},{4,12},{8,0},{12,4},{16,24},{20,28},{24,16},{28,20},{1,9},{5... | collective-permute-start | bytes 1769480 | tf_op jit(solution)/shard_map/ppermute | solution.py:403
  52.5 18.2 %collective-permute-start.8 = (bf16[8,24,640]{2,1,0:T(8,128)(2,1)S(1)}, bf16[8,24,640]{2,1,0:T(8,128)(2,1)S(1)}, u32[]{:S(2)}, u32[]{:S(2)}) collective-permute-start(bf16[8,24,640]{2,1,0:T(8,128)(2,1)S(1)} %get-tuple-element.58), channel_id=1, source_target_pairs={{0,16},{4,20},{8,24},{12,28},{16,0},{20,4},{24,8},{28,12},{1,17},{... | collective-permute-start | bytes 737288 | tf_op jit(solution)/shard_map/ppermute | solution.py:403
  70.7 9.9 %collective-permute-start.9 = (bf16[2,1,96,640]{3,2,1,0:T(8,128)(2,1)S(1)}, bf16[2,1,96,640]{3,2,1,0:T(8,128)(2,1)S(1)}, u32[]{:S(2)}, u32[]{:S(2)}) collective-permute-start(bf16[2,1,96,640]{3,2,1,0:T(8,128)(2,1)S(1)} %shard_map.99.signs_02), channel_id=1, source_target_pairs={{0,8},{4,12},{8,0},{12,4},{16,24},{20,28},{24,16},{28,20},{1,9},{5... | collective-permute-start | bytes 737288 | tf_op jit(solution)/shard_map/ppermute | solution.py:403
  83.2 2.0 %copy-start.9 = (bf16[2,640,320]{1,2,0:T(8,128)(2,1)S(1)}, bf16[2,640,320]{1,2,0:T(8,128)(2,1)}, u32[]{:S(2)}) copy-start(bf16[2,640,320]{1,2,0:T(8,128)(2,1)} %param.15) | copy-start | bytes 2457604
  83.2 19.3 %copy-start.7 = (f32[640]{0:T(1024)S(1)}, f32[640]{0:T(1024)}, u32[]{:S(2)}) copy-start(f32[640]{0:T(1024)} %param.14) | copy-start | bytes 7684
  83.3 31.0 %copy-start.8 = (f32[640]{0:T(1024)S(1)}, f32[640]{0:T(1024)}, u32[]{:S(2)}) copy-start(f32[640]{0:T(1024)} %param.13) | copy-start | bytes 7684
  83.4 19.2 %collective-permute-start.13 = (bf16[1536,128]{1,0:T(8,128)(2,1)S(1)}, bf16[1536,128]{1,0:T(8,128)(2,1)S(1)}, u32[]{:S(2)}, u32[]{:S(2)}) collective-permute-start(bf16[1536,128]{1,0:T(8,128)(2,1)S(1)} %get-tuple-element.70), channel_id=1, source_target_pairs={{0,16},{4,20},{8,24},{12,28},{16,0},{20,4},{24,8},{28,12},{1,17},{... | collective-permute-start | bytes 1179656 | tf_op jit(solution)/shard_map/ppermute | solution.py:403
  84.1 12.3 %collective-permute-start.10 = (bf16[960,128]{1,0:T(8,128)(2,1)S(1)}, bf16[960,128]{1,0:T(8,128)(2,1)S(1)}, u32[]{:S(2)}, u32[]{:S(2)}) collective-permute-start(bf16[960,128]{1,0:T(8,128)(2,1)S(1)} %get-tuple-element.62), channel_id=1, source_target_pairs={{0,8},{4,12},{8,0},{12,4},{16,24},{20,28},{24,16},{28,20},{1,9},{5... | collective-permute-start | bytes 737288 | tf_op jit(solution)/shard_map/ppermute | solution.py:403
  85.2 36.7 %collective-permute-start.18 = (bf16[2,320,640]{2,1,0:T(8,128)(2,1)S(1)}, bf16[2,320,640]{2,1,0:T(8,128)(2,1)}, u32[]{:S(2)}, u32[]{:S(2)}) collective-permute-start(bf16[2,320,640]{2,1,0:T(8,128)(2,1)S(1)} %bitcast.36), channel_id=1, source_target_pairs={{0,4},{4,0},{8,12},{12,8},{16,20},{20,16},{24,28},{28,24},{1,5},{5... | collective-permute-start | bytes 2457608 | tf_op jit(solution)/shard_map/ppermute | solution.py:400
  103.3 11.1 %collective-permute-start.14 = (bf16[1536,128]{1,0:T(8,128)(2,1)S(1)}, bf16[1536,128]{1,0:T(8,128)(2,1)S(1)}, u32[]{:S(2)}, u32[]{:S(2)}) collective-permute-start(bf16[1536,128]{1,0:T(8,128)(2,1)S(1)} %shard_map.103.own), channel_id=1, source_target_pairs={{0,4},{4,0},{8,12},{12,8},{16,20},{20,16},{24,28},{28,24},{1,5},{5... | collective-permute-start | bytes 1179656 | tf_op jit(solution)/shard_map/ppermute | solution.py:400
  104.6 16.7 %collective-permute-start.19 = (bf16[12,24,640]{2,1,0:T(8,128)(2,1)S(1)}, bf16[12,24,640]{2,1,0:T(8,128)(2,1)S(1)}, u32[]{:S(2)}, u32[]{:S(2)}) collective-permute-start(bf16[12,24,640]{2,1,0:T(8,128)(2,1)S(1)} %shard_map.105), channel_id=1, source_target_pairs={{0,8},{4,12},{8,0},{12,4},{16,24},{20,28},{24,16},{28,20},{1,9},{5... | collective-permute-start | bytes 1105928 | tf_op jit(solution)/shard_map/ppermute | solution.py:403
  104.7 9.7 %collective-permute-start.12 = (bf16[480,128]{1,0:T(8,128)(2,1)S(1)}, bf16[480,128]{1,0:T(8,128)(2,1)S(1)}, u32[]{:S(2)}, u32[]{:S(2)}) collective-permute-start(bf16[480,128]{1,0:T(8,128)(2,1)S(1)} %get-tuple-element.69), channel_id=1, source_target_pairs={{0,16},{4,20},{8,24},{12,28},{16,0},{20,4},{24,8},{28,12},{1,17},{... | collective-permute-start | bytes 368648 | tf_op jit(solution)/shard_map/ppermute | solution.py:403
  115.8 7.9 %collective-permute-start.15 = (bf16[480,128]{1,0:T(8,128)(2,1)S(1)}, bf16[480,128]{1,0:T(8,128)(2,1)S(1)}, u32[]{:S(2)}, u32[]{:S(2)}) collective-permute-start(bf16[480,128]{1,0:T(8,128)(2,1)S(1)} %shard_map.104), channel_id=1, source_target_pairs={{0,8},{4,12},{8,0},{12,4},{16,24},{20,28},{24,16},{28,20},{1,9},{5... | collective-permute-start | bytes 368648 | tf_op jit(solution)/shard_map/ppermute | solution.py:403
  118.8 10.4 %collective-permute-start.16 = (bf16[480,128]{1,0:T(8,128)(2,1)S(1)}, bf16[480,128]{1,0:T(8,128)(2,1)S(1)}, u32[]{:S(2)}, u32[]{:S(2)}) collective-permute-start(bf16[480,128]{1,0:T(8,128)(2,1)S(1)} %shard_map.104), channel_id=1, source_target_pairs={{0,16},{4,20},{8,24},{12,28},{16,0},{20,4},{24,8},{28,12},{1,17},{... | collective-permute-start | bytes 368648 | tf_op jit(solution)/shard_map/ppermute | solution.py:403
  119.3 10.0 %collective-permute-start.17 = (bf16[480,128]{1,0:T(8,128)(2,1)S(1)}, bf16[480,128]{1,0:T(8,128)(2,1)S(1)}, u32[]{:S(2)}, u32[]{:S(2)}) collective-permute-start(bf16[480,128]{1,0:T(8,128)(2,1)S(1)} %shard_map.104), channel_id=1, source_target_pairs={{0,24},{4,28},{8,16},{12,20},{16,8},{20,12},{24,0},{28,4},{1,25},{... | collective-permute-start | bytes 368648 | tf_op jit(solution)/shard_map/ppermute | solution.py:403
  131.2 1.9 %collective-permute-start.20 = (bf16[2,4,2,24,640]{4,3,2,1,0:T(8,128)(2,1)S(1)}, bf16[2,4,2,24,640]{4,3,2,1,0:T(8,128)(2,1)S(1)}, u32[]{:S(2)}, u32[]{:S(2)}) collective-permute-start(bf16[2,4,2,24,640]{4,3,2,1,0:T(8,128)(2,1)S(1)} %get-tuple-element.87), channel_id=1, source_target_pairs={{0,1},{1,0},{2,3},{3,2},{4,5},{5,4},{6,7},{7,6},{8,9},{9,8},{10,11... | collective-permute-start | bytes 1474568 | tf_op jit(solution)/shard_map/ppermute | solution.py:406
  133.3 5.4 %collective-permute-start.21 = (bf16[4,24,640]{2,1,0:T(8,128)(2,1)S(1)}, bf16[4,24,640]{2,1,0:T(8,128)(2,1)S(1)}, u32[]{:S(2)}, u32[]{:S(2)}) collective-permute-start(bf16[4,24,640]{2,1,0:T(8,128)(2,1)S(1)} %get-tuple-element.80), channel_id=1, source_target_pairs={{0,2},{1,3},{2,0},{3,1},{4,6},{5,7},{6,4},{7,5},{8,10},{9,11},{10,... | collective-permute-start | bytes 368648 | tf_op jit(solution)/shard_map/ppermute | solution.py:406
  138.7 5.1 %collective-permute-start.22 = (bf16[24,640]{1,0:T(8,128)(2,1)S(1)}, bf16[24,640]{1,0:T(8,128)(2,1)S(1)}, u32[]{:S(2)}, u32[]{:S(2)}) collective-permute-start(bf16[24,640]{1,0:T(8,128)(2,1)S(1)} %get-tuple-element.82), channel_id=1, source_target_pairs={{0,8},{4,12},{8,0},{12,4},{16,24},{20,28},{24,16},{28,20},{1,9},{5... | collective-permute-start | bytes 92168 | tf_op jit(solution)/shard_map/ppermute | solution.py:403
  141.3 4.8 %collective-permute-start.23 = (bf16[24,640]{1,0:T(8,128)(2,1)S(1)}, bf16[24,640]{1,0:T(8,128)(2,1)S(1)}, u32[]{:S(2)}, u32[]{:S(2)}) collective-permute-start(bf16[24,640]{1,0:T(8,128)(2,1)S(1)} %get-tuple-element.83), channel_id=1, source_target_pairs={{0,16},{4,20},{8,24},{12,28},{16,0},{20,4},{24,8},{28,12},{1,17},{... | collective-permute-start | bytes 92168 | tf_op jit(solution)/shard_map/ppermute | solution.py:403
  141.5 5.7 %collective-permute-start.24 = (bf16[24,640]{1,0:T(8,128)(2,1)S(1)}, bf16[24,640]{1,0:T(8,128)(2,1)S(1)}, u32[]{:S(2)}, u32[]{:S(2)}) collective-permute-start(bf16[24,640]{1,0:T(8,128)(2,1)S(1)} %get-tuple-element.84), channel_id=1, source_target_pairs={{0,24},{4,28},{8,16},{12,20},{16,8},{20,12},{24,0},{28,4},{1,25},{... | collective-permute-start | bytes 92168 | tf_op jit(solution)/shard_map/ppermute | solution.py:403
where the time goes:
time: 149 us; the launch traced here: 148 us
  waiting for transfers between devices  89.1 us (60%)
  starting transfers between devices  37.9 us (25%)
  Pallas kernels  13.6 us (9%)
  local copies, waits for them, and re-layouts  3.89 us (3%)
  other arithmetic  2.15 us (1%)
    ppermute x17, waiting for transfers between devices, swap_z(): lax.ppermute(value, 'blk', [(i, i ^ 2 * step) for i in range(groups)])  77.3 us
    ppermute x17, starting transfers between devices, swap_z(): lax.ppermute(value, 'blk', [(i, i ^ 2 * step) for i in range(groups)])  28.4 us
    ppermute x4, waiting for transfers between devices, swap_u(): return lax.ppermute(value, 'uly', [(i, i ^ bit) for i in range(team)])  11.8 us
    pallas_call x2, Pallas kernels, project(): call(functools.partial(project_kernel, parts, size), [shape(counts[0], HE...  7.02 us
    ppermute x4, starting transfers between devices, swap_x(): return lax.ppermute(value, 'blk', [(i, i ^ 1) for i in range(groups)])  6.32 us
    unnamed x21, local copies, waits for them, and re-layouts  3.77 us
    ppermute x4, starting transfers between devices, swap_u(): return lax.ppermute(value, 'uly', [(i, i ^ bit) for i in range(team)])  3.18 us
  transfers between devices with their start and end apart: 25, of which 13 were waited for; matrix products, arithmetic and copies ran while one was open for 1% of the time, Pallas kernels for 8%

commit v1 on v0

--- a/solution.py
+++ b/solution.py
@@ -226,12 +226,11 @@
     out[1] = taken[...]
 
 
-def sign_pair_kernel(first, own, taken, out):
+def sign_pair_kernel(own, taken, out):
     team = (own.shape[0] - 2) // 3
     for b, ref in enumerate((own, taken)):
-        for i in range(out.shape[1]):
-            at = 2 + team * (first + i)
-            pieces = [ref[at + r].astype(jnp.float32) for r in range(team)]
+        for i in range(3):
+            pieces = [ref[2 + team * i + r].astype(jnp.float32) for r in range(team)]
             out[b, i] = jnp.concatenate(pieces, axis=0).astype(bf)
 
 
@@ -279,7 +278,8 @@
             copy.wait()
         total[...] = dot32(rows[1], held[i, 1])
         plain = dot32(rows[0], held[i, 0])
-        signs = (signs_02[0, i], signs_13[0, i], signs_02[1, i], signs_13[1, i])
+        at = part - 1 if part else 2
+        signs = (signs_02[0, at], signs_13[0, at], signs_02[1, at], signs_13[1, at])
         for j in range(depth):
             cut = slice(j * size, (j + 1) * size)
             total[cut] = plain[cut] + signs[j].astype(jnp.float32) * total[cut]
@@ -426,19 +426,15 @@
     def pair(first, second):
         return call(pair_kernel, shape(2, *first.shape), VMEM, [VMEM] * 2)(first, second)
 
-    def sign_pair(first, count):
-        return call(
-            functools.partial(sign_pair_kernel, first),
-            shape(2, count, size, columns), VMEM, [VMEM] * 2,
-        )(blocks[2], got[2])
-
     held_shape = (depth, 2, own_rows, 2 * slab)
     held = call(stack_kernel, shape(*held_shape), VMEM, [VMEM] * depth)(*got)
-    both_pair = sign_pair(0, 2)
-    both_near = swap_z(after(both_pair, held), 1)
+    signs = call(sign_pair_kernel, shape(2, 3, size, columns), VMEM, [VMEM] * 2)(
+        blocks[2], got[2]
+    )
+    signs_near = swap_z(after(signs, held), 1)
     held = pair(held, swap_u(held, 2))
     rows = call(rows_kernel, shape(2, half, 2 * slab), VMEM, [VMEM] * 2)(
-        held, swap_u(after(held, both_near), 1)
+        held, swap_u(held, 1)
     )
 
     query_weights, late_own, late_near, late_far = call(
@@ -450,13 +446,11 @@
         [pltpu.SemaphoreType.DMA((2,))],
     )(place, after(out_bits, blocks[0]), mix_bits, qkv_weights)
     late_far = swap_z(after(late_far, held), 2)
-    query_pair = sign_pair(2, 1)
-    query_near = swap_z(after(query_pair, both_near, late_far), 1)
-    partner_query = swap_x(after(query_weights, partner_early, both_pair))
+    partner_query = swap_x(after(query_weights, partner_early, rows, signs))
     out_t = jnp.transpose(out_weights, (0, 2, 1))
     out_partner = swap_x(after(out_t, partner_query))
 
-    def project(parts, rows, partner, pair, near):
+    def project(parts, rows, partner):
         whole = len(parts)
         count = half + size
         counts = (3 * half * whole, 2 * half * whole, half * whole)
@@ -472,7 +466,7 @@
                 pltpu.VMEM((half, columns), f32),
                 pltpu.SemaphoreType.DMA((whole, 2, 2)),
             ],
-        )(place, rows, qkv_weights, partner, pair, near)
+        )(place, rows, qkv_weights, partner, signs, signs_near)
 
     def middle(keep_own, keep_two, taken):
         count = keep_own.shape[0]
@@ -484,15 +478,14 @@
         )(keep_own, keep_two, taken)
 
     both_send, both_own, both_two = project(
-        (1, 2), rows, partner_early, both_pair, both_near
+        (1, 2), rows, partner_early
     )
     taken = swap_z(both_send, 1)
     query_send, query_own, query_two = project(
         (0,), after(rows, both_send), partner_query.reshape(2, 1, slab, columns),
-        query_pair, query_near,
     )
     query_taken = swap_z(query_send, 1)
-    send, both_total = middle(both_own, both_two, after(taken, query_send))
+    send, both_total = middle(both_own, both_two, after(taken, query_send, late_far))
     both_last = swap_z(send, 2)
     send, query_total = middle(query_own, query_two, after(query_taken, both_total))
     query_last = swap_z(send, 2)

time: 149 us -> 141 us (0.946)
  waiting for transfers between devices: 89.1 us -> 83.4 us
    ppermute x17 -> x16, waiting for transfers between devices: 77.3 us -> 70.7 us  [swap_z(): lax.ppermute(value, 'blk', [(i, i ^ 2 * step) for i in range(groups)])]
    ppermute x4, waiting for transfers between devices: 0.01 us -> 2.09 us  [swap_x(): return lax.ppermute(value, 'blk', [(i, i ^ 1) for i in range(groups)])]
    ppermute x17 -> x16, starting transfers between devices: 28.4 us -> 27.6 us  [swap_z(): lax.ppermute(value, 'blk', [(i, i ^ 2 * step) for i in range(groups)])]
  transfers between devices with their start and end apart: 25 -> 24, of which waited for: 13 -> 18; matrix products, arithmetic and copies ran while one was open for 1% -> 1% of each run, Pallas kernels for 8% -> 8%
where the time goes in v1:
time: 141 us
  waiting for transfers between devices  83.4 us (59%)
  starting transfers between devices  36.5 us (26%)
  Pallas kernels  13.6 us (10%)
  local copies, waits for them, and re-layouts  3.89 us (3%)
  other arithmetic  2.15 us (2%)
    ppermute x16, waiting for transfers between devices, swap_z(): lax.ppermute(value, 'blk', [(i, i ^ 2 * step) for i in range(groups)])  70.7 us
    ppermute x16, starting transfers between devices, swap_z(): lax.ppermute(value, 'blk', [(i, i ^ 2 * step) for i in range(groups)])  27.6 us
    ppermute x4, waiting for transfers between devices, swap_u(): return lax.ppermute(value, 'uly', [(i, i ^ bit) for i in range(team)])  10.7 us
    pallas_call x2, Pallas kernels, project(): call(functools.partial(project_kernel, parts, size), [shape(counts[0], HE...  7.02 us
    ppermute x4, starting transfers between devices, swap_x(): return lax.ppermute(value, 'blk', [(i, i ^ 1) for i in range(groups)])  6.53 us
    unnamed x21, local copies, waits for them, and re-layouts  3.76 us
  transfers between devices with their start and end apart: 24, of which 18 were waited for; matrix products, arithmetic and copies ran while one was open for 1% of the time, Pallas kernels for 8%

profile of v1, /device:TPU:0, one launch (start us, length us, event | category | flops | bytes accessed | tf_op | source)
XLA Modules:
  0.0 141.2 jit_solution(16197495663367361241)
XLA Ops:
  0.0 1.7 %copy-done = bf16[2,3,320,640]{3,2,1,0:T(8,128)(2,1)S(1)} copy-done((bf16[2,3,320,640]{3,2,1,0:T(8,128)(2,1)S(1)}, bf16[2,3,320,640]{3,2,1,0:T(8,128)(2,1)}, u32[]{:S(2)}) %copy-start) | copy-done | bytes 2457624
  1.9 3.0 %collective-permute-start.5 = (bf16[2,2,320,640]{3,2,1,0:T(8,128)(2,1)S(1)}, bf16[2,2,320,640]{3,2,1,0:T(8,128)(2,1)S(1)}, u32[]{:S(2)}, u32[]{:S(2)}) collective-permute-start(bf16[2,2,320,640]{3,2,1,0:T(8,128)(2,1)S(1)} %shard_map.91), channel_id=1, source_target_pairs={{0,4},{4,0},{8,12},{12,8},{16,20},{20,16},{24,28},{28,24},{1,5},{5... | collective-permute-start | bytes 4915208 | tf_op jit(solution)/shard_map/ppermute | solution.py:400
  5.0 1.1 copy-done.3
  6.1 0.9 copy-done.6
  7.0 0.7 shard_map.92
  7.7 2.7 %collective-permute-start.1 = (bf16[14,24,640]{2,1,0:T(8,128)(2,1)S(1)}, bf16[14,24,640]{2,1,0:T(8,128)(2,1)S(1)}, u32[]{:S(2)}, u32[]{:S(2)}) collective-permute-start(bf16[14,24,640]{2,1,0:T(8,128)(2,1)S(1)} %get-tuple-element.46.own), channel_id=1, source_target_pairs={{0,16},{4,20},{8,24},{12,28},{16,0},{20,4},{24,8},{28,12},{1,17},{... | collective-permute-start | bytes 1290248 | tf_op jit(solution)/shard_map/ppermute | solution.py:403
  10.4 1.6 %collective-permute-start = (bf16[2,24,640]{2,1,0:T(8,128)(2,1)S(1)}, bf16[2,24,640]{2,1,0:T(8,128)(2,1)S(1)}, u32[]{:S(2)}, u32[]{:S(2)}) collective-permute-start(bf16[2,24,640]{2,1,0:T(8,128)(2,1)S(1)} %get-tuple-element.45), channel_id=1, source_target_pairs={{0,8},{4,12},{8,0},{12,4},{16,24},{20,28},{24,16},{28,20},{1,9},{5... | collective-permute-start | bytes 184328 | tf_op jit(solution)/shard_map/ppermute | solution.py:403
  12.2 9.1 %collective-permute-done.refs_1_ = bf16[2,24,640]{2,1,0:T(8,128)(2,1)S(1)} collective-permute-done((bf16[2,24,640]{2,1,0:T(8,128)(2,1)S(1)}, bf16[2,24,640]{2,1,0:T(8,128)(2,1)S(1)}, u32[]{:S(2)}, u32[]{:S(2)}) %collective-permute-start) | collective-permute-done | bytes 61472 | tf_op jit(solution)/shard_map/ppermute | solution.py:403
  21.3 2.6 %collective-permute-done.2.refs_3_ = bf16[2,24,640]{2,1,0:T(8,128)(2,1)S(1)} collective-permute-done((bf16[2,24,640]{2,1,0:T(8,128)(2,1)S(1)}, bf16[2,24,640]{2,1,0:T(8,128)(2,1)S(1)}, u32[]{:S(2)}, u32[]{:S(2)}) %collective-permute-start.2) | collective-permute-done | bytes 61472 | tf_op jit(solution)/shard_map/ppermute | solution.py:403
  23.8 7.4 %collective-permute-done.1.refs_2_.taken = bf16[14,24,640]{2,1,0:T(8,128)(2,1)S(1)} collective-permute-done((bf16[14,24,640]{2,1,0:T(8,128)(2,1)S(1)}, bf16[14,24,640]{2,1,0:T(8,128)(2,1)S(1)}, u32[]{:S(2)}, u32[]{:S(2)}) %collective-permute-start.1) | collective-permute-done | bytes 430112 | tf_op jit(solution)/shard_map/ppermute | solution.py:403
  31.3 1.6 %collective-permute-start.3 = (bf16[4,2,24,640]{3,2,1,0:T(8,128)(2,1)S(1)}, bf16[4,2,24,640]{3,2,1,0:T(8,128)(2,1)S(1)}, u32[]{:S(2)}, u32[]{:S(2)}) collective-permute-start(bf16[4,2,24,640]{3,2,1,0:T(8,128)(2,1)S(1)} %shard_map.93.own), channel_id=1, source_target_pairs={{0,2},{1,3},{2,0},{3,1},{4,6},{5,7},{6,4},{7,5},{8,10},{9,11},{10,... | collective-permute-start | bytes 737288 | tf_op jit(solution)/shard_map/ppermute | solution.py:406
  32.9 1.4 collective-permute-start.6
  34.3 3.2 %collective-permute-done.3.taken = bf16[4,2,24,640]{3,2,1,0:T(8,128)(2,1)S(1)} collective-permute-done((bf16[4,2,24,640]{3,2,1,0:T(8,128)(2,1)S(1)}, bf16[4,2,24,640]{3,2,1,0:T(8,128)(2,1)S(1)}, u32[]{:S(2)}, u32[]{:S(2)}) %collective-permute-start.3) | collective-permute-done | bytes 245792 | tf_op jit(solution)/shard_map/ppermute | solution.py:406
  37.7 1.1 shard_map.98
  38.8 0.7 collective-permute-done.4.taken
  39.6 1.1 collective-permute-done.5.partner
  40.7 1.7 %collective-permute-start.7 = (bf16[2,320,640]{2,1,0:T(8,128)(2,1)S(1)}, bf16[2,320,640]{2,1,0:T(8,128)(2,1)S(1)}, u32[]{:S(2)}, u32[]{:S(2)}) collective-permute-start(bf16[2,320,640]{2,1,0:T(8,128)(2,1)S(1)} %get-tuple-element.53), channel_id=1, source_target_pairs={{0,4},{4,0},{8,12},{12,8},{16,20},{20,16},{24,28},{28,24},{1,5},{5... | collective-permute-start | bytes 2457608 | tf_op jit(solution)/shard_map/ppermute | solution.py:400
  42.5 8.2 %collective-permute-done.6.signs_13 = bf16[2,3,96,640]{3,2,1,0:T(8,128)(2,1)S(1)} collective-permute-done((bf16[2,3,96,640]{3,2,1,0:T(8,128)(2,1)S(1)}, bf16[2,3,96,640]{3,2,1,0:T(8,128)(2,1)S(1)}, u32[]{:S(2)}, u32[]{:S(2)}) %collective-permute-start.6) | collective-permute-done | bytes 737312 | tf_op jit(solution)/shard_map/ppermute | solution.py:403
  50.7 4.5 %shard_map.97 = (bf16[2304,128]{1,0:T(8,128)(2,1)S(1)}, f32[1536,128]{1,0:T(8,128)S(1)}, f32[768,128]{1,0:T(8,128)S(1)}) custom-call(s32[3]{0:T(128)S(1)} %pad_add_fusion.place, bf16[2,384,640]{2,1,0:T(8,128)(2,1)S(1)} %shard_map.95.rows, bf16[2,3,320,640]{3,2,1,0:T(8,128)(2,1)S(1)} %copy-done.1, ...), custom_call_target="tpu_custom_call" | custom-call | tf_op jit(solution)/shard_map/pallas_call | solution.py:459
  55.2 1.8 %collective-permute-start.9 = (bf16[2304,128]{1,0:T(8,128)(2,1)S(1)}, bf16[2304,128]{1,0:T(8,128)(2,1)S(1)}, u32[]{:S(2)}, u32[]{:S(2)}) collective-permute-start(bf16[2304,128]{1,0:T(8,128)(2,1)S(1)} %get-tuple-element.49), channel_id=1, source_target_pairs={{0,8},{4,12},{8,0},{12,4},{16,24},{20,28},{24,16},{28,20},{1,9},{5... | collective-permute-start | bytes 1769480 | tf_op jit(solution)/shard_map/ppermute | solution.py:403
  57.0 2.2 %collective-permute-start.10 = (bf16[8,24,640]{2,1,0:T(8,128)(2,1)S(1)}, bf16[8,24,640]{2,1,0:T(8,128)(2,1)S(1)}, u32[]{:S(2)}, u32[]{:S(2)}) collective-permute-start(bf16[8,24,640]{2,1,0:T(8,128)(2,1)S(1)} %get-tuple-element.60), channel_id=1, source_target_pairs={{0,16},{4,20},{8,24},{12,28},{16,0},{20,4},{24,8},{28,12},{1,17},{... | collective-permute-start | bytes 737288 | tf_op jit(solution)/shard_map/ppermute | solution.py:403
  59.2 0.9 collective-permute-done.7
  60.1 2.5 %shard_map.99 = (bf16[960,128]{1,0:T(8,128)(2,1)S(1)}, f32[480,128]{1,0:T(8,128)S(1)}, f32[480,128]{1,0:T(8,128)S(1)}) custom-call(s32[3]{0:T(128)S(1)} %pad_add_fusion.place, bf16[2,384,640]{2,1,0:T(8,128)(2,1)S(1)} %shard_map.95.rows, bf16[2,3,320,640]{3,2,1,0:T(8,128)(2,1)S(1)} %copy-done.1, bf16[2,1,320,640]{3,2,1,0:T(8,128)(2,1)S(1)} %bitcast.32, ...), custom_call_target="tpu_custom_call" | custom-call | tf_op jit(solution)/shard_map/pallas_call | solution.py:459
  62.7 11.2 %collective-permute-done.10.far = bf16[8,24,640]{2,1,0:T(8,128)(2,1)S(1)} collective-permute-done((bf16[8,24,640]{2,1,0:T(8,128)(2,1)S(1)}, bf16[8,24,640]{2,1,0:T(8,128)(2,1)S(1)}, u32[]{:S(2)}, u32[]{:S(2)}) %collective-permute-start.10) | collective-permute-done | bytes 245792 | tf_op jit(solution)/shard_map/ppermute | solution.py:403
  73.9 0.7 collective-permute-done.9.taken
  74.7 2.7 %collective-permute-start.12 = (bf16[1536,128]{1,0:T(8,128)(2,1)S(1)}, bf16[1536,128]{1,0:T(8,128)(2,1)S(1)}, u32[]{:S(2)}, u32[]{:S(2)}) collective-permute-start(bf16[1536,128]{1,0:T(8,128)(2,1)S(1)} %get-tuple-element.66), channel_id=1, source_target_pairs={{0,16},{4,20},{8,24},{12,28},{16,0},{20,4},{24,8},{28,12},{1,17},{... | collective-permute-start | bytes 1179656 | tf_op jit(solution)/shard_map/ppermute | solution.py:403
  77.4 1.4 collective-permute-start.8
  78.8 0.9 collective-permute-start.17
  79.7 9.6 %collective-permute-done.8.taken = bf16[960,128]{1,0:T(8,128)(2,1)S(1)} collective-permute-done((bf16[960,128]{1,0:T(8,128)(2,1)S(1)}, bf16[960,128]{1,0:T(8,128)(2,1)S(1)}, u32[]{:S(2)}, u32[]{:S(2)}) %collective-permute-start.8) | collective-permute-done | bytes 245792 | tf_op jit(solution)/shard_map/ppermute | solution.py:403
  89.3 5.3 %collective-permute-done.12.taken = bf16[1536,128]{1,0:T(8,128)(2,1)S(1)} collective-permute-done((bf16[1536,128]{1,0:T(8,128)(2,1)S(1)}, bf16[1536,128]{1,0:T(8,128)(2,1)S(1)}, u32[]{:S(2)}, u32[]{:S(2)}) %collective-permute-start.12) | collective-permute-done | bytes 393248 | tf_op jit(solution)/shard_map/ppermute | solution.py:403
  94.6 0.8 shard_map.102.own
  95.4 0.9 collective-permute-start.13
  96.4 2.5 %collective-permute-start.11 = (bf16[480,128]{1,0:T(8,128)(2,1)S(1)}, bf16[480,128]{1,0:T(8,128)(2,1)S(1)}, u32[]{:S(2)}, u32[]{:S(2)}) collective-permute-start(bf16[480,128]{1,0:T(8,128)(2,1)S(1)} %get-tuple-element.65), channel_id=1, source_target_pairs={{0,16},{4,20},{8,24},{12,28},{16,0},{20,4},{24,8},{28,12},{1,17},{... | collective-permute-start | bytes 368648 | tf_op jit(solution)/shard_map/ppermute | solution.py:403
  98.9 7.0 %collective-permute-done.11.taken = bf16[480,128]{1,0:T(8,128)(2,1)S(1)} collective-permute-done((bf16[480,128]{1,0:T(8,128)(2,1)S(1)}, bf16[480,128]{1,0:T(8,128)(2,1)S(1)}, u32[]{:S(2)}, u32[]{:S(2)}) %collective-permute-start.11) | collective-permute-done | bytes 122912 | tf_op jit(solution)/shard_map/ppermute | solution.py:403
  105.9 1.4 %shard_map.103 = bf16[480,128]{1,0:T(8,128)(2,1)S(1)} custom-call(s32[3]{0:T(128)S(1)} %pad_add_fusion.place, f32[480,128]{1,0:T(8,128)S(1)} %get-tuple-element.64.total, bf16[480,128]{1,0:T(8,128)(2,1)S(1)} %collective-permute-done.11.taken, f32[5,128]{1,0:T(8,128)S(1)} %bitcast.35, bf16[1536,128]{1,0:T(8,128)(2,1)S(1)} %shard_map.102.own, ...), custom_call_target="tpu_custom_call" | custom-call | tf_op jit(solution)/shard_map/pallas_call | solution.py:501
  107.3 4.2 %collective-permute-start.14 = (bf16[480,128]{1,0:T(8,128)(2,1)S(1)}, bf16[480,128]{1,0:T(8,128)(2,1)S(1)}, u32[]{:S(2)}, u32[]{:S(2)}) collective-permute-start(bf16[480,128]{1,0:T(8,128)(2,1)S(1)} %shard_map.103), channel_id=1, source_target_pairs={{0,8},{4,12},{8,0},{12,4},{16,24},{20,28},{24,16},{28,20},{1,9},{5... | collective-permute-start | bytes 368648 | tf_op jit(solution)/shard_map/ppermute | solution.py:403
  111.5 2.4 %collective-permute-start.16 = (bf16[480,128]{1,0:T(8,128)(2,1)S(1)}, bf16[480,128]{1,0:T(8,128)(2,1)S(1)}, u32[]{:S(2)}, u32[]{:S(2)}) collective-permute-start(bf16[480,128]{1,0:T(8,128)(2,1)S(1)} %shard_map.103), channel_id=1, source_target_pairs={{0,24},{4,28},{8,16},{12,20},{16,8},{20,12},{24,0},{28,4},{1,25},{... | collective-permute-start | bytes 368648 | tf_op jit(solution)/shard_map/ppermute | solution.py:403
  114.7 1.3 broadcast_select_fusion
  116.5 6.2 %collective-permute-done.15 = bf16[480,128]{1,0:T(8,128)(2,1)S(1)} collective-permute-done((bf16[480,128]{1,0:T(8,128)(2,1)S(1)}, bf16[480,128]{1,0:T(8,128)(2,1)S(1)}, u32[]{:S(2)}, u32[]{:S(2)}) %collective-permute-start.15) | collective-permute-done | bytes 122912 | tf_op jit(solution)/shard_map/ppermute | solution.py:403
  123.0 0.7 fusion.1
  123.7 0.7 fusion
  124.7 1.9 %collective-permute-done.19.taken = bf16[2,4,2,24,640]{4,3,2,1,0:T(8,128)(2,1)S(1)} collective-permute-done((bf16[2,4,2,24,640]{4,3,2,1,0:T(8,128)(2,1)S(1)}, bf16[2,4,2,24,640]{4,3,2,1,0:T(8,128)(2,1)S(1)}, u32[]{:S(2)}, u32[]{:S(2)}) %collective-permute-start.19) | collective-permute-done | bytes 491552 | tf_op jit(solution)/shard_map/ppermute | solution.py:406
  127.3 4.9 %collective-permute-done.20.taken = bf16[4,24,640]{2,1,0:T(8,128)(2,1)S(1)} collective-permute-done((bf16[4,24,640]{2,1,0:T(8,128)(2,1)S(1)}, bf16[4,24,640]{2,1,0:T(8,128)(2,1)S(1)}, u32[]{:S(2)}, u32[]{:S(2)}) %collective-permute-start.20) | collective-permute-done | bytes 122912 | tf_op jit(solution)/shard_map/ppermute | solution.py:406
  132.1 2.0 %collective-permute-start.21 = (bf16[24,640]{1,0:T(8,128)(2,1)S(1)}, bf16[24,640]{1,0:T(8,128)(2,1)S(1)}, u32[]{:S(2)}, u32[]{:S(2)}) collective-permute-start(bf16[24,640]{1,0:T(8,128)(2,1)S(1)} %get-tuple-element.78), channel_id=1, source_target_pairs={{0,8},{4,12},{8,0},{12,4},{16,24},{20,28},{24,16},{28,20},{1,9},{5... | collective-permute-start | bytes 92168 | tf_op jit(solution)/shard_map/ppermute | solution.py:403
  134.3 2.3 %collective-permute-start.23 = (bf16[24,640]{1,0:T(8,128)(2,1)S(1)}, bf16[24,640]{1,0:T(8,128)(2,1)S(1)}, u32[]{:S(2)}, u32[]{:S(2)}) collective-permute-start(bf16[24,640]{1,0:T(8,128)(2,1)S(1)} %get-tuple-element.80), channel_id=1, source_target_pairs={{0,24},{4,28},{8,16},{12,20},{16,8},{20,12},{24,0},{28,4},{1,25},{... | collective-permute-start | bytes 92168 | tf_op jit(solution)/shard_map/ppermute | solution.py:403
  136.6 2.3 %collective-permute-done.22.refs_2_ = bf16[24,640]{1,0:T(8,128)(2,1)S(1)} collective-permute-done((bf16[24,640]{1,0:T(8,128)(2,1)S(1)}, bf16[24,640]{1,0:T(8,128)(2,1)S(1)}, u32[]{:S(2)}, u32[]{:S(2)}) %collective-permute-start.22) | collective-permute-done | bytes 30752 | tf_op jit(solution)/shard_map/ppermute | solution.py:403
  139.0 1.0 collective-permute-done.23.refs_3_
  140.0 1.2 shard_map.108
  (60 shorter events, 3.6 us)
Async XLA Ops:
  0.0 1.7 %copy-start = (bf16[2,3,320,640]{3,2,1,0:T(8,128)(2,1)S(1)}, bf16[2,3,320,640]{3,2,1,0:T(8,128)(2,1)}, u32[]{:S(2)}) copy-start(bf16[2,3,320,640]{3,2,1,0:T(8,128)(2,1)} %weights.7) | copy-start | bytes 7372804
  1.7 3.3 %copy-start.4 = (s32[24,2560]{1,0:T(8,128)S(1)}, s32[24,2560]{1,0:T(8,128)}, u32[]{:S(2)}) copy-start(s32[24,2560]{1,0:T(8,128)} %in_bits.1) | copy-start | bytes 737284
  1.9 38.8 %collective-permute-start.5 = (bf16[2,2,320,640]{3,2,1,0:T(8,128)(2,1)S(1)}, bf16[2,2,320,640]{3,2,1,0:T(8,128)(2,1)S(1)}, u32[]{:S(2)}, u32[]{:S(2)}) collective-permute-start(bf16[2,2,320,640]{3,2,1,0:T(8,128)(2,1)S(1)} %shard_map.91), channel_id=1, source_target_pairs={{0,4},{4,0},{8,12},{12,8},{16,20},{20,16},{24,28},{28,24},{1,5},{5... | collective-permute-start | bytes 4915208 | tf_op jit(solution)/shard_map/ppermute | solution.py:400
  5.0 1.1 copy-start.3
  6.1 0.9 copy-start.6
  7.0 30.6 %copy-start.5 = (s32[96,640]{1,0:T(8,128)S(1)}, s32[96,640]{1,0:T(8,128)}, u32[]{:S(2)}) copy-start(s32[96,640]{1,0:T(8,128)} %mix_bits.1) | copy-start | bytes 737284
  7.7 23.5 %collective-permute-start.1 = (bf16[14,24,640]{2,1,0:T(8,128)(2,1)S(1)}, bf16[14,24,640]{2,1,0:T(8,128)(2,1)S(1)}, u32[]{:S(2)}, u32[]{:S(2)}) collective-permute-start(bf16[14,24,640]{2,1,0:T(8,128)(2,1)S(1)} %get-tuple-element.46.own), channel_id=1, source_target_pairs={{0,16},{4,20},{8,24},{12,28},{16,0},{20,4},{24,8},{28,12},{1,17},{... | collective-permute-start | bytes 1290248 | tf_op jit(solution)/shard_map/ppermute | solution.py:403
  10.4 10.9 %collective-permute-start = (bf16[2,24,640]{2,1,0:T(8,128)(2,1)S(1)}, bf16[2,24,640]{2,1,0:T(8,128)(2,1)S(1)}, u32[]{:S(2)}, u32[]{:S(2)}) collective-permute-start(bf16[2,24,640]{2,1,0:T(8,128)(2,1)S(1)} %get-tuple-element.45), channel_id=1, source_target_pairs={{0,8},{4,12},{8,0},{12,4},{16,24},{20,28},{24,16},{28,20},{1,9},{5... | collective-permute-start | bytes 184328 | tf_op jit(solution)/shard_map/ppermute | solution.py:403
  11.9 11.9 %collective-permute-start.2 = (bf16[2,24,640]{2,1,0:T(8,128)(2,1)S(1)}, bf16[2,24,640]{2,1,0:T(8,128)(2,1)S(1)}, u32[]{:S(2)}, u32[]{:S(2)}) collective-permute-start(bf16[2,24,640]{2,1,0:T(8,128)(2,1)S(1)} %get-tuple-element.47), channel_id=1, source_target_pairs={{0,24},{4,28},{8,16},{12,20},{16,8},{20,12},{24,0},{28,4},{1,25},{... | collective-permute-start | bytes 184328 | tf_op jit(solution)/shard_map/ppermute | solution.py:403
  31.2 6.4 %copy-start.2 = (s32[96,2560]{1,0:T(8,128)S(1)}, s32[96,2560]{1,0:T(8,128)}, u32[]{:S(2)}) copy-start(s32[96,2560]{1,0:T(8,128)} %out_bits) | copy-start | bytes 2949124
  31.2 6.4 %copy-start.1 = (bf16[2,3,320,640]{3,2,1,0:T(8,128)(2,1)S(1)}, bf16[2,3,320,640]{3,2,1,0:T(8,128)(2,1)}, u32[]{:S(2)}) copy-start(bf16[2,3,320,640]{3,2,1,0:T(8,128)(2,1)} %weights.7) | copy-start | bytes 7372804
  31.3 6.3 %collective-permute-start.3 = (bf16[4,2,24,640]{3,2,1,0:T(8,128)(2,1)S(1)}, bf16[4,2,24,640]{3,2,1,0:T(8,128)(2,1)S(1)}, u32[]{:S(2)}, u32[]{:S(2)}) collective-permute-start(bf16[4,2,24,640]{3,2,1,0:T(8,128)(2,1)S(1)} %shard_map.93.own), channel_id=1, source_target_pairs={{0,2},{1,3},{2,0},{3,1},{4,6},{5,7},{6,4},{7,5},{8,10},{9,11},{10,... | collective-permute-start | bytes 737288 | tf_op jit(solution)/shard_map/ppermute | solution.py:406
  32.9 17.8 %collective-permute-start.6 = (bf16[2,3,96,640]{3,2,1,0:T(8,128)(2,1)S(1)}, bf16[2,3,96,640]{3,2,1,0:T(8,128)(2,1)S(1)}, u32[]{:S(2)}, u32[]{:S(2)}) collective-permute-start(bf16[2,3,96,640]{3,2,1,0:T(8,128)(2,1)S(1)} %shard_map.96.signs_02), channel_id=1, source_target_pairs={{0,8},{4,12},{8,0},{12,4},{16,24},{20,28},{24,16},{28,20},{1,9},{5... | collective-permute-start | bytes 2211848 | tf_op jit(solution)/shard_map/ppermute | solution.py:403
  37.6 1.9 %collective-permute-start.4 = (bf16[2,4,2,24,640]{4,3,2,1,0:T(8,128)(2,1)S(1)}, bf16[2,4,2,24,640]{4,3,2,1,0:T(8,128)(2,1)S(1)}, u32[]{:S(2)}, u32[]{:S(2)}) collective-permute-start(bf16[2,4,2,24,640]{4,3,2,1,0:T(8,128)(2,1)S(1)} %shard_map.94.own), channel_id=1, source_target_pairs={{0,1},{1,0},{2,3},{3,2},{4,5},{5,4},{6,7},{7,6},{8,9},{9,8},{10,11... | collective-permute-start | bytes 1474568 | tf_op jit(solution)/shard_map/ppermute | solution.py:406
  40.7 19.4 %collective-permute-start.7 = (bf16[2,320,640]{2,1,0:T(8,128)(2,1)S(1)}, bf16[2,320,640]{2,1,0:T(8,128)(2,1)S(1)}, u32[]{:S(2)}, u32[]{:S(2)}) collective-permute-start(bf16[2,320,640]{2,1,0:T(8,128)(2,1)S(1)} %get-tuple-element.53), channel_id=1, source_target_pairs={{0,4},{4,0},{8,12},{12,8},{16,20},{20,16},{24,28},{28,24},{1,5},{5... | collective-permute-start | bytes 2457608 | tf_op jit(solution)/shard_map/ppermute | solution.py:400
  55.2 19.4 %collective-permute-start.9 = (bf16[2304,128]{1,0:T(8,128)(2,1)S(1)}, bf16[2304,128]{1,0:T(8,128)(2,1)S(1)}, u32[]{:S(2)}, u32[]{:S(2)}) collective-permute-start(bf16[2304,128]{1,0:T(8,128)(2,1)S(1)} %get-tuple-element.49), channel_id=1, source_target_pairs={{0,8},{4,12},{8,0},{12,4},{16,24},{20,28},{24,16},{28,20},{1,9},{5... | collective-permute-start | bytes 1769480 | tf_op jit(solution)/shard_map/ppermute | solution.py:403
  57.0 16.9 %collective-permute-start.10 = (bf16[8,24,640]{2,1,0:T(8,128)(2,1)S(1)}, bf16[8,24,640]{2,1,0:T(8,128)(2,1)S(1)}, u32[]{:S(2)}, u32[]{:S(2)}) collective-permute-start(bf16[8,24,640]{2,1,0:T(8,128)(2,1)S(1)} %get-tuple-element.60), channel_id=1, source_target_pairs={{0,16},{4,20},{8,24},{12,28},{16,0},{20,4},{24,8},{28,12},{1,17},{... | collective-permute-start | bytes 737288 | tf_op jit(solution)/shard_map/ppermute | solution.py:403
  62.7 16.1 %copy-start.9 = (bf16[2,640,320]{1,2,0:T(8,128)(2,1)S(1)}, bf16[2,640,320]{1,2,0:T(8,128)(2,1)}, u32[]{:S(2)}) copy-start(bf16[2,640,320]{1,2,0:T(8,128)(2,1)} %param.15) | copy-start | bytes 2457604
  62.7 31.9 %copy-start.7 = (f32[640]{0:T(1024)S(1)}, f32[640]{0:T(1024)}, u32[]{:S(2)}) copy-start(f32[640]{0:T(1024)} %param.14) | copy-start | bytes 7684
  74.7 31.2 %copy-start.8 = (f32[640]{0:T(1024)S(1)}, f32[640]{0:T(1024)}, u32[]{:S(2)}) copy-start(f32[640]{0:T(1024)} %param.13) | copy-start | bytes 7684
  74.7 19.9 %collective-permute-start.12 = (bf16[1536,128]{1,0:T(8,128)(2,1)S(1)}, bf16[1536,128]{1,0:T(8,128)(2,1)S(1)}, u32[]{:S(2)}, u32[]{:S(2)}) collective-permute-start(bf16[1536,128]{1,0:T(8,128)(2,1)S(1)} %get-tuple-element.66), channel_id=1, source_target_pairs={{0,16},{4,20},{8,24},{12,28},{16,0},{20,4},{24,8},{28,12},{1,17},{... | collective-permute-start | bytes 1179656 | tf_op jit(solution)/shard_map/ppermute | solution.py:403
  77.4 11.8 %collective-permute-start.8 = (bf16[960,128]{1,0:T(8,128)(2,1)S(1)}, bf16[960,128]{1,0:T(8,128)(2,1)S(1)}, u32[]{:S(2)}, u32[]{:S(2)}) collective-permute-start(bf16[960,128]{1,0:T(8,128)(2,1)S(1)} %get-tuple-element.56), channel_id=1, source_target_pairs={{0,8},{4,12},{8,0},{12,4},{16,24},{20,28},{24,16},{28,20},{1,9},{5... | collective-permute-start | bytes 737288 | tf_op jit(solution)/shard_map/ppermute | solution.py:403
  78.8 35.8 %collective-permute-start.17 = (bf16[2,320,640]{2,1,0:T(8,128)(2,1)S(1)}, bf16[2,320,640]{2,1,0:T(8,128)(2,1)}, u32[]{:S(2)}, u32[]{:S(2)}) collective-permute-start(bf16[2,320,640]{2,1,0:T(8,128)(2,1)S(1)} %bitcast.36), channel_id=1, source_target_pairs={{0,4},{4,0},{8,12},{12,8},{16,20},{20,16},{24,28},{28,24},{1,5},{5... | collective-permute-start | bytes 2457608 | tf_op jit(solution)/shard_map/ppermute | solution.py:400
  95.4 10.5 %collective-permute-start.13 = (bf16[1536,128]{1,0:T(8,128)(2,1)S(1)}, bf16[1536,128]{1,0:T(8,128)(2,1)S(1)}, u32[]{:S(2)}, u32[]{:S(2)}) collective-permute-start(bf16[1536,128]{1,0:T(8,128)(2,1)S(1)} %shard_map.102.own), channel_id=1, source_target_pairs={{0,4},{4,0},{8,12},{12,8},{16,20},{20,16},{24,28},{28,24},{1,5},{5... | collective-permute-start | bytes 1179656 | tf_op jit(solution)/shard_map/ppermute | solution.py:400
  96.3 17.6 %collective-permute-start.18 = (bf16[12,24,640]{2,1,0:T(8,128)(2,1)S(1)}, bf16[12,24,640]{2,1,0:T(8,128)(2,1)S(1)}, u32[]{:S(2)}, u32[]{:S(2)}) collective-permute-start(bf16[12,24,640]{2,1,0:T(8,128)(2,1)S(1)} %shard_map.104), channel_id=1, source_target_pairs={{0,8},{4,12},{8,0},{12,4},{16,24},{20,28},{24,16},{28,20},{1,9},{5... | collective-permute-start | bytes 1105928 | tf_op jit(solution)/shard_map/ppermute | solution.py:403
  96.4 9.5 %collective-permute-start.11 = (bf16[480,128]{1,0:T(8,128)(2,1)S(1)}, bf16[480,128]{1,0:T(8,128)(2,1)S(1)}, u32[]{:S(2)}, u32[]{:S(2)}) collective-permute-start(bf16[480,128]{1,0:T(8,128)(2,1)S(1)} %get-tuple-element.65), channel_id=1, source_target_pairs={{0,16},{4,20},{8,24},{12,28},{16,0},{20,4},{24,8},{28,12},{1,17},{... | collective-permute-start | bytes 368648 | tf_op jit(solution)/shard_map/ppermute | solution.py:403
  107.3 9.1 %collective-permute-start.14 = (bf16[480,128]{1,0:T(8,128)(2,1)S(1)}, bf16[480,128]{1,0:T(8,128)(2,1)S(1)}, u32[]{:S(2)}, u32[]{:S(2)}) collective-permute-start(bf16[480,128]{1,0:T(8,128)(2,1)S(1)} %shard_map.103), channel_id=1, source_target_pairs={{0,8},{4,12},{8,0},{12,4},{16,24},{20,28},{24,16},{28,20},{1,9},{5... | collective-permute-start | bytes 368648 | tf_op jit(solution)/shard_map/ppermute | solution.py:403
  111.5 11.2 %collective-permute-start.15 = (bf16[480,128]{1,0:T(8,128)(2,1)S(1)}, bf16[480,128]{1,0:T(8,128)(2,1)S(1)}, u32[]{:S(2)}, u32[]{:S(2)}) collective-permute-start(bf16[480,128]{1,0:T(8,128)(2,1)S(1)} %shard_map.103), channel_id=1, source_target_pairs={{0,16},{4,20},{8,24},{12,28},{16,0},{20,4},{24,8},{28,12},{1,17},{... | collective-permute-start | bytes 368648 | tf_op jit(solution)/shard_map/ppermute | solution.py:403
  111.5 11.3 %collective-permute-start.16 = (bf16[480,128]{1,0:T(8,128)(2,1)S(1)}, bf16[480,128]{1,0:T(8,128)(2,1)S(1)}, u32[]{:S(2)}, u32[]{:S(2)}) collective-permute-start(bf16[480,128]{1,0:T(8,128)(2,1)S(1)} %shard_map.103), channel_id=1, source_target_pairs={{0,24},{4,28},{8,16},{12,20},{16,8},{20,12},{24,0},{28,4},{1,25},{... | collective-permute-start | bytes 368648 | tf_op jit(solution)/shard_map/ppermute | solution.py:403
  124.6 1.9 %collective-permute-start.19 = (bf16[2,4,2,24,640]{4,3,2,1,0:T(8,128)(2,1)S(1)}, bf16[2,4,2,24,640]{4,3,2,1,0:T(8,128)(2,1)S(1)}, u32[]{:S(2)}, u32[]{:S(2)}) collective-permute-start(bf16[2,4,2,24,640]{4,3,2,1,0:T(8,128)(2,1)S(1)} %get-tuple-element.83), channel_id=1, source_target_pairs={{0,1},{1,0},{2,3},{3,2},{4,5},{5,4},{6,7},{7,6},{8,9},{9,8},{10,11... | collective-permute-start | bytes 1474568 | tf_op jit(solution)/shard_map/ppermute | solution.py:406
  126.7 5.4 %collective-permute-start.20 = (bf16[4,24,640]{2,1,0:T(8,128)(2,1)S(1)}, bf16[4,24,640]{2,1,0:T(8,128)(2,1)S(1)}, u32[]{:S(2)}, u32[]{:S(2)}) collective-permute-start(bf16[4,24,640]{2,1,0:T(8,128)(2,1)S(1)} %get-tuple-element.76), channel_id=1, source_target_pairs={{0,2},{1,3},{2,0},{3,1},{4,6},{5,7},{6,4},{7,5},{8,10},{9,11},{10,... | collective-permute-start | bytes 368648 | tf_op jit(solution)/shard_map/ppermute | solution.py:406
  132.1 4.5 %collective-permute-start.21 = (bf16[24,640]{1,0:T(8,128)(2,1)S(1)}, bf16[24,640]{1,0:T(8,128)(2,1)S(1)}, u32[]{:S(2)}, u32[]{:S(2)}) collective-permute-start(bf16[24,640]{1,0:T(8,128)(2,1)S(1)} %get-tuple-element.78), channel_id=1, source_target_pairs={{0,8},{4,12},{8,0},{12,4},{16,24},{20,28},{24,16},{28,20},{1,9},{5... | collective-permute-start | bytes 92168 | tf_op jit(solution)/shard_map/ppermute | solution.py:403
  134.2 4.8 %collective-permute-start.22 = (bf16[24,640]{1,0:T(8,128)(2,1)S(1)}, bf16[24,640]{1,0:T(8,128)(2,1)S(1)}, u32[]{:S(2)}, u32[]{:S(2)}) collective-permute-start(bf16[24,640]{1,0:T(8,128)(2,1)S(1)} %get-tuple-element.79), channel_id=1, source_target_pairs={{0,16},{4,20},{8,24},{12,28},{16,0},{20,4},{24,8},{28,12},{1,17},{... | collective-permute-start | bytes 92168 | tf_op jit(solution)/shard_map/ppermute | solution.py:403
  134.3 5.7 %collective-permute-start.23 = (bf16[24,640]{1,0:T(8,128)(2,1)S(1)}, bf16[24,640]{1,0:T(8,128)(2,1)S(1)}, u32[]{:S(2)}, u32[]{:S(2)}) collective-permute-start(bf16[24,640]{1,0:T(8,128)(2,1)S(1)} %get-tuple-element.80), channel_id=1, source_target_pairs={{0,24},{4,28},{8,16},{12,20},{16,8},{20,12},{24,0},{28,4},{1,25},{... | collective-permute-start | bytes 92168 | tf_op jit(solution)/shard_map/ppermute | solution.py:403

commit v2 on v1

--- a/solution.py
+++ b/solution.py
@@ -164,7 +164,8 @@
         block[1] = (plain.astype(jnp.float32) * sign).astype(bf)
     for i, part in enumerate((1, 2, 0)):
         for r, piece in enumerate(sign_pieces(sign_bits.at[part], place[2], team)):
-            blocks[2][2 + team * i + r] = piece.astype(bf)
+            for block in blocks[1:3]:
+                block[2 + team * i + r] = piece.astype(bf)
 
 
 def late_signs_kernel(team, place, out_bits, mix_bits, weights, query_weights, out, near, far, sems):
@@ -226,12 +227,8 @@
     out[1] = taken[...]
 
 
-def sign_pair_kernel(own, taken, out):
-    team = (own.shape[0] - 2) // 3
-    for b, ref in enumerate((own, taken)):
-        for i in range(3):
-            pieces = [ref[2 + team * i + r].astype(jnp.float32) for r in range(team)]
-            out[b, i] = jnp.concatenate(pieces, axis=0).astype(bf)
+def forward_kernel(taken, out):
+    out[...] = taken[taken.shape[0] - out.shape[0] :]
 
 
 def rows_kernel(own, taken, rows):
@@ -244,7 +241,7 @@
 
 
 def project_kernel(
-    parts, size, place, rows, weights, partner, signs_02, signs_13,
+    parts, size, place, rows, weights, partner, signs_0, signs_1, signs_2, signs_3,
     send, keep_own, keep_two, held, total, sems,
 ):
     z, x = place[0], place[1]
@@ -279,10 +276,13 @@
         total[...] = dot32(rows[1], held[i, 1])
         plain = dot32(rows[0], held[i, 0])
         at = part - 1 if part else 2
-        signs = (signs_02[0, at], signs_13[0, at], signs_02[1, at], signs_13[1, at])
+        team = signs_3.shape[0] // 3
         for j in range(depth):
             cut = slice(j * size, (j + 1) * size)
-            total[cut] = plain[cut] + signs[j].astype(jnp.float32) * total[cut]
+            ref = (signs_0, signs_1, signs_2, signs_3)[j]
+            start = ref.shape[0] - (3 - at) * team
+            pieces = [ref[start + r].astype(jnp.float32) for r in range(team)]
+            total[cut] = plain[cut] + jnp.concatenate(pieces, axis=0) * total[cut]
         if part:
             main(send, 3 * half * i, 1)
             main(send, 3 * half * i + half, 3)
@@ -415,7 +415,7 @@
     partner_early = swap_x(early)
 
     sign_bits = jnp.transpose(qkv_bits, (1, 0, 2))
-    counts = [2 + 3 * team if k == 2 else 2 for k in steps]
+    counts = [2 + 3 * team if k in (1, 2) else 2 for k in steps]
     blocks = call(
         functools.partial(prepare_kernel, team),
         [shape(count, own_rows, 2 * slab) for count in counts],
@@ -428,13 +428,11 @@
 
     held_shape = (depth, 2, own_rows, 2 * slab)
     held = call(stack_kernel, shape(*held_shape), VMEM, [VMEM] * depth)(*got)
-    signs = call(sign_pair_kernel, shape(2, 3, size, columns), VMEM, [VMEM] * 2)(
-        blocks[2], got[2]
-    )
-    signs_near = swap_z(after(signs, held), 1)
+    forward = call(forward_kernel, shape(3 * team, own_rows, columns), VMEM, [VMEM])(got[2])
+    signs = (blocks[2], got[1], got[2], swap_z(after(forward, held), 1))
     held = pair(held, swap_u(held, 2))
     rows = call(rows_kernel, shape(2, half, 2 * slab), VMEM, [VMEM] * 2)(
-        held, swap_u(held, 1)
+        held, swap_u(after(held, signs[3]), 1)
     )
 
     query_weights, late_own, late_near, late_far = call(
@@ -446,7 +444,7 @@
         [pltpu.SemaphoreType.DMA((2,))],
     )(place, after(out_bits, blocks[0]), mix_bits, qkv_weights)
     late_far = swap_z(after(late_far, held), 2)
-    partner_query = swap_x(after(query_weights, partner_early, rows, signs))
+    partner_query = swap_x(after(query_weights, partner_early, forward))
     out_t = jnp.transpose(out_weights, (0, 2, 1))
     out_partner = swap_x(after(out_t, partner_query))
 
@@ -460,13 +458,13 @@
             functools.partial(project_kernel, parts, size),
             [shape(counts[0], HEAD)] + [shape(count, HEAD, dtype=f32) for count in counts[1:]],
             [VMEM] * 3,
-            [SMEM, VMEM, ANY, ANY] + [VMEM] * 2,
+            [SMEM, VMEM, ANY, ANY] + [VMEM] * 4,
             [
                 pltpu.VMEM((whole, 2, 2 * slab, columns), bf),
                 pltpu.VMEM((half, columns), f32),
                 pltpu.SemaphoreType.DMA((whole, 2, 2)),
             ],
-        )(place, rows, qkv_weights, partner, signs, signs_near)
+        )(place, rows, qkv_weights, partner, *signs)
 
     def middle(keep_own, keep_two, taken):
         count = keep_own.shape[0]

time: 141 us -> 137 us (0.972)
  waiting for transfers between devices: 83.4 us -> 77.6 us
    ppermute x16, waiting for transfers between devices: 70.7 us -> 54.7 us  [swap_z(): lax.ppermute(value, 'blk', [(i, i ^ 2 * step) for i in range(groups)])]
    ppermute x4, waiting for transfers between devices: 2.09 us -> 11.2 us  [swap_x(): return lax.ppermute(value, 'blk', [(i, i ^ 1) for i in range(groups)])]
  transfers between devices with their start and end apart: 24 -> 24, of which waited for: 18 -> 15; matrix products, arithmetic and copies ran while one was open for 1% -> 1% of each run, Pallas kernels for 8% -> 9%
where the time goes in v2:
time: 137 us
  waiting for transfers between devices  77.6 us (57%)
  starting transfers between devices  37.9 us (28%)
  Pallas kernels  13.6 us (10%)
  local copies, waits for them, and re-layouts  3.89 us (3%)
  other arithmetic  2.15 us (2%)
    ppermute x16, waiting for transfers between devices, swap_z(): lax.ppermute(value, 'blk', [(i, i ^ 2 * step) for i in range(groups)])  54.7 us
    ppermute x16, starting transfers between devices, swap_z(): lax.ppermute(value, 'blk', [(i, i ^ 2 * step) for i in range(groups)])  28.4 us
    ppermute x4, waiting for transfers between devices, swap_u(): return lax.ppermute(value, 'uly', [(i, i ^ bit) for i in range(team)])  11.8 us
    ppermute x4, waiting for transfers between devices, swap_x(): return lax.ppermute(value, 'blk', [(i, i ^ 1) for i in range(groups)])  11.2 us
    pallas_call x2, Pallas kernels, project(): call(functools.partial(project_kernel, parts, size), [shape(counts[0], HE...  7.03 us
    ppermute x4, starting transfers between devices, swap_x(): return lax.ppermute(value, 'blk', [(i, i ^ 1) for i in range(groups)])  6.33 us
    unnamed x21, local copies, waits for them, and re-layouts  3.77 us
    ppermute x4, starting transfers between devices, swap_u(): return lax.ppermute(value, 'uly', [(i, i ^ bit) for i in range(team)])  3.17 us
  transfers between devices with their start and end apart: 24, of which 15 were waited for; matrix products, arithmetic and copies ran while one was open for 1% of the time, Pallas kernels for 9%

profile of v2, /device:TPU:0, one launch (start us, length us, event | category | flops | bytes accessed | tf_op | source)
XLA Modules:
  0.0 136.9 jit_solution(8165009751005138725)
XLA Ops:
  0.0 1.7 %copy-done = bf16[2,3,320,640]{3,2,1,0:T(8,128)(2,1)S(1)} copy-done((bf16[2,3,320,640]{3,2,1,0:T(8,128)(2,1)S(1)}, bf16[2,3,320,640]{3,2,1,0:T(8,128)(2,1)}, u32[]{:S(2)}) %copy-start) | copy-done | bytes 2457624
  1.9 3.0 %collective-permute-start.6 = (bf16[2,2,320,640]{3,2,1,0:T(8,128)(2,1)S(1)}, bf16[2,2,320,640]{3,2,1,0:T(8,128)(2,1)S(1)}, u32[]{:S(2)}, u32[]{:S(2)}) collective-permute-start(bf16[2,2,320,640]{3,2,1,0:T(8,128)(2,1)S(1)} %shard_map.91), channel_id=1, source_target_pairs={{0,4},{4,0},{8,12},{12,8},{16,20},{20,16},{24,28},{28,24},{1,5},{5... | collective-permute-start | bytes 4915208 | tf_op jit(solution)/shard_map/ppermute | solution.py:400
  5.0 1.1 copy-done.3
  6.1 0.9 copy-done.6
  7.0 0.7 shard_map.92
  7.7 2.7 %collective-permute-start.1 = (bf16[14,24,640]{2,1,0:T(8,128)(2,1)S(1)}, bf16[14,24,640]{2,1,0:T(8,128)(2,1)S(1)}, u32[]{:S(2)}, u32[]{:S(2)}) collective-permute-start(bf16[14,24,640]{2,1,0:T(8,128)(2,1)S(1)} %get-tuple-element.47.signs_0), channel_id=1, source_target_pairs={{0,16},{4,20},{8,24},{12,28},{16,0},{20,4},{24,8},{28,12},{1,17},{... | collective-permute-start | bytes 1290248 | tf_op jit(solution)/shard_map/ppermute | solution.py:403
  10.4 1.6 %collective-permute-start = (bf16[14,24,640]{2,1,0:T(8,128)(2,1)S(1)}, bf16[14,24,640]{2,1,0:T(8,128)(2,1)S(1)}, u32[]{:S(2)}, u32[]{:S(2)}) collective-permute-start(bf16[14,24,640]{2,1,0:T(8,128)(2,1)S(1)} %get-tuple-element.46), channel_id=1, source_target_pairs={{0,8},{4,12},{8,0},{12,4},{16,24},{20,28},{24,16},{28,20},{1,9},{5... | collective-permute-start | bytes 1290248 | tf_op jit(solution)/shard_map/ppermute | solution.py:403
  12.2 18.5 %collective-permute-done.1.refs_2_.taken.signs_2 = bf16[14,24,640]{2,1,0:T(8,128)(2,1)S(1)} collective-permute-done((bf16[14,24,640]{2,1,0:T(8,128)(2,1)S(1)}, bf16[14,24,640]{2,1,0:T(8,128)(2,1)S(1)}, u32[]{:S(2)}, u32[]{:S(2)}) %collective-permute-start.1) | collective-permute-done | bytes 430112 | tf_op jit(solution)/shard_map/ppermute | solution.py:403
  30.7 1.1 collective-permute-done.2.refs_3_
  31.8 0.9 collective-permute-start.4
  32.7 1.5 %collective-permute-start.3 = (bf16[4,2,24,640]{3,2,1,0:T(8,128)(2,1)S(1)}, bf16[4,2,24,640]{3,2,1,0:T(8,128)(2,1)S(1)}, u32[]{:S(2)}, u32[]{:S(2)}) collective-permute-start(bf16[4,2,24,640]{3,2,1,0:T(8,128)(2,1)S(1)} %shard_map.93.own), channel_id=1, source_target_pairs={{0,2},{1,3},{2,0},{3,1},{4,6},{5,7},{6,4},{7,5},{8,10},{9,11},{10,... | collective-permute-start | bytes 737288 | tf_op jit(solution)/shard_map/ppermute | solution.py:406
  34.2 6.1 %collective-permute-done.3.taken = bf16[4,2,24,640]{3,2,1,0:T(8,128)(2,1)S(1)} collective-permute-done((bf16[4,2,24,640]{3,2,1,0:T(8,128)(2,1)S(1)}, bf16[4,2,24,640]{3,2,1,0:T(8,128)(2,1)S(1)}, u32[]{:S(2)}, u32[]{:S(2)}) %collective-permute-start.3) | collective-permute-done | bytes 245792 | tf_op jit(solution)/shard_map/ppermute | solution.py:406
  40.3 1.1 collective-permute-done.4.signs_3
  41.5 1.1 shard_map.98
  42.6 0.9 collective-permute-start.7
  43.6 4.5 %shard_map.97 = (bf16[2304,128]{1,0:T(8,128)(2,1)S(1)}, f32[1536,128]{1,0:T(8,128)S(1)}, f32[768,128]{1,0:T(8,128)S(1)}) custom-call(s32[3]{0:T(128)S(1)} %pad_add_fusion.place, bf16[2,384,640]{2,1,0:T(8,128)(2,1)S(1)} %shard_map.96.rows, bf16[2,3,320,640]{3,2,1,0:T(8,128)(2,1)S(1)} %copy-done.1, ...), custom_call_target="tpu_custom_call" | custom-call | tf_op jit(solution)/shard_map/pallas_call | solution.py:457
  48.1 1.8 %collective-permute-start.9 = (bf16[2304,128]{1,0:T(8,128)(2,1)S(1)}, bf16[2304,128]{1,0:T(8,128)(2,1)S(1)}, u32[]{:S(2)}, u32[]{:S(2)}) collective-permute-start(bf16[2304,128]{1,0:T(8,128)(2,1)S(1)} %get-tuple-element.51), channel_id=1, source_target_pairs={{0,8},{4,12},{8,0},{12,4},{16,24},{20,28},{24,16},{28,20},{1,9},{5... | collective-permute-start | bytes 1769480 | tf_op jit(solution)/shard_map/ppermute | solution.py:403
  49.9 2.2 %collective-permute-start.10 = (bf16[8,24,640]{2,1,0:T(8,128)(2,1)S(1)}, bf16[8,24,640]{2,1,0:T(8,128)(2,1)S(1)}, u32[]{:S(2)}, u32[]{:S(2)}) collective-permute-start(bf16[8,24,640]{2,1,0:T(8,128)(2,1)S(1)} %get-tuple-element.62), channel_id=1, source_target_pairs={{0,16},{4,20},{8,24},{12,28},{16,0},{20,4},{24,8},{28,12},{1,17},{... | collective-permute-start | bytes 737288 | tf_op jit(solution)/shard_map/ppermute | solution.py:403
  52.1 11.2 %collective-permute-done.7 = bf16[2,320,640]{2,1,0:T(8,128)(2,1)S(1)} collective-permute-done((bf16[2,320,640]{2,1,0:T(8,128)(2,1)S(1)}, bf16[2,320,640]{2,1,0:T(8,128)(2,1)S(1)}, u32[]{:S(2)}, u32[]{:S(2)}) %collective-permute-start.7) | collective-permute-done | bytes 819232 | tf_op jit(solution)/shard_map/ppermute | solution.py:400
  63.3 2.5 %shard_map.99 = (bf16[960,128]{1,0:T(8,128)(2,1)S(1)}, f32[480,128]{1,0:T(8,128)S(1)}, f32[480,128]{1,0:T(8,128)S(1)}) custom-call(s32[3]{0:T(128)S(1)} %pad_add_fusion.place, bf16[2,384,640]{2,1,0:T(8,128)(2,1)S(1)} %shard_map.96.rows, bf16[2,3,320,640]{3,2,1,0:T(8,128)(2,1)S(1)} %copy-done.1, bf16[2,1,320,640]{3,2,1,0:T(8,128)(2,1)S(1)} %bitcast.32, ...), custom_call_target="tpu_custom_call" | custom-call | tf_op jit(solution)/shard_map/pallas_call | solution.py:457
  65.8 2.3 %collective-permute-done.10.far = bf16[8,24,640]{2,1,0:T(8,128)(2,1)S(1)} collective-permute-done((bf16[8,24,640]{2,1,0:T(8,128)(2,1)S(1)}, bf16[8,24,640]{2,1,0:T(8,128)(2,1)S(1)}, u32[]{:S(2)}, u32[]{:S(2)}) %collective-permute-start.10) | collective-permute-done | bytes 245792 | tf_op jit(solution)/shard_map/ppermute | solution.py:403
  68.1 0.7 collective-permute-done.9.taken
  69.0 2.7 %collective-permute-start.12 = (bf16[1536,128]{1,0:T(8,128)(2,1)S(1)}, bf16[1536,128]{1,0:T(8,128)(2,1)S(1)}, u32[]{:S(2)}, u32[]{:S(2)}) collective-permute-start(bf16[1536,128]{1,0:T(8,128)(2,1)S(1)} %get-tuple-element.68), channel_id=1, source_target_pairs={{0,16},{4,20},{8,24},{12,28},{16,0},{20,4},{24,8},{28,12},{1,17},{... | collective-permute-start | bytes 1179656 | tf_op jit(solution)/shard_map/ppermute | solution.py:403
  71.7 1.3 collective-permute-start.8
  73.0 1.2 collective-permute-start.17
  74.2 10.8 %collective-permute-done.8.taken = bf16[960,128]{1,0:T(8,128)(2,1)S(1)} collective-permute-done((bf16[960,128]{1,0:T(8,128)(2,1)S(1)}, bf16[960,128]{1,0:T(8,128)(2,1)S(1)}, u32[]{:S(2)}, u32[]{:S(2)}) %collective-permute-start.8) | collective-permute-done | bytes 245792 | tf_op jit(solution)/shard_map/ppermute | solution.py:403
  85.0 3.8 %collective-permute-done.12.taken = bf16[1536,128]{1,0:T(8,128)(2,1)S(1)} collective-permute-done((bf16[1536,128]{1,0:T(8,128)(2,1)S(1)}, bf16[1536,128]{1,0:T(8,128)(2,1)S(1)}, u32[]{:S(2)}, u32[]{:S(2)}) %collective-permute-start.12) | collective-permute-done | bytes 393248 | tf_op jit(solution)/shard_map/ppermute | solution.py:403
  88.8 0.8 shard_map.102.own
  89.6 1.2 collective-permute-start.13
  90.9 0.6 collective-permute-start.18
  91.5 3.4 %collective-permute-start.11 = (bf16[480,128]{1,0:T(8,128)(2,1)S(1)}, bf16[480,128]{1,0:T(8,128)(2,1)S(1)}, u32[]{:S(2)}, u32[]{:S(2)}) collective-permute-start(bf16[480,128]{1,0:T(8,128)(2,1)S(1)} %get-tuple-element.67), channel_id=1, source_target_pairs={{0,16},{4,20},{8,24},{12,28},{16,0},{20,4},{24,8},{28,12},{1,17},{... | collective-permute-start | bytes 368648 | tf_op jit(solution)/shard_map/ppermute | solution.py:403
  94.9 6.8 %collective-permute-done.11.taken = bf16[480,128]{1,0:T(8,128)(2,1)S(1)} collective-permute-done((bf16[480,128]{1,0:T(8,128)(2,1)S(1)}, bf16[480,128]{1,0:T(8,128)(2,1)S(1)}, u32[]{:S(2)}, u32[]{:S(2)}) %collective-permute-start.11) | collective-permute-done | bytes 122912 | tf_op jit(solution)/shard_map/ppermute | solution.py:403
  101.7 1.4 %shard_map.103 = bf16[480,128]{1,0:T(8,128)(2,1)S(1)} custom-call(s32[3]{0:T(128)S(1)} %pad_add_fusion.place, f32[480,128]{1,0:T(8,128)S(1)} %get-tuple-element.66.total, bf16[480,128]{1,0:T(8,128)(2,1)S(1)} %collective-permute-done.11.taken, f32[5,128]{1,0:T(8,128)S(1)} %bitcast.35, bf16[1536,128]{1,0:T(8,128)(2,1)S(1)} %shard_map.102.own, ...), custom_call_target="tpu_custom_call" | custom-call | tf_op jit(solution)/shard_map/pallas_call | solution.py:499
  103.1 4.2 %collective-permute-start.14 = (bf16[480,128]{1,0:T(8,128)(2,1)S(1)}, bf16[480,128]{1,0:T(8,128)(2,1)S(1)}, u32[]{:S(2)}, u32[]{:S(2)}) collective-permute-start(bf16[480,128]{1,0:T(8,128)(2,1)S(1)} %shard_map.103), channel_id=1, source_target_pairs={{0,8},{4,12},{8,0},{12,4},{16,24},{20,28},{24,16},{28,20},{1,9},{5... | collective-permute-start | bytes 368648 | tf_op jit(solution)/shard_map/ppermute | solution.py:403
  107.3 2.4 %collective-permute-start.16 = (bf16[480,128]{1,0:T(8,128)(2,1)S(1)}, bf16[480,128]{1,0:T(8,128)(2,1)S(1)}, u32[]{:S(2)}, u32[]{:S(2)}) collective-permute-start(bf16[480,128]{1,0:T(8,128)(2,1)S(1)} %shard_map.103), channel_id=1, source_target_pairs={{0,24},{4,28},{8,16},{12,20},{16,8},{20,12},{24,0},{28,4},{1,25},{... | collective-permute-start | bytes 368648 | tf_op jit(solution)/shard_map/ppermute | solution.py:403
  109.8 0.6 shard_map.105
  110.5 1.3 broadcast_select_fusion
  112.3 6.1 %collective-permute-done.15 = bf16[480,128]{1,0:T(8,128)(2,1)S(1)} collective-permute-done((bf16[480,128]{1,0:T(8,128)(2,1)S(1)}, bf16[480,128]{1,0:T(8,128)(2,1)S(1)}, u32[]{:S(2)}, u32[]{:S(2)}) %collective-permute-start.15) | collective-permute-done | bytes 122912 | tf_op jit(solution)/shard_map/ppermute | solution.py:403
  118.7 0.7 fusion.1
  119.4 0.7 fusion
  120.4 1.9 %collective-permute-done.19.taken = bf16[2,4,2,24,640]{4,3,2,1,0:T(8,128)(2,1)S(1)} collective-permute-done((bf16[2,4,2,24,640]{4,3,2,1,0:T(8,128)(2,1)S(1)}, bf16[2,4,2,24,640]{4,3,2,1,0:T(8,128)(2,1)S(1)}, u32[]{:S(2)}, u32[]{:S(2)}) %collective-permute-start.19) | collective-permute-done | bytes 491552 | tf_op jit(solution)/shard_map/ppermute | solution.py:406
  122.4 1.6 %collective-permute-start.20 = (bf16[4,24,640]{2,1,0:T(8,128)(2,1)S(1)}, bf16[4,24,640]{2,1,0:T(8,128)(2,1)S(1)}, u32[]{:S(2)}, u32[]{:S(2)}) collective-permute-start(bf16[4,24,640]{2,1,0:T(8,128)(2,1)S(1)} %get-tuple-element.78), channel_id=1, source_target_pairs={{0,2},{1,3},{2,0},{3,1},{4,6},{5,7},{6,4},{7,5},{8,10},{9,11},{10,... | collective-permute-start | bytes 368648 | tf_op jit(solution)/shard_map/ppermute | solution.py:406
  123.9 3.8 %collective-permute-done.20.taken = bf16[4,24,640]{2,1,0:T(8,128)(2,1)S(1)} collective-permute-done((bf16[4,24,640]{2,1,0:T(8,128)(2,1)S(1)}, bf16[4,24,640]{2,1,0:T(8,128)(2,1)S(1)}, u32[]{:S(2)}, u32[]{:S(2)}) %collective-permute-start.20) | collective-permute-done | bytes 122912 | tf_op jit(solution)/shard_map/ppermute | solution.py:406
  127.8 2.0 %collective-permute-start.21 = (bf16[24,640]{1,0:T(8,128)(2,1)S(1)}, bf16[24,640]{1,0:T(8,128)(2,1)S(1)}, u32[]{:S(2)}, u32[]{:S(2)}) collective-permute-start(bf16[24,640]{1,0:T(8,128)(2,1)S(1)} %get-tuple-element.80), channel_id=1, source_target_pairs={{0,8},{4,12},{8,0},{12,4},{16,24},{20,28},{24,16},{28,20},{1,9},{5... | collective-permute-start | bytes 92168 | tf_op jit(solution)/shard_map/ppermute | solution.py:403
  130.0 2.3 %collective-permute-start.23 = (bf16[24,640]{1,0:T(8,128)(2,1)S(1)}, bf16[24,640]{1,0:T(8,128)(2,1)S(1)}, u32[]{:S(2)}, u32[]{:S(2)}) collective-permute-start(bf16[24,640]{1,0:T(8,128)(2,1)S(1)} %get-tuple-element.82), channel_id=1, source_target_pairs={{0,24},{4,28},{8,16},{12,20},{16,8},{20,12},{24,0},{28,4},{1,25},{... | collective-permute-start | bytes 92168 | tf_op jit(solution)/shard_map/ppermute | solution.py:403
  132.3 2.3 %collective-permute-done.22.refs_2_ = bf16[24,640]{1,0:T(8,128)(2,1)S(1)} collective-permute-done((bf16[24,640]{1,0:T(8,128)(2,1)S(1)}, bf16[24,640]{1,0:T(8,128)(2,1)S(1)}, u32[]{:S(2)}, u32[]{:S(2)}) %collective-permute-start.22) | collective-permute-done | bytes 30752 | tf_op jit(solution)/shard_map/ppermute | solution.py:403
  134.6 1.1 collective-permute-done.23.refs_3_
  135.7 1.2 shard_map.108
  (60 shorter events, 2.3 us)
Async XLA Ops:
  0.0 1.7 %copy-start = (bf16[2,3,320,640]{3,2,1,0:T(8,128)(2,1)S(1)}, bf16[2,3,320,640]{3,2,1,0:T(8,128)(2,1)}, u32[]{:S(2)}) copy-start(bf16[2,3,320,640]{3,2,1,0:T(8,128)(2,1)} %weights.7) | copy-start | bytes 7372804
  1.7 3.3 %copy-start.4 = (s32[24,2560]{1,0:T(8,128)S(1)}, s32[24,2560]{1,0:T(8,128)}, u32[]{:S(2)}) copy-start(s32[24,2560]{1,0:T(8,128)} %in_bits.1) | copy-start | bytes 737284
  1.9 40.6 %collective-permute-start.6 = (bf16[2,2,320,640]{3,2,1,0:T(8,128)(2,1)S(1)}, bf16[2,2,320,640]{3,2,1,0:T(8,128)(2,1)S(1)}, u32[]{:S(2)}, u32[]{:S(2)}) collective-permute-start(bf16[2,2,320,640]{3,2,1,0:T(8,128)(2,1)S(1)} %shard_map.91), channel_id=1, source_target_pairs={{0,4},{4,0},{8,12},{12,8},{16,20},{20,16},{24,28},{28,24},{1,5},{5... | collective-permute-start | bytes 4915208 | tf_op jit(solution)/shard_map/ppermute | solution.py:400
  5.0 1.1 copy-start.3
  6.1 0.9 copy-start.6
  7.0 34.4 %copy-start.2 = (s32[96,2560]{1,0:T(8,128)S(1)}, s32[96,2560]{1,0:T(8,128)}, u32[]{:S(2)}) copy-start(s32[96,2560]{1,0:T(8,128)} %out_bits) | copy-start | bytes 2949124
  7.7 33.7 %copy-start.1 = (bf16[2,3,320,640]{3,2,1,0:T(8,128)(2,1)S(1)}, bf16[2,3,320,640]{3,2,1,0:T(8,128)(2,1)}, u32[]{:S(2)}) copy-start(bf16[2,3,320,640]{3,2,1,0:T(8,128)(2,1)} %weights.7) | copy-start | bytes 7372804
  7.7 33.7 %copy-start.5 = (s32[96,640]{1,0:T(8,128)S(1)}, s32[96,640]{1,0:T(8,128)}, u32[]{:S(2)}) copy-start(s32[96,640]{1,0:T(8,128)} %mix_bits.1) | copy-start | bytes 737284
  7.7 22.9 %collective-permute-start.1 = (bf16[14,24,640]{2,1,0:T(8,128)(2,1)S(1)}, bf16[14,24,640]{2,1,0:T(8,128)(2,1)S(1)}, u32[]{:S(2)}, u32[]{:S(2)}) collective-permute-start(bf16[14,24,640]{2,1,0:T(8,128)(2,1)S(1)} %get-tuple-element.47.signs_0), channel_id=1, source_target_pairs={{0,16},{4,20},{8,24},{12,28},{16,0},{20,4},{24,8},{28,12},{1,17},{... | collective-permute-start | bytes 1290248 | tf_op jit(solution)/shard_map/ppermute | solution.py:403
  10.4 21.4 %collective-permute-start = (bf16[14,24,640]{2,1,0:T(8,128)(2,1)S(1)}, bf16[14,24,640]{2,1,0:T(8,128)(2,1)S(1)}, u32[]{:S(2)}, u32[]{:S(2)}) collective-permute-start(bf16[14,24,640]{2,1,0:T(8,128)(2,1)S(1)} %get-tuple-element.46), channel_id=1, source_target_pairs={{0,8},{4,12},{8,0},{12,4},{16,24},{20,28},{24,16},{28,20},{1,9},{5... | collective-permute-start | bytes 1290248 | tf_op jit(solution)/shard_map/ppermute | solution.py:403
  12.0 19.8 %collective-permute-start.2 = (bf16[2,24,640]{2,1,0:T(8,128)(2,1)S(1)}, bf16[2,24,640]{2,1,0:T(8,128)(2,1)S(1)}, u32[]{:S(2)}, u32[]{:S(2)}) collective-permute-start(bf16[2,24,640]{2,1,0:T(8,128)(2,1)S(1)} %get-tuple-element.48), channel_id=1, source_target_pairs={{0,24},{4,28},{8,16},{12,20},{16,8},{20,12},{24,0},{28,4},{1,25},{... | collective-permute-start | bytes 184328 | tf_op jit(solution)/shard_map/ppermute | solution.py:403
  31.8 9.7 %collective-permute-start.4 = (bf16[12,24,640]{2,1,0:T(8,128)(2,1)S(1)}, bf16[12,24,640]{2,1,0:T(8,128)(2,1)S(1)}, u32[]{:S(2)}, u32[]{:S(2)}) collective-permute-start(bf16[12,24,640]{2,1,0:T(8,128)(2,1)S(1)} %shard_map.95), channel_id=1, source_target_pairs={{0,8},{4,12},{8,0},{12,4},{16,24},{20,28},{24,16},{28,20},{1,9},{5... | collective-permute-start | bytes 1105928 | tf_op jit(solution)/shard_map/ppermute | solution.py:403
  32.7 7.6 %collective-permute-start.3 = (bf16[4,2,24,640]{3,2,1,0:T(8,128)(2,1)S(1)}, bf16[4,2,24,640]{3,2,1,0:T(8,128)(2,1)S(1)}, u32[]{:S(2)}, u32[]{:S(2)}) collective-permute-start(bf16[4,2,24,640]{3,2,1,0:T(8,128)(2,1)S(1)} %shard_map.93.own), channel_id=1, source_target_pairs={{0,2},{1,3},{2,0},{3,1},{4,6},{5,7},{6,4},{7,5},{8,10},{9,11},{10,... | collective-permute-start | bytes 737288 | tf_op jit(solution)/shard_map/ppermute | solution.py:406
  41.4 2.0 %collective-permute-start.5 = (bf16[2,4,2,24,640]{4,3,2,1,0:T(8,128)(2,1)S(1)}, bf16[2,4,2,24,640]{4,3,2,1,0:T(8,128)(2,1)S(1)}, u32[]{:S(2)}, u32[]{:S(2)}) collective-permute-start(bf16[2,4,2,24,640]{4,3,2,1,0:T(8,128)(2,1)S(1)} %shard_map.94.own), channel_id=1, source_target_pairs={{0,1},{1,0},{2,3},{3,2},{4,5},{5,4},{6,7},{7,6},{8,9},{9,8},{10,11... | collective-permute-start | bytes 1474568 | tf_op jit(solution)/shard_map/ppermute | solution.py:406
  42.6 20.7 %collective-permute-start.7 = (bf16[2,320,640]{2,1,0:T(8,128)(2,1)S(1)}, bf16[2,320,640]{2,1,0:T(8,128)(2,1)S(1)}, u32[]{:S(2)}, u32[]{:S(2)}) collective-permute-start(bf16[2,320,640]{2,1,0:T(8,128)(2,1)S(1)} %get-tuple-element.55), channel_id=1, source_target_pairs={{0,4},{4,0},{8,12},{12,8},{16,20},{20,16},{24,28},{28,24},{1,5},{5... | collective-permute-start | bytes 2457608 | tf_op jit(solution)/shard_map/ppermute | solution.py:400
  48.1 20.8 %collective-permute-start.9 = (bf16[2304,128]{1,0:T(8,128)(2,1)S(1)}, bf16[2304,128]{1,0:T(8,128)(2,1)S(1)}, u32[]{:S(2)}, u32[]{:S(2)}) collective-permute-start(bf16[2304,128]{1,0:T(8,128)(2,1)S(1)} %get-tuple-element.51), channel_id=1, source_target_pairs={{0,8},{4,12},{8,0},{12,4},{16,24},{20,28},{24,16},{28,20},{1,9},{5... | collective-permute-start | bytes 1769480 | tf_op jit(solution)/shard_map/ppermute | solution.py:403
  49.9 18.2 %collective-permute-start.10 = (bf16[8,24,640]{2,1,0:T(8,128)(2,1)S(1)}, bf16[8,24,640]{2,1,0:T(8,128)(2,1)S(1)}, u32[]{:S(2)}, u32[]{:S(2)}) collective-permute-start(bf16[8,24,640]{2,1,0:T(8,128)(2,1)S(1)} %get-tuple-element.62), channel_id=1, source_target_pairs={{0,16},{4,20},{8,24},{12,28},{16,0},{20,4},{24,8},{28,12},{1,17},{... | collective-permute-start | bytes 737288 | tf_op jit(solution)/shard_map/ppermute | solution.py:403
  65.8 7.2 %copy-start.9 = (bf16[2,640,320]{1,2,0:T(8,128)(2,1)S(1)}, bf16[2,640,320]{1,2,0:T(8,128)(2,1)}, u32[]{:S(2)}) copy-start(bf16[2,640,320]{1,2,0:T(8,128)(2,1)} %param.15) | copy-start | bytes 2457604
  65.8 23.0 %copy-start.7 = (f32[640]{0:T(1024)S(1)}, f32[640]{0:T(1024)}, u32[]{:S(2)}) copy-start(f32[640]{0:T(1024)} %param.14) | copy-start | bytes 7684
  69.0 32.7 %copy-start.8 = (f32[640]{0:T(1024)S(1)}, f32[640]{0:T(1024)}, u32[]{:S(2)}) copy-start(f32[640]{0:T(1024)} %param.13) | copy-start | bytes 7684
  69.0 19.8 %collective-permute-start.12 = (bf16[1536,128]{1,0:T(8,128)(2,1)S(1)}, bf16[1536,128]{1,0:T(8,128)(2,1)S(1)}, u32[]{:S(2)}, u32[]{:S(2)}) collective-permute-start(bf16[1536,128]{1,0:T(8,128)(2,1)S(1)} %get-tuple-element.68), channel_id=1, source_target_pairs={{0,16},{4,20},{8,24},{12,28},{16,0},{20,4},{24,8},{28,12},{1,17},{... | collective-permute-start | bytes 1179656 | tf_op jit(solution)/shard_map/ppermute | solution.py:403
  71.7 13.2 %collective-permute-start.8 = (bf16[960,128]{1,0:T(8,128)(2,1)S(1)}, bf16[960,128]{1,0:T(8,128)(2,1)S(1)}, u32[]{:S(2)}, u32[]{:S(2)}) collective-permute-start(bf16[960,128]{1,0:T(8,128)(2,1)S(1)} %get-tuple-element.58), channel_id=1, source_target_pairs={{0,8},{4,12},{8,0},{12,4},{16,24},{20,28},{24,16},{28,20},{1,9},{5... | collective-permute-start | bytes 737288 | tf_op jit(solution)/shard_map/ppermute | solution.py:403
  73.0 37.4 %collective-permute-start.17 = (bf16[2,320,640]{2,1,0:T(8,128)(2,1)S(1)}, bf16[2,320,640]{2,1,0:T(8,128)(2,1)}, u32[]{:S(2)}, u32[]{:S(2)}) collective-permute-start(bf16[2,320,640]{2,1,0:T(8,128)(2,1)S(1)} %bitcast.36), channel_id=1, source_target_pairs={{0,4},{4,0},{8,12},{12,8},{16,20},{20,16},{24,28},{28,24},{1,5},{5... | collective-permute-start | bytes 2457608 | tf_op jit(solution)/shard_map/ppermute | solution.py:400
  89.6 12.1 %collective-permute-start.13 = (bf16[1536,128]{1,0:T(8,128)(2,1)S(1)}, bf16[1536,128]{1,0:T(8,128)(2,1)S(1)}, u32[]{:S(2)}, u32[]{:S(2)}) collective-permute-start(bf16[1536,128]{1,0:T(8,128)(2,1)S(1)} %shard_map.102.own), channel_id=1, source_target_pairs={{0,4},{4,0},{8,12},{12,8},{16,20},{20,16},{24,28},{28,24},{1,5},{5... | collective-permute-start | bytes 1179656 | tf_op jit(solution)/shard_map/ppermute | solution.py:400
  90.9 18.9 %collective-permute-start.18 = (bf16[12,24,640]{2,1,0:T(8,128)(2,1)S(1)}, bf16[12,24,640]{2,1,0:T(8,128)(2,1)S(1)}, u32[]{:S(2)}, u32[]{:S(2)}) collective-permute-start(bf16[12,24,640]{2,1,0:T(8,128)(2,1)S(1)} %shard_map.104), channel_id=1, source_target_pairs={{0,8},{4,12},{8,0},{12,4},{16,24},{20,28},{24,16},{28,20},{1,9},{5... | collective-permute-start | bytes 1105928 | tf_op jit(solution)/shard_map/ppermute | solution.py:403
  91.5 10.2 %collective-permute-start.11 = (bf16[480,128]{1,0:T(8,128)(2,1)S(1)}, bf16[480,128]{1,0:T(8,128)(2,1)S(1)}, u32[]{:S(2)}, u32[]{:S(2)}) collective-permute-start(bf16[480,128]{1,0:T(8,128)(2,1)S(1)} %get-tuple-element.67), channel_id=1, source_target_pairs={{0,16},{4,20},{8,24},{12,28},{16,0},{20,4},{24,8},{28,12},{1,17},{... | collective-permute-start | bytes 368648 | tf_op jit(solution)/shard_map/ppermute | solution.py:403
  103.1 9.1 %collective-permute-start.14 = (bf16[480,128]{1,0:T(8,128)(2,1)S(1)}, bf16[480,128]{1,0:T(8,128)(2,1)S(1)}, u32[]{:S(2)}, u32[]{:S(2)}) collective-permute-start(bf16[480,128]{1,0:T(8,128)(2,1)S(1)} %shard_map.103), channel_id=1, source_target_pairs={{0,8},{4,12},{8,0},{12,4},{16,24},{20,28},{24,16},{28,20},{1,9},{5... | collective-permute-start | bytes 368648 | tf_op jit(solution)/shard_map/ppermute | solution.py:403
  107.3 11.0 %collective-permute-start.15 = (bf16[480,128]{1,0:T(8,128)(2,1)S(1)}, bf16[480,128]{1,0:T(8,128)(2,1)S(1)}, u32[]{:S(2)}, u32[]{:S(2)}) collective-permute-start(bf16[480,128]{1,0:T(8,128)(2,1)S(1)} %shard_map.103), channel_id=1, source_target_pairs={{0,16},{4,20},{8,24},{12,28},{16,0},{20,4},{24,8},{28,12},{1,17},{... | collective-permute-start | bytes 368648 | tf_op jit(solution)/shard_map/ppermute | solution.py:403
  107.3 11.1 %collective-permute-start.16 = (bf16[480,128]{1,0:T(8,128)(2,1)S(1)}, bf16[480,128]{1,0:T(8,128)(2,1)S(1)}, u32[]{:S(2)}, u32[]{:S(2)}) collective-permute-start(bf16[480,128]{1,0:T(8,128)(2,1)S(1)} %shard_map.103), channel_id=1, source_target_pairs={{0,24},{4,28},{8,16},{12,20},{16,8},{20,12},{24,0},{28,4},{1,25},{... | collective-permute-start | bytes 368648 | tf_op jit(solution)/shard_map/ppermute | solution.py:403
  120.3 1.9 %collective-permute-start.19 = (bf16[2,4,2,24,640]{4,3,2,1,0:T(8,128)(2,1)S(1)}, bf16[2,4,2,24,640]{4,3,2,1,0:T(8,128)(2,1)S(1)}, u32[]{:S(2)}, u32[]{:S(2)}) collective-permute-start(bf16[2,4,2,24,640]{4,3,2,1,0:T(8,128)(2,1)S(1)} %get-tuple-element.85), channel_id=1, source_target_pairs={{0,1},{1,0},{2,3},{3,2},{4,5},{5,4},{6,7},{7,6},{8,9},{9,8},{10,11... | collective-permute-start | bytes 1474568 | tf_op jit(solution)/shard_map/ppermute | solution.py:406
  122.4 5.4 %collective-permute-start.20 = (bf16[4,24,640]{2,1,0:T(8,128)(2,1)S(1)}, bf16[4,24,640]{2,1,0:T(8,128)(2,1)S(1)}, u32[]{:S(2)}, u32[]{:S(2)}) collective-permute-start(bf16[4,24,640]{2,1,0:T(8,128)(2,1)S(1)} %get-tuple-element.78), channel_id=1, source_target_pairs={{0,2},{1,3},{2,0},{3,1},{4,6},{5,7},{6,4},{7,5},{8,10},{9,11},{10,... | collective-permute-start | bytes 368648 | tf_op jit(solution)/shard_map/ppermute | solution.py:406
  127.8 4.5 %collective-permute-start.21 = (bf16[24,640]{1,0:T(8,128)(2,1)S(1)}, bf16[24,640]{1,0:T(8,128)(2,1)S(1)}, u32[]{:S(2)}, u32[]{:S(2)}) collective-permute-start(bf16[24,640]{1,0:T(8,128)(2,1)S(1)} %get-tuple-element.80), channel_id=1, source_target_pairs={{0,8},{4,12},{8,0},{12,4},{16,24},{20,28},{24,16},{28,20},{1,9},{5... | collective-permute-start | bytes 92168 | tf_op jit(solution)/shard_map/ppermute | solution.py:403
  129.8 4.8 %collective-permute-start.22 = (bf16[24,640]{1,0:T(8,128)(2,1)S(1)}, bf16[24,640]{1,0:T(8,128)(2,1)S(1)}, u32[]{:S(2)}, u32[]{:S(2)}) collective-permute-start(bf16[24,640]{1,0:T(8,128)(2,1)S(1)} %get-tuple-element.81), channel_id=1, source_target_pairs={{0,16},{4,20},{8,24},{12,28},{16,0},{20,4},{24,8},{28,12},{1,17},{... | collective-permute-start | bytes 92168 | tf_op jit(solution)/shard_map/ppermute | solution.py:403
  130.0 5.7 %collective-permute-start.23 = (bf16[24,640]{1,0:T(8,128)(2,1)S(1)}, bf16[24,640]{1,0:T(8,128)(2,1)S(1)}, u32[]{:S(2)}, u32[]{:S(2)}) collective-permute-start(bf16[24,640]{1,0:T(8,128)(2,1)S(1)} %get-tuple-element.82), channel_id=1, source_target_pairs={{0,24},{4,28},{8,16},{12,20},{16,8},{20,12},{24,0},{28,4},{1,25},{... | collective-permute-start | bytes 92168 | tf_op jit(solution)/shard_map/ppermute | solution.py:403

commit v3 on v2

--- a/solution.py
+++ b/solution.py
@@ -231,33 +231,27 @@
     out[...] = taken[taken.shape[0] - out.shape[0] :]
 
 
-def rows_kernel(own, taken, rows):
+def rows_kernel(place, own, taken, rows):
     depth, kinds, piece = own.shape[1:4]
     for m in range(kinds):
         for j in range(depth):
             parts = [ref[y, j, m].astype(jnp.float32) for y in (0, 1) for ref in (own, taken)]
             at = j * 4 * piece
-            rows[m, at : at + 4 * piece] = jnp.concatenate(parts, axis=0).astype(bf)
+            wide = jnp.concatenate(parts, axis=0)
+            slab = wide.shape[1] // 2
+            low, high = wide[:, :slab], wide[:, slab:]
+            first = place[1] == 0
+            rows[m, 0, at : at + 4 * piece] = jnp.where(first, low, high).astype(bf)
+            rows[m, 1, at : at + 4 * piece] = jnp.where(first, high, low).astype(bf)
 
 
 def project_kernel(
     parts, size, place, rows, weights, partner, signs_0, signs_1, signs_2, signs_3,
-    send, keep_own, keep_two, held, total, sems,
+    send, keep_own, keep_two, total,
 ):
-    z, x = place[0], place[1]
-    slab = weights.shape[2]
-    own = pl.ds(pl.multiple_of(x * slab, 64), slab)
-    other = pl.ds(pl.multiple_of((1 - x) * slab, 64), slab)
-    depth = rows.shape[1] // size
-    half = depth * size
-    copies = []
-    for i, part in enumerate(parts):
-        for m in (0, 1):
-            near, far = weights.at[m, part], partner.at[m, i]
-            copies.append(pltpu.make_async_copy(near, held.at[i, m, own], sems.at[i, m, 0]))
-            copies.append(pltpu.make_async_copy(far, held.at[i, m, other], sems.at[i, m, 1]))
-    for copy in copies:
-        copy.start()
+    z = place[0]
+    half = rows.shape[2]
+    depth = half // size
 
     def block(j, head):
         return total[j * size : (j + 1) * size, lanes(head, HEAD)]
@@ -271,10 +265,11 @@
         target[start : start + size] = block(j, depth).astype(target.dtype)
 
     for i, part in enumerate(parts):
-        for copy in copies[4 * i : 4 * i + 4]:
-            copy.wait()
-        total[...] = dot32(rows[1], held[i, 1])
-        plain = dot32(rows[0], held[i, 0])
+        near, far = [
+            dot32(rows[m, 0], weights[m, part]) + dot32(rows[m, 1], partner[m, i]) for m in (0, 1)
+        ]
+        total[...] = far
+        plain = near
         at = part - 1 if part else 2
         team = signs_3.shape[0] // 3
         for j in range(depth):
@@ -431,8 +426,8 @@
     forward = call(forward_kernel, shape(3 * team, own_rows, columns), VMEM, [VMEM])(got[2])
     signs = (blocks[2], got[1], got[2], swap_z(after(forward, held), 1))
     held = pair(held, swap_u(held, 2))
-    rows = call(rows_kernel, shape(2, half, 2 * slab), VMEM, [VMEM] * 2)(
-        held, swap_u(after(held, signs[3]), 1)
+    rows = call(rows_kernel, shape(2, 2, half, slab), VMEM, [SMEM] + [VMEM] * 2)(
+        place, held, swap_u(after(held, signs[3]), 1)
     )
 
     query_weights, late_own, late_near, late_far = call(
@@ -443,7 +438,6 @@
         [SMEM] + [VMEM] * 2 + [ANY],
         [pltpu.SemaphoreType.DMA((2,))],
     )(place, after(out_bits, blocks[0]), mix_bits, qkv_weights)
-    late_far = swap_z(after(late_far, held), 2)
     partner_query = swap_x(after(query_weights, partner_early, forward))
     out_t = jnp.transpose(out_weights, (0, 2, 1))
     out_partner = swap_x(after(out_t, partner_query))
@@ -458,11 +452,9 @@
             functools.partial(project_kernel, parts, size),
             [shape(counts[0], HEAD)] + [shape(count, HEAD, dtype=f32) for count in counts[1:]],
             [VMEM] * 3,
-            [SMEM, VMEM, ANY, ANY] + [VMEM] * 4,
+            [SMEM] + [VMEM] * 7,
             [
-                pltpu.VMEM((whole, 2, 2 * slab, columns), bf),
                 pltpu.VMEM((half, columns), f32),
-                pltpu.SemaphoreType.DMA((whole, 2, 2)),
             ],
         )(place, rows, qkv_weights, partner, *signs)
 
@@ -479,12 +471,12 @@
         (1, 2), rows, partner_early
     )
     taken = swap_z(both_send, 1)
+    send, both_total = middle(both_own, both_two, taken)
+    both_last = swap_z(send, 2)
     query_send, query_own, query_two = project(
-        (0,), after(rows, both_send), partner_query.reshape(2, 1, slab, columns),
+        (0,), after(rows, both_total), partner_query.reshape(2, 1, slab, columns),
     )
     query_taken = swap_z(query_send, 1)
-    send, both_total = middle(both_own, both_two, after(taken, query_send, late_far))
-    both_last = swap_z(send, 2)
     send, query_total = middle(query_own, query_two, after(query_taken, both_total))
     query_last = swap_z(send, 2)
     both = call(
@@ -492,14 +484,16 @@
         shape(4 * half, HEAD), VMEM, [SMEM] + [VMEM] * 3,
     )(place, both_total, after(both_last, query_total), gain_key.reshape(heads, HEAD))
     both_partner = swap_x(both)
-    late_got = call(near_kernel, shape(2 * team + 4, own_rows, 2 * slab), VMEM, [VMEM] * 2)(
-        late_near, late_far
-    )
-    late_got = swap_z(after(late_got, both), 1)
+    late_far = swap_z(after(late_far, both), 2)
     done = call(
         functools.partial(attend_kernel, half),
         shape(half + size, HEAD), VMEM, [SMEM] + [VMEM] * 5,
     )(place, query_total, query_last, gain_query.reshape(heads, HEAD), both, both_partner)
+
+    late_got = call(near_kernel, shape(2 * team + 4, own_rows, 2 * slab), VMEM, [VMEM] * 2)(
+        after(late_near, done), late_far
+    )
+    late_got = swap_z(late_got, 1)
 
     by_head, last_head = [], []
     for k in steps:

time: 137 us -> 144 us (1.051)
  waiting for transfers between devices: 77.6 us -> 91.6 us
  starting transfers between devices: 37.9 us -> 32.3 us
    ppermute x16, waiting for transfers between devices: 54.7 us -> 79.8 us  [swap_z(): lax.ppermute(value, 'blk', [(i, i ^ 2 * step) for i in range(groups)])]
    ppermute x4, waiting for transfers between devices: 11.2 us -> 0.01 us  [swap_x(): return lax.ppermute(value, 'blk', [(i, i ^ 1) for i in range(groups)])]
    ppermute x16, starting transfers between devices: 28.4 us -> 23.1 us  [swap_z(): lax.ppermute(value, 'blk', [(i, i ^ 2 * step) for i in range(groups)])]
    pallas_call x2, Pallas kernels: 7.03 us -> 4.95 us  [project(): call(functools.partial(project_kernel, parts, size), [shape(counts[0], HE...]
    pallas_call x1, Pallas kernels: 0.08 us -> 1.53 us  [stationary_plan(): call(rows_kernel, shape(2, 2, half, slab), VMEM, [SMEM] + [VMEM] * 2)]
    unnamed x21 -> x23, local copies, waits for them, and re-layouts: 3.77 us -> 3.77 us
  transfers between devices with their start and end apart: 24 -> 24, of which waited for: 15 -> 15; matrix products, arithmetic and copies ran while one was open for 1% -> 1% of each run, Pallas kernels for 9% -> 7%
where the time goes in v3:
time: 144 us
  waiting for transfers between devices  91.6 us (64%)
  starting transfers between devices  32.3 us (22%)
  Pallas kernels  13.7 us (10%)
  local copies, waits for them, and re-layouts  3.89 us (3%)
    ppermute x16, waiting for transfers between devices, swap_z(): lax.ppermute(value, 'blk', [(i, i ^ 2 * step) for i in range(groups)])  79.8 us
    ppermute x16, starting transfers between devices, swap_z(): lax.ppermute(value, 'blk', [(i, i ^ 2 * step) for i in range(groups)])  23.1 us
    ppermute x4, waiting for transfers between devices, swap_u(): return lax.ppermute(value, 'uly', [(i, i ^ bit) for i in range(team)])  11.8 us
    ppermute x4, starting transfers between devices, swap_x(): return lax.ppermute(value, 'blk', [(i, i ^ 1) for i in range(groups)])  6.02 us
    pallas_call x2, Pallas kernels, project(): call(functools.partial(project_kernel, parts, size), [shape(counts[0], HE...  4.95 us
    unnamed x23, local copies, waits for them, and re-layouts  3.77 us
    ppermute x4, starting transfers between devices, swap_u(): return lax.ppermute(value, 'uly', [(i, i ^ bit) for i in range(team)])  3.17 us
  transfers between devices with their start and end apart: 24, of which 15 were waited for; matrix products, arithmetic and copies ran while one was open for 1% of the time, Pallas kernels for 7%

profile of v3, /device:TPU:0, one launch (start us, length us, event | category | flops | bytes accessed | tf_op | source)
XLA Modules:
  0.0 144.2 jit_solution(12115544306066524847)
XLA Ops:
  0.0 1.7 %copy-done = bf16[2,3,320,640]{3,2,1,0:T(8,128)(2,1)S(1)} copy-done((bf16[2,3,320,640]{3,2,1,0:T(8,128)(2,1)S(1)}, bf16[2,3,320,640]{3,2,1,0:T(8,128)(2,1)}, u32[]{:S(2)}) %copy-start) | copy-done | bytes 2457624
  1.9 3.0 %collective-permute-start.6 = (bf16[2,2,320,640]{3,2,1,0:T(8,128)(2,1)S(1)}, bf16[2,2,320,640]{3,2,1,0:T(8,128)(2,1)S(1)}, u32[]{:S(2)}, u32[]{:S(2)}) collective-permute-start(bf16[2,2,320,640]{3,2,1,0:T(8,128)(2,1)S(1)} %shard_map.91), channel_id=1, source_target_pairs={{0,4},{4,0},{8,12},{12,8},{16,20},{20,16},{24,28},{28,24},{1,5},{5... | collective-permute-start | bytes 4915208 | tf_op jit(solution)/shard_map/ppermute | solution.py:395
  5.0 1.1 copy-done.3
  6.1 0.9 copy-done.6
  7.0 0.7 shard_map.92
  7.7 2.7 %collective-permute-start.1 = (bf16[14,24,640]{2,1,0:T(8,128)(2,1)S(1)}, bf16[14,24,640]{2,1,0:T(8,128)(2,1)S(1)}, u32[]{:S(2)}, u32[]{:S(2)}) collective-permute-start(bf16[14,24,640]{2,1,0:T(8,128)(2,1)S(1)} %get-tuple-element.45.signs_0), channel_id=1, source_target_pairs={{0,16},{4,20},{8,24},{12,28},{16,0},{20,4},{24,8},{28,12},{1,17},{... | collective-permute-start | bytes 1290248 | tf_op jit(solution)/shard_map/ppermute | solution.py:398
  10.4 1.6 %collective-permute-start = (bf16[14,24,640]{2,1,0:T(8,128)(2,1)S(1)}, bf16[14,24,640]{2,1,0:T(8,128)(2,1)S(1)}, u32[]{:S(2)}, u32[]{:S(2)}) collective-permute-start(bf16[14,24,640]{2,1,0:T(8,128)(2,1)S(1)} %get-tuple-element.44), channel_id=1, source_target_pairs={{0,8},{4,12},{8,0},{12,4},{16,24},{20,28},{24,16},{28,20},{1,9},{5... | collective-permute-start | bytes 1290248 | tf_op jit(solution)/shard_map/ppermute | solution.py:398
  12.0 0.2 collective-permute-start.2
  12.2 18.5 %collective-permute-done.1.refs_2_.taken.signs_2 = bf16[14,24,640]{2,1,0:T(8,128)(2,1)S(1)} collective-permute-done((bf16[14,24,640]{2,1,0:T(8,128)(2,1)S(1)}, bf16[14,24,640]{2,1,0:T(8,128)(2,1)S(1)}, u32[]{:S(2)}, u32[]{:S(2)}) %collective-permute-start.1) | collective-permute-done | bytes 430112 | tf_op jit(solution)/shard_map/ppermute | solution.py:398
  30.7 1.1 collective-permute-done.2.refs_3_
  31.8 0.9 collective-permute-start.4
  32.7 1.5 %collective-permute-start.3 = (bf16[4,2,24,640]{3,2,1,0:T(8,128)(2,1)S(1)}, bf16[4,2,24,640]{3,2,1,0:T(8,128)(2,1)S(1)}, u32[]{:S(2)}, u32[]{:S(2)}) collective-permute-start(bf16[4,2,24,640]{3,2,1,0:T(8,128)(2,1)S(1)} %shard_map.93.own), channel_id=1, source_target_pairs={{0,2},{1,3},{2,0},{3,1},{4,6},{5,7},{6,4},{7,5},{8,10},{9,11},{10,... | collective-permute-start | bytes 737288 | tf_op jit(solution)/shard_map/ppermute | solution.py:401
  34.2 6.1 %collective-permute-done.3.taken = bf16[4,2,24,640]{3,2,1,0:T(8,128)(2,1)S(1)} collective-permute-done((bf16[4,2,24,640]{3,2,1,0:T(8,128)(2,1)S(1)}, bf16[4,2,24,640]{3,2,1,0:T(8,128)(2,1)S(1)}, u32[]{:S(2)}, u32[]{:S(2)}) %collective-permute-start.3) | collective-permute-done | bytes 245792 | tf_op jit(solution)/shard_map/ppermute | solution.py:401
  40.3 1.1 collective-permute-done.4.signs_3
  41.5 1.8 %shard_map.99 = (bf16[2,320,640]{2,1,0:T(8,128)(2,1)S(1)}, bf16[2,24,640]{2,1,0:T(8,128)(2,1)S(1)}, bf16[6,24,640]{2,1,0:T(8,128)(2,1)S(1)}, bf16[8,24,640]{2,1,0:T(8,128)(2,1)}) custom-call(s32[3]{0:T(128)S(1)} %pad_add_fusion.place, s32[96,2560]{1,0:T(8,128)S(1)} %copy-done.2, s32[96,640]{1,0:T(8,128)S(1)} %copy-done.5, bf16[2,3,320,640]{3,2,1,0:T(8,128)(2,1)S(1)} %copy-done.1), custom_call_target="tpu_custom_call" | custom-call | tf_op jit(solution)/shard_map/pallas_call | solution.py:433
  43.3 0.9 collective-permute-start.8
  44.2 1.5 %shard_map.96.rows = bf16[2,2,384,320]{3,2,1,0:T(8,128)(2,1)S(1)} custom-call(s32[3]{0:T(128)S(1)} %pad_add_fusion.place, bf16[2,4,2,24,640]{4,3,2,1,0:T(8,128)(2,1)S(1)} %shard_map.94.own, bf16[2,4,2,24,640]{4,3,2,1,0:T(8,128)(2,1)S(1)} %collective-permute-done.5.taken), custom_call_target="tpu_custom_call" | custom-call | tf_op jit(solution)/shard_map/pallas_call | solution.py:429
  45.7 3.1 %shard_map.97 = (bf16[2304,128]{1,0:T(8,128)(2,1)S(1)}, f32[1536,128]{1,0:T(8,128)S(1)}, f32[768,128]{1,0:T(8,128)S(1)}) custom-call(s32[3]{0:T(128)S(1)} %pad_add_fusion.place, bf16[2,2,384,320]{3,2,1,0:T(8,128)(2,1)S(1)} %shard_map.96.rows, bf16[2,3,320,640]{3,2,1,0:T(8,128)(2,1)S(1)} %copy-done.1, ...), custom_call_target="tpu_custom_call" | custom-call | tf_op jit(solution)/shard_map/pallas_call | solution.py:451
  48.8 1.8 %collective-permute-start.7 = (bf16[2304,128]{1,0:T(8,128)(2,1)S(1)}, bf16[2304,128]{1,0:T(8,128)(2,1)S(1)}, u32[]{:S(2)}, u32[]{:S(2)}) collective-permute-start(bf16[2304,128]{1,0:T(8,128)(2,1)S(1)} %get-tuple-element.51), channel_id=1, source_target_pairs={{0,8},{4,12},{8,0},{12,4},{16,24},{20,28},{24,16},{28,20},{1,9},{5... | collective-permute-start | bytes 1769480 | tf_op jit(solution)/shard_map/ppermute | solution.py:398
  50.6 13.7 %collective-permute-done.7.taken = bf16[2304,128]{1,0:T(8,128)(2,1)S(1)} collective-permute-done((bf16[2304,128]{1,0:T(8,128)(2,1)S(1)}, bf16[2304,128]{1,0:T(8,128)(2,1)S(1)}, u32[]{:S(2)}, u32[]{:S(2)}) %collective-permute-start.7) | collective-permute-done | bytes 589856 | tf_op jit(solution)/shard_map/ppermute | solution.py:398
  64.4 3.7 %collective-permute-start.11 = (bf16[1536,128]{1,0:T(8,128)(2,1)S(1)}, bf16[1536,128]{1,0:T(8,128)(2,1)S(1)}, u32[]{:S(2)}, u32[]{:S(2)}) collective-permute-start(bf16[1536,128]{1,0:T(8,128)(2,1)S(1)} %get-tuple-element.63), channel_id=1, source_target_pairs={{0,16},{4,20},{8,24},{12,28},{16,0},{20,4},{24,8},{28,12},{1,17},{... | collective-permute-start | bytes 1179656 | tf_op jit(solution)/shard_map/ppermute | solution.py:398
  68.2 1.9 %shard_map.100 = (bf16[960,128]{1,0:T(8,128)(2,1)S(1)}, f32[480,128]{1,0:T(8,128)S(1)}, f32[480,128]{1,0:T(8,128)S(1)}) custom-call(s32[3]{0:T(128)S(1)} %pad_add_fusion.place, bf16[2,2,384,320]{3,2,1,0:T(8,128)(2,1)S(1)} %shard_map.96.rows, bf16[2,3,320,640]{3,2,1,0:T(8,128)(2,1)S(1)} %copy-done.1, bf16[2,1,320,640]{3,2,1,0:T(8,128)(2,1)S(1)} %bitcast.32, ...), custom_call_target="tpu_custom_call" | custom-call | tf_op jit(solution)/shard_map/pallas_call | solution.py:451
  70.1 0.3 collective-permute-start.9
  70.5 11.0 %collective-permute-done.9.taken = bf16[960,128]{1,0:T(8,128)(2,1)S(1)} collective-permute-done((bf16[960,128]{1,0:T(8,128)(2,1)S(1)}, bf16[960,128]{1,0:T(8,128)(2,1)S(1)}, u32[]{:S(2)}, u32[]{:S(2)}) %collective-permute-start.9) | collective-permute-done | bytes 245792 | tf_op jit(solution)/shard_map/ppermute | solution.py:398
  81.5 3.8 %collective-permute-done.11.taken = bf16[1536,128]{1,0:T(8,128)(2,1)S(1)} collective-permute-done((bf16[1536,128]{1,0:T(8,128)(2,1)S(1)}, bf16[1536,128]{1,0:T(8,128)(2,1)S(1)}, u32[]{:S(2)}, u32[]{:S(2)}) %collective-permute-start.11) | collective-permute-done | bytes 393248 | tf_op jit(solution)/shard_map/ppermute | solution.py:398
  85.3 0.8 shard_map.102.own
  86.1 1.2 collective-permute-start.12
  87.3 2.9 %collective-permute-start.10 = (bf16[480,128]{1,0:T(8,128)(2,1)S(1)}, bf16[480,128]{1,0:T(8,128)(2,1)S(1)}, u32[]{:S(2)}, u32[]{:S(2)}) collective-permute-start(bf16[480,128]{1,0:T(8,128)(2,1)S(1)} %get-tuple-element.62), channel_id=1, source_target_pairs={{0,16},{4,20},{8,24},{12,28},{16,0},{20,4},{24,8},{28,12},{1,17},{... | collective-permute-start | bytes 368648 | tf_op jit(solution)/shard_map/ppermute | solution.py:398
  90.3 0.9 collective-permute-start.16
  91.1 13.9 %collective-permute-done.10.taken = bf16[480,128]{1,0:T(8,128)(2,1)S(1)} collective-permute-done((bf16[480,128]{1,0:T(8,128)(2,1)S(1)}, bf16[480,128]{1,0:T(8,128)(2,1)S(1)}, u32[]{:S(2)}, u32[]{:S(2)}) %collective-permute-start.10) | collective-permute-done | bytes 122912 | tf_op jit(solution)/shard_map/ppermute | solution.py:398
  105.0 1.4 shard_map.103
  106.5 3.1 %collective-permute-start.14 = (bf16[480,128]{1,0:T(8,128)(2,1)S(1)}, bf16[480,128]{1,0:T(8,128)(2,1)S(1)}, u32[]{:S(2)}, u32[]{:S(2)}) collective-permute-start(bf16[480,128]{1,0:T(8,128)(2,1)S(1)} %shard_map.103), channel_id=1, source_target_pairs={{0,16},{4,20},{8,24},{12,28},{16,0},{20,4},{24,8},{28,12},{1,17},{... | collective-permute-start | bytes 368648 | tf_op jit(solution)/shard_map/ppermute | solution.py:398
  109.6 1.3 collective-permute-start.15
  111.0 3.6 %collective-permute-done.13 = bf16[480,128]{1,0:T(8,128)(2,1)S(1)} collective-permute-done((bf16[480,128]{1,0:T(8,128)(2,1)S(1)}, bf16[480,128]{1,0:T(8,128)(2,1)S(1)}, u32[]{:S(2)}, u32[]{:S(2)}) %collective-permute-start.13) | collective-permute-done | bytes 122912 | tf_op jit(solution)/shard_map/ppermute | solution.py:398
  114.6 4.5 %collective-permute-done.14 = bf16[480,128]{1,0:T(8,128)(2,1)S(1)} collective-permute-done((bf16[480,128]{1,0:T(8,128)(2,1)S(1)}, bf16[480,128]{1,0:T(8,128)(2,1)S(1)}, u32[]{:S(2)}, u32[]{:S(2)}) %collective-permute-start.14) | collective-permute-done | bytes 122912 | tf_op jit(solution)/shard_map/ppermute | solution.py:398
  119.9 0.7 fusion
  120.6 4.3 %collective-permute-done.18.got = bf16[12,24,640]{2,1,0:T(8,128)(2,1)S(1)} collective-permute-done((bf16[12,24,640]{2,1,0:T(8,128)(2,1)S(1)}, bf16[12,24,640]{2,1,0:T(8,128)(2,1)S(1)}, u32[]{:S(2)}, u32[]{:S(2)}) %collective-permute-start.18) | collective-permute-done | bytes 368672 | tf_op jit(solution)/shard_map/ppermute | solution.py:398
  124.9 0.6 shard_map.105
  125.7 0.7 fusion.1
  126.7 1.9 %collective-permute-done.19.taken = bf16[2,4,2,24,640]{4,3,2,1,0:T(8,128)(2,1)S(1)} collective-permute-done((bf16[2,4,2,24,640]{4,3,2,1,0:T(8,128)(2,1)S(1)}, bf16[2,4,2,24,640]{4,3,2,1,0:T(8,128)(2,1)S(1)}, u32[]{:S(2)}, u32[]{:S(2)}) %collective-permute-start.19) | collective-permute-done | bytes 491552 | tf_op jit(solution)/shard_map/ppermute | solution.py:401
  128.7 1.6 %collective-permute-start.20 = (bf16[4,24,640]{2,1,0:T(8,128)(2,1)S(1)}, bf16[4,24,640]{2,1,0:T(8,128)(2,1)S(1)}, u32[]{:S(2)}, u32[]{:S(2)}) collective-permute-start(bf16[4,24,640]{2,1,0:T(8,128)(2,1)S(1)} %get-tuple-element.74), channel_id=1, source_target_pairs={{0,2},{1,3},{2,0},{3,1},{4,6},{5,7},{6,4},{7,5},{8,10},{9,11},{10,... | collective-permute-start | bytes 368648 | tf_op jit(solution)/shard_map/ppermute | solution.py:401
  130.3 3.8 %collective-permute-done.20.taken = bf16[4,24,640]{2,1,0:T(8,128)(2,1)S(1)} collective-permute-done((bf16[4,24,640]{2,1,0:T(8,128)(2,1)S(1)}, bf16[4,24,640]{2,1,0:T(8,128)(2,1)S(1)}, u32[]{:S(2)}, u32[]{:S(2)}) %collective-permute-start.20) | collective-permute-done | bytes 122912 | tf_op jit(solution)/shard_map/ppermute | solution.py:401
  134.1 0.4 collective-permute-start.21
  134.5 2.8 %collective-permute-start.22 = (bf16[24,640]{1,0:T(8,128)(2,1)S(1)}, bf16[24,640]{1,0:T(8,128)(2,1)S(1)}, u32[]{:S(2)}, u32[]{:S(2)}) collective-permute-start(bf16[24,640]{1,0:T(8,128)(2,1)S(1)} %get-tuple-element.77), channel_id=1, source_target_pairs={{0,16},{4,20},{8,24},{12,28},{16,0},{20,4},{24,8},{28,12},{1,17},{... | collective-permute-start | bytes 92168 | tf_op jit(solution)/shard_map/ppermute | solution.py:398
  137.3 1.3 collective-permute-start.23
  138.6 0.7 collective-permute-done.22.refs_2_
  139.3 3.7 %collective-permute-done.23.refs_3_ = bf16[24,640]{1,0:T(8,128)(2,1)S(1)} collective-permute-done((bf16[24,640]{1,0:T(8,128)(2,1)S(1)}, bf16[24,640]{1,0:T(8,128)(2,1)S(1)}, u32[]{:S(2)}, u32[]{:S(2)}) %collective-permute-start.23) | collective-permute-done | bytes 30752 | tf_op jit(solution)/shard_map/ppermute | solution.py:398
  143.0 1.2 shard_map.108
  (62 shorter events, 2.1 us)
Async XLA Ops:
  0.0 1.7 %copy-start = (bf16[2,3,320,640]{3,2,1,0:T(8,128)(2,1)S(1)}, bf16[2,3,320,640]{3,2,1,0:T(8,128)(2,1)}, u32[]{:S(2)}) copy-start(bf16[2,3,320,640]{3,2,1,0:T(8,128)(2,1)} %weights.7) | copy-start | bytes 7372804
  1.7 3.3 %copy-start.4 = (s32[24,2560]{1,0:T(8,128)S(1)}, s32[24,2560]{1,0:T(8,128)}, u32[]{:S(2)}) copy-start(s32[24,2560]{1,0:T(8,128)} %in_bits.1) | copy-start | bytes 737284
  1.9 41.3 %collective-permute-start.6 = (bf16[2,2,320,640]{3,2,1,0:T(8,128)(2,1)S(1)}, bf16[2,2,320,640]{3,2,1,0:T(8,128)(2,1)S(1)}, u32[]{:S(2)}, u32[]{:S(2)}) collective-permute-start(bf16[2,2,320,640]{3,2,1,0:T(8,128)(2,1)S(1)} %shard_map.91), channel_id=1, source_target_pairs={{0,4},{4,0},{8,12},{12,8},{16,20},{20,16},{24,28},{28,24},{1,5},{5... | collective-permute-start | bytes 4915208 | tf_op jit(solution)/shard_map/ppermute | solution.py:395
  5.0 1.1 copy-start.3
  6.1 0.9 copy-start.6
  7.0 34.4 %copy-start.2 = (s32[96,2560]{1,0:T(8,128)S(1)}, s32[96,2560]{1,0:T(8,128)}, u32[]{:S(2)}) copy-start(s32[96,2560]{1,0:T(8,128)} %out_bits) | copy-start | bytes 2949124
  7.7 33.7 %copy-start.1 = (bf16[2,3,320,640]{3,2,1,0:T(8,128)(2,1)S(1)}, bf16[2,3,320,640]{3,2,1,0:T(8,128)(2,1)}, u32[]{:S(2)}) copy-start(bf16[2,3,320,640]{3,2,1,0:T(8,128)(2,1)} %weights.7) | copy-start | bytes 7372804
  7.7 33.7 %copy-start.5 = (s32[96,640]{1,0:T(8,128)S(1)}, s32[96,640]{1,0:T(8,128)}, u32[]{:S(2)}) copy-start(s32[96,640]{1,0:T(8,128)} %mix_bits.1) | copy-start | bytes 737284
  7.7 22.9 %collective-permute-start.1 = (bf16[14,24,640]{2,1,0:T(8,128)(2,1)S(1)}, bf16[14,24,640]{2,1,0:T(8,128)(2,1)S(1)}, u32[]{:S(2)}, u32[]{:S(2)}) collective-permute-start(bf16[14,24,640]{2,1,0:T(8,128)(2,1)S(1)} %get-tuple-element.45.signs_0), channel_id=1, source_target_pairs={{0,16},{4,20},{8,24},{12,28},{16,0},{20,4},{24,8},{28,12},{1,17},{... | collective-permute-start | bytes 1290248 | tf_op jit(solution)/shard_map/ppermute | solution.py:398
  10.4 21.4 %collective-permute-start = (bf16[14,24,640]{2,1,0:T(8,128)(2,1)S(1)}, bf16[14,24,640]{2,1,0:T(8,128)(2,1)S(1)}, u32[]{:S(2)}, u32[]{:S(2)}) collective-permute-start(bf16[14,24,640]{2,1,0:T(8,128)(2,1)S(1)} %get-tuple-element.44), channel_id=1, source_target_pairs={{0,8},{4,12},{8,0},{12,4},{16,24},{20,28},{24,16},{28,20},{1,9},{5... | collective-permute-start | bytes 1290248 | tf_op jit(solution)/shard_map/ppermute | solution.py:398
  12.0 19.8 %collective-permute-start.2 = (bf16[2,24,640]{2,1,0:T(8,128)(2,1)S(1)}, bf16[2,24,640]{2,1,0:T(8,128)(2,1)S(1)}, u32[]{:S(2)}, u32[]{:S(2)}) collective-permute-start(bf16[2,24,640]{2,1,0:T(8,128)(2,1)S(1)} %get-tuple-element.46), channel_id=1, source_target_pairs={{0,24},{4,28},{8,16},{12,20},{16,8},{20,12},{24,0},{28,4},{1,25},{... | collective-permute-start | bytes 184328 | tf_op jit(solution)/shard_map/ppermute | solution.py:398
  31.8 9.7 %collective-permute-start.4 = (bf16[12,24,640]{2,1,0:T(8,128)(2,1)S(1)}, bf16[12,24,640]{2,1,0:T(8,128)(2,1)S(1)}, u32[]{:S(2)}, u32[]{:S(2)}) collective-permute-start(bf16[12,24,640]{2,1,0:T(8,128)(2,1)S(1)} %shard_map.95), channel_id=1, source_target_pairs={{0,8},{4,12},{8,0},{12,4},{16,24},{20,28},{24,16},{28,20},{1,9},{5... | collective-permute-start | bytes 1105928 | tf_op jit(solution)/shard_map/ppermute | solution.py:398
  32.7 7.6 %collective-permute-start.3 = (bf16[4,2,24,640]{3,2,1,0:T(8,128)(2,1)S(1)}, bf16[4,2,24,640]{3,2,1,0:T(8,128)(2,1)S(1)}, u32[]{:S(2)}, u32[]{:S(2)}) collective-permute-start(bf16[4,2,24,640]{3,2,1,0:T(8,128)(2,1)S(1)} %shard_map.93.own), channel_id=1, source_target_pairs={{0,2},{1,3},{2,0},{3,1},{4,6},{5,7},{6,4},{7,5},{8,10},{9,11},{10,... | collective-permute-start | bytes 737288 | tf_op jit(solution)/shard_map/ppermute | solution.py:401
  41.4 2.7 %collective-permute-start.5 = (bf16[2,4,2,24,640]{4,3,2,1,0:T(8,128)(2,1)S(1)}, bf16[2,4,2,24,640]{4,3,2,1,0:T(8,128)(2,1)S(1)}, u32[]{:S(2)}, u32[]{:S(2)}) collective-permute-start(bf16[2,4,2,24,640]{4,3,2,1,0:T(8,128)(2,1)S(1)} %shard_map.94.own), channel_id=1, source_target_pairs={{0,1},{1,0},{2,3},{3,2},{4,5},{5,4},{6,7},{7,6},{8,9},{9,8},{10,11... | collective-permute-start | bytes 1474568 | tf_op jit(solution)/shard_map/ppermute | solution.py:401
  43.3 24.9 %collective-permute-start.8 = (bf16[2,320,640]{2,1,0:T(8,128)(2,1)S(1)}, bf16[2,320,640]{2,1,0:T(8,128)(2,1)S(1)}, u32[]{:S(2)}, u32[]{:S(2)}) collective-permute-start(bf16[2,320,640]{2,1,0:T(8,128)(2,1)S(1)} %get-tuple-element.56), channel_id=1, source_target_pairs={{0,4},{4,0},{8,12},{12,8},{16,20},{20,16},{24,28},{28,24},{1,5},{5... | collective-permute-start | bytes 2457608 | tf_op jit(solution)/shard_map/ppermute | solution.py:395
  48.8 15.5 %collective-permute-start.7 = (bf16[2304,128]{1,0:T(8,128)(2,1)S(1)}, bf16[2304,128]{1,0:T(8,128)(2,1)S(1)}, u32[]{:S(2)}, u32[]{:S(2)}) collective-permute-start(bf16[2304,128]{1,0:T(8,128)(2,1)S(1)} %get-tuple-element.51), channel_id=1, source_target_pairs={{0,8},{4,12},{8,0},{12,4},{16,24},{20,28},{24,16},{28,20},{1,9},{5... | collective-permute-start | bytes 1769480 | tf_op jit(solution)/shard_map/ppermute | solution.py:398
  64.4 20.9 %collective-permute-start.11 = (bf16[1536,128]{1,0:T(8,128)(2,1)S(1)}, bf16[1536,128]{1,0:T(8,128)(2,1)S(1)}, u32[]{:S(2)}, u32[]{:S(2)}) collective-permute-start(bf16[1536,128]{1,0:T(8,128)(2,1)S(1)} %get-tuple-element.63), channel_id=1, source_target_pairs={{0,16},{4,20},{8,24},{12,28},{16,0},{20,4},{24,8},{28,12},{1,17},{... | collective-permute-start | bytes 1179656 | tf_op jit(solution)/shard_map/ppermute | solution.py:398
  68.2 17.2 %copy-start.7 = (f32[640]{0:T(1024)S(1)}, f32[640]{0:T(1024)}, u32[]{:S(2)}) copy-start(f32[640]{0:T(1024)} %param.14) | copy-start | bytes 7684
  70.1 20.2 %copy-start.9 = (bf16[2,640,320]{1,2,0:T(8,128)(2,1)S(1)}, bf16[2,640,320]{1,2,0:T(8,128)(2,1)}, u32[]{:S(2)}) copy-start(bf16[2,640,320]{1,2,0:T(8,128)(2,1)} %param.15) | copy-start | bytes 2457604
  70.1 34.9 %copy-start.8 = (f32[640]{0:T(1024)S(1)}, f32[640]{0:T(1024)}, u32[]{:S(2)}) copy-start(f32[640]{0:T(1024)} %param.13) | copy-start | bytes 7684
  70.1 11.3 %collective-permute-start.9 = (bf16[960,128]{1,0:T(8,128)(2,1)S(1)}, bf16[960,128]{1,0:T(8,128)(2,1)S(1)}, u32[]{:S(2)}, u32[]{:S(2)}) collective-permute-start(bf16[960,128]{1,0:T(8,128)(2,1)S(1)} %get-tuple-element.59), channel_id=1, source_target_pairs={{0,8},{4,12},{8,0},{12,4},{16,24},{20,28},{24,16},{28,20},{1,9},{5... | collective-permute-start | bytes 737288 | tf_op jit(solution)/shard_map/ppermute | solution.py:398
  86.1 18.9 %collective-permute-start.12 = (bf16[1536,128]{1,0:T(8,128)(2,1)S(1)}, bf16[1536,128]{1,0:T(8,128)(2,1)S(1)}, u32[]{:S(2)}, u32[]{:S(2)}) collective-permute-start(bf16[1536,128]{1,0:T(8,128)(2,1)S(1)} %shard_map.102.own), channel_id=1, source_target_pairs={{0,4},{4,0},{8,12},{12,8},{16,20},{20,16},{24,28},{28,24},{1,5},{5... | collective-permute-start | bytes 1179656 | tf_op jit(solution)/shard_map/ppermute | solution.py:395
  87.3 23.6 %collective-permute-start.17 = (bf16[8,24,640]{2,1,0:T(8,128)(2,1)}, bf16[8,24,640]{2,1,0:T(8,128)(2,1)S(1)}, u32[]{:S(2)}, u32[]{:S(2)}) collective-permute-start(bf16[8,24,640]{2,1,0:T(8,128)(2,1)} %get-tuple-element.70), channel_id=1, source_target_pairs={{0,16},{4,20},{8,24},{12,28},{16,0},{20,4},{24,8},{28,12},{1,17},{... | collective-permute-start | bytes 737288 | tf_op jit(solution)/shard_map/ppermute | solution.py:398
  87.3 17.7 %collective-permute-start.10 = (bf16[480,128]{1,0:T(8,128)(2,1)S(1)}, bf16[480,128]{1,0:T(8,128)(2,1)S(1)}, u32[]{:S(2)}, u32[]{:S(2)}) collective-permute-start(bf16[480,128]{1,0:T(8,128)(2,1)S(1)} %get-tuple-element.62), channel_id=1, source_target_pairs={{0,16},{4,20},{8,24},{12,28},{16,0},{20,4},{24,8},{28,12},{1,17},{... | collective-permute-start | bytes 368648 | tf_op jit(solution)/shard_map/ppermute | solution.py:398
  90.3 29.1 %collective-permute-start.16 = (bf16[2,320,640]{2,1,0:T(8,128)(2,1)S(1)}, bf16[2,320,640]{2,1,0:T(8,128)(2,1)S(1)}, u32[]{:S(2)}, u32[]{:S(2)}) collective-permute-start(bf16[2,320,640]{2,1,0:T(8,128)(2,1)S(1)} %bitcast.36), channel_id=1, source_target_pairs={{0,4},{4,0},{8,12},{12,8},{16,20},{20,16},{24,28},{28,24},{1,5},{5... | collective-permute-start | bytes 2457608 | tf_op jit(solution)/shard_map/ppermute | solution.py:395
  105.0 14.3 %copy-start.10 = (bf16[2,640,320]{1,2,0:T(8,128)(2,1)S(1)}, bf16[2,640,320]{1,2,0:T(8,128)(2,1)}, u32[]{:S(2)}) copy-start(bf16[2,640,320]{1,2,0:T(8,128)(2,1)} %param.15) | copy-start | bytes 2457604
  106.4 8.2 %collective-permute-start.13 = (bf16[480,128]{1,0:T(8,128)(2,1)S(1)}, bf16[480,128]{1,0:T(8,128)(2,1)S(1)}, u32[]{:S(2)}, u32[]{:S(2)}) collective-permute-start(bf16[480,128]{1,0:T(8,128)(2,1)S(1)} %shard_map.103), channel_id=1, source_target_pairs={{0,8},{4,12},{8,0},{12,4},{16,24},{20,28},{24,16},{28,20},{1,9},{5... | collective-permute-start | bytes 368648 | tf_op jit(solution)/shard_map/ppermute | solution.py:398
  106.5 12.6 %collective-permute-start.14 = (bf16[480,128]{1,0:T(8,128)(2,1)S(1)}, bf16[480,128]{1,0:T(8,128)(2,1)S(1)}, u32[]{:S(2)}, u32[]{:S(2)}) collective-permute-start(bf16[480,128]{1,0:T(8,128)(2,1)S(1)} %shard_map.103), channel_id=1, source_target_pairs={{0,16},{4,20},{8,24},{12,28},{16,0},{20,4},{24,8},{28,12},{1,17},{... | collective-permute-start | bytes 368648 | tf_op jit(solution)/shard_map/ppermute | solution.py:398
  109.6 9.6 %collective-permute-start.15 = (bf16[480,128]{1,0:T(8,128)(2,1)S(1)}, bf16[480,128]{1,0:T(8,128)(2,1)S(1)}, u32[]{:S(2)}, u32[]{:S(2)}) collective-permute-start(bf16[480,128]{1,0:T(8,128)(2,1)S(1)} %shard_map.103), channel_id=1, source_target_pairs={{0,24},{4,28},{8,16},{12,20},{16,8},{20,12},{24,0},{28,4},{1,25},{... | collective-permute-start | bytes 368648 | tf_op jit(solution)/shard_map/ppermute | solution.py:398
  110.9 14.0 %collective-permute-start.18 = (bf16[12,24,640]{2,1,0:T(8,128)(2,1)S(1)}, bf16[12,24,640]{2,1,0:T(8,128)(2,1)S(1)}, u32[]{:S(2)}, u32[]{:S(2)}) collective-permute-start(bf16[12,24,640]{2,1,0:T(8,128)(2,1)S(1)} %shard_map.104), channel_id=1, source_target_pairs={{0,8},{4,12},{8,0},{12,4},{16,24},{20,28},{24,16},{28,20},{1,9},{5... | collective-permute-start | bytes 1105928 | tf_op jit(solution)/shard_map/ppermute | solution.py:398
  126.6 1.9 %collective-permute-start.19 = (bf16[2,4,2,24,640]{4,3,2,1,0:T(8,128)(2,1)S(1)}, bf16[2,4,2,24,640]{4,3,2,1,0:T(8,128)(2,1)S(1)}, u32[]{:S(2)}, u32[]{:S(2)}) collective-permute-start(bf16[2,4,2,24,640]{4,3,2,1,0:T(8,128)(2,1)S(1)} %get-tuple-element.81), channel_id=1, source_target_pairs={{0,1},{1,0},{2,3},{3,2},{4,5},{5,4},{6,7},{7,6},{8,9},{9,8},{10,11... | collective-permute-start | bytes 1474568 | tf_op jit(solution)/shard_map/ppermute | solution.py:401
  128.7 5.4 %collective-permute-start.20 = (bf16[4,24,640]{2,1,0:T(8,128)(2,1)S(1)}, bf16[4,24,640]{2,1,0:T(8,128)(2,1)S(1)}, u32[]{:S(2)}, u32[]{:S(2)}) collective-permute-start(bf16[4,24,640]{2,1,0:T(8,128)(2,1)S(1)} %get-tuple-element.74), channel_id=1, source_target_pairs={{0,2},{1,3},{2,0},{3,1},{4,6},{5,7},{6,4},{7,5},{8,10},{9,11},{10,... | collective-permute-start | bytes 368648 | tf_op jit(solution)/shard_map/ppermute | solution.py:401
  134.1 4.5 %collective-permute-start.21 = (bf16[24,640]{1,0:T(8,128)(2,1)S(1)}, bf16[24,640]{1,0:T(8,128)(2,1)S(1)}, u32[]{:S(2)}, u32[]{:S(2)}) collective-permute-start(bf16[24,640]{1,0:T(8,128)(2,1)S(1)} %get-tuple-element.76), channel_id=1, source_target_pairs={{0,8},{4,12},{8,0},{12,4},{16,24},{20,28},{24,16},{28,20},{1,9},{5... | collective-permute-start | bytes 92168 | tf_op jit(solution)/shard_map/ppermute | solution.py:398
  134.5 4.8 %collective-permute-start.22 = (bf16[24,640]{1,0:T(8,128)(2,1)S(1)}, bf16[24,640]{1,0:T(8,128)(2,1)S(1)}, u32[]{:S(2)}, u32[]{:S(2)}) collective-permute-start(bf16[24,640]{1,0:T(8,128)(2,1)S(1)} %get-tuple-element.77), channel_id=1, source_target_pairs={{0,16},{4,20},{8,24},{12,28},{16,0},{20,4},{24,8},{28,12},{1,17},{... | collective-permute-start | bytes 92168 | tf_op jit(solution)/shard_map/ppermute | solution.py:398
  137.3 5.7 %collective-permute-start.23 = (bf16[24,640]{1,0:T(8,128)(2,1)S(1)}, bf16[24,640]{1,0:T(8,128)(2,1)S(1)}, u32[]{:S(2)}, u32[]{:S(2)}) collective-permute-start(bf16[24,640]{1,0:T(8,128)(2,1)S(1)} %get-tuple-element.78), channel_id=1, source_target_pairs={{0,24},{4,28},{8,16},{12,20},{16,8},{20,12},{24,0},{28,4},{1,25},{... | collective-permute-start | bytes 92168 | tf_op jit(solution)/shard_map/ppermute | solution.py:398

commit v4 on v3

--- a/solution.py
+++ b/solution.py
@@ -438,6 +438,7 @@
         [SMEM] + [VMEM] * 2 + [ANY],
         [pltpu.SemaphoreType.DMA((2,))],
     )(place, after(out_bits, blocks[0]), mix_bits, qkv_weights)
+    late_far = swap_z(after(late_far, held), 2)
     partner_query = swap_x(after(query_weights, partner_early, forward))
     out_t = jnp.transpose(out_weights, (0, 2, 1))
     out_partner = swap_x(after(out_t, partner_query))
@@ -474,7 +475,7 @@
     send, both_total = middle(both_own, both_two, taken)
     both_last = swap_z(send, 2)
     query_send, query_own, query_two = project(
-        (0,), after(rows, both_total), partner_query.reshape(2, 1, slab, columns),
+        (0,), after(rows, both_total, late_far), partner_query.reshape(2, 1, slab, columns),
     )
     query_taken = swap_z(query_send, 1)
     send, query_total = middle(query_own, query_two, after(query_taken, both_total))
@@ -484,16 +485,14 @@
         shape(4 * half, HEAD), VMEM, [SMEM] + [VMEM] * 3,
     )(place, both_total, after(both_last, query_total), gain_key.reshape(heads, HEAD))
     both_partner = swap_x(both)
-    late_far = swap_z(after(late_far, both), 2)
+    late_got = call(near_kernel, shape(2 * team + 4, own_rows, 2 * slab), VMEM, [VMEM] * 2)(
+        late_near, late_far
+    )
+    late_got = swap_z(after(late_got, both), 1)
     done = call(
         functools.partial(attend_kernel, half),
         shape(half + size, HEAD), VMEM, [SMEM] + [VMEM] * 5,
     )(place, query_total, query_last, gain_query.reshape(heads, HEAD), both, both_partner)
-
-    late_got = call(near_kernel, shape(2 * team + 4, own_rows, 2 * slab), VMEM, [VMEM] * 2)(
-        after(late_near, done), late_far
-    )
-    late_got = swap_z(late_got, 1)
 
     by_head, last_head = [], []
     for k in steps:

time: 144 us -> 139 us (0.965)
  waiting for transfers between devices: 91.6 us -> 82.5 us
  starting transfers between devices: 32.3 us -> 35.9 us
    ppermute x16, waiting for transfers between devices: 79.8 us -> 69.8 us  [swap_z(): lax.ppermute(value, 'blk', [(i, i ^ 2 * step) for i in range(groups)])]
    ppermute x16, starting transfers between devices: 23.1 us -> 26.7 us  [swap_z(): lax.ppermute(value, 'blk', [(i, i ^ 2 * step) for i in range(groups)])]
    unnamed x23 -> x19, local copies, waits for them, and re-layouts: 3.77 us -> 3.76 us
  transfers between devices with their start and end apart: 24 -> 24, of which waited for: 15 -> 15; matrix products, arithmetic and copies ran while one was open for 1% -> 0% of each run, Pallas kernels for 7% -> 8%
where the time goes in v4:
time: 139 us
  waiting for transfers between devices  82.5 us (59%)
  starting transfers between devices  35.9 us (26%)
  Pallas kernels  13 us (9%)
  local copies, waits for them, and re-layouts  3.88 us (3%)
  other arithmetic  2.14 us (2%)
    ppermute x16, waiting for transfers between devices, swap_z(): lax.ppermute(value, 'blk', [(i, i ^ 2 * step) for i in range(groups)])  69.8 us
    ppermute x16, starting transfers between devices, swap_z(): lax.ppermute(value, 'blk', [(i, i ^ 2 * step) for i in range(groups)])  26.7 us
    ppermute x4, waiting for transfers between devices, swap_u(): return lax.ppermute(value, 'uly', [(i, i ^ bit) for i in range(team)])  11.8 us
    ppermute x4, starting transfers between devices, swap_x(): return lax.ppermute(value, 'blk', [(i, i ^ 1) for i in range(groups)])  6.01 us
    pallas_call x2, Pallas kernels, project(): call(functools.partial(project_kernel, parts, size), [shape(counts[0], HE...  4.95 us
    unnamed x19, local copies, waits for them, and re-layouts  3.76 us
    ppermute x4, starting transfers between devices, swap_u(): return lax.ppermute(value, 'uly', [(i, i ^ bit) for i in range(team)])  3.17 us
  transfers between devices with their start and end apart: 24, of which 15 were waited for; matrix products, arithmetic and copies ran while one was open for 0% of the time, Pallas kernels for 8%

profile of v4, /device:TPU:0, one launch (start us, length us, event | category | flops | bytes accessed | tf_op | source)
XLA Modules:
  0.0 139.0 jit_solution(1378904497014985459)
XLA Ops:
  0.0 1.7 %copy-done = bf16[2,3,320,640]{3,2,1,0:T(8,128)(2,1)S(1)} copy-done((bf16[2,3,320,640]{3,2,1,0:T(8,128)(2,1)S(1)}, bf16[2,3,320,640]{3,2,1,0:T(8,128)(2,1)}, u32[]{:S(2)}) %copy-start) | copy-done | bytes 2457624
  1.9 3.0 %collective-permute-start.6 = (bf16[2,2,320,640]{3,2,1,0:T(8,128)(2,1)S(1)}, bf16[2,2,320,640]{3,2,1,0:T(8,128)(2,1)S(1)}, u32[]{:S(2)}, u32[]{:S(2)}) collective-permute-start(bf16[2,2,320,640]{3,2,1,0:T(8,128)(2,1)S(1)} %shard_map.91), channel_id=1, source_target_pairs={{0,4},{4,0},{8,12},{12,8},{16,20},{20,16},{24,28},{28,24},{1,5},{5... | collective-permute-start | bytes 4915208 | tf_op jit(solution)/shard_map/ppermute | solution.py:395
  5.0 1.1 copy-done.3
  6.1 0.9 copy-done.6
  7.0 0.7 shard_map.92
  7.7 2.7 %collective-permute-start.1 = (bf16[14,24,640]{2,1,0:T(8,128)(2,1)S(1)}, bf16[14,24,640]{2,1,0:T(8,128)(2,1)S(1)}, u32[]{:S(2)}, u32[]{:S(2)}) collective-permute-start(bf16[14,24,640]{2,1,0:T(8,128)(2,1)S(1)} %get-tuple-element.46.signs_0), channel_id=1, source_target_pairs={{0,16},{4,20},{8,24},{12,28},{16,0},{20,4},{24,8},{28,12},{1,17},{... | collective-permute-start | bytes 1290248 | tf_op jit(solution)/shard_map/ppermute | solution.py:398
  10.4 1.6 %collective-permute-start = (bf16[14,24,640]{2,1,0:T(8,128)(2,1)S(1)}, bf16[14,24,640]{2,1,0:T(8,128)(2,1)S(1)}, u32[]{:S(2)}, u32[]{:S(2)}) collective-permute-start(bf16[14,24,640]{2,1,0:T(8,128)(2,1)S(1)} %get-tuple-element.45), channel_id=1, source_target_pairs={{0,8},{4,12},{8,0},{12,4},{16,24},{20,28},{24,16},{28,20},{1,9},{5... | collective-permute-start | bytes 1290248 | tf_op jit(solution)/shard_map/ppermute | solution.py:398
  12.2 18.5 %collective-permute-done.1.refs_2_.taken.signs_2 = bf16[14,24,640]{2,1,0:T(8,128)(2,1)S(1)} collective-permute-done((bf16[14,24,640]{2,1,0:T(8,128)(2,1)S(1)}, bf16[14,24,640]{2,1,0:T(8,128)(2,1)S(1)}, u32[]{:S(2)}, u32[]{:S(2)}) %collective-permute-start.1) | collective-permute-done | bytes 430112 | tf_op jit(solution)/shard_map/ppermute | solution.py:398
  30.7 1.1 collective-permute-done.2.refs_3_
  31.8 0.9 collective-permute-start.4
  32.7 1.5 %collective-permute-start.3 = (bf16[4,2,24,640]{3,2,1,0:T(8,128)(2,1)S(1)}, bf16[4,2,24,640]{3,2,1,0:T(8,128)(2,1)S(1)}, u32[]{:S(2)}, u32[]{:S(2)}) collective-permute-start(bf16[4,2,24,640]{3,2,1,0:T(8,128)(2,1)S(1)} %shard_map.93.own), channel_id=1, source_target_pairs={{0,2},{1,3},{2,0},{3,1},{4,6},{5,7},{6,4},{7,5},{8,10},{9,11},{10,... | collective-permute-start | bytes 737288 | tf_op jit(solution)/shard_map/ppermute | solution.py:401
  34.2 6.1 %collective-permute-done.3.taken = bf16[4,2,24,640]{3,2,1,0:T(8,128)(2,1)S(1)} collective-permute-done((bf16[4,2,24,640]{3,2,1,0:T(8,128)(2,1)S(1)}, bf16[4,2,24,640]{3,2,1,0:T(8,128)(2,1)S(1)}, u32[]{:S(2)}, u32[]{:S(2)}) %collective-permute-start.3) | collective-permute-done | bytes 245792 | tf_op jit(solution)/shard_map/ppermute | solution.py:401
  40.3 1.1 collective-permute-done.4.signs_3
  41.5 1.1 shard_map.99
  42.6 0.9 collective-permute-start.9
  43.5 1.5 %shard_map.96.rows = bf16[2,2,384,320]{3,2,1,0:T(8,128)(2,1)S(1)} custom-call(s32[3]{0:T(128)S(1)} %pad_add_fusion.place, bf16[2,4,2,24,640]{4,3,2,1,0:T(8,128)(2,1)S(1)} %shard_map.94.own, bf16[2,4,2,24,640]{4,3,2,1,0:T(8,128)(2,1)S(1)} %collective-permute-done.5.taken), custom_call_target="tpu_custom_call" | custom-call | tf_op jit(solution)/shard_map/pallas_call | solution.py:429
  45.0 3.1 %shard_map.97 = (bf16[2304,128]{1,0:T(8,128)(2,1)S(1)}, f32[1536,128]{1,0:T(8,128)S(1)}, f32[768,128]{1,0:T(8,128)S(1)}) custom-call(s32[3]{0:T(128)S(1)} %pad_add_fusion.place, bf16[2,2,384,320]{3,2,1,0:T(8,128)(2,1)S(1)} %shard_map.96.rows, bf16[2,3,320,640]{3,2,1,0:T(8,128)(2,1)S(1)} %copy-done.1, ...), custom_call_target="tpu_custom_call" | custom-call | tf_op jit(solution)/shard_map/pallas_call | solution.py:452
  48.1 1.8 %collective-permute-start.7 = (bf16[2304,128]{1,0:T(8,128)(2,1)S(1)}, bf16[2304,128]{1,0:T(8,128)(2,1)S(1)}, u32[]{:S(2)}, u32[]{:S(2)}) collective-permute-start(bf16[2304,128]{1,0:T(8,128)(2,1)S(1)} %get-tuple-element.52), channel_id=1, source_target_pairs={{0,8},{4,12},{8,0},{12,4},{16,24},{20,28},{24,16},{28,20},{1,9},{5... | collective-permute-start | bytes 1769480 | tf_op jit(solution)/shard_map/ppermute | solution.py:398
  49.9 2.2 %collective-permute-start.8 = (bf16[8,24,640]{2,1,0:T(8,128)(2,1)S(1)}, bf16[8,24,640]{2,1,0:T(8,128)(2,1)S(1)}, u32[]{:S(2)}, u32[]{:S(2)}) collective-permute-start(bf16[8,24,640]{2,1,0:T(8,128)(2,1)S(1)} %get-tuple-element.56), channel_id=1, source_target_pairs={{0,16},{4,20},{8,24},{12,28},{16,0},{20,4},{24,8},{28,12},{1,17},{... | collective-permute-start | bytes 737288 | tf_op jit(solution)/shard_map/ppermute | solution.py:398
  52.1 16.8 %collective-permute-done.7.taken = bf16[2304,128]{1,0:T(8,128)(2,1)S(1)} collective-permute-done((bf16[2304,128]{1,0:T(8,128)(2,1)S(1)}, bf16[2304,128]{1,0:T(8,128)(2,1)S(1)}, u32[]{:S(2)}, u32[]{:S(2)}) %collective-permute-start.7) | collective-permute-done | bytes 589856 | tf_op jit(solution)/shard_map/ppermute | solution.py:398
  69.0 1.5 %collective-permute-start.12 = (bf16[1536,128]{1,0:T(8,128)(2,1)S(1)}, bf16[1536,128]{1,0:T(8,128)(2,1)S(1)}, u32[]{:S(2)}, u32[]{:S(2)}) collective-permute-start(bf16[1536,128]{1,0:T(8,128)(2,1)S(1)} %get-tuple-element.66), channel_id=1, source_target_pairs={{0,16},{4,20},{8,24},{12,28},{16,0},{20,4},{24,8},{28,12},{1,17},{... | collective-permute-start | bytes 1179656 | tf_op jit(solution)/shard_map/ppermute | solution.py:398
  70.6 1.9 %shard_map.100 = (bf16[960,128]{1,0:T(8,128)(2,1)S(1)}, f32[480,128]{1,0:T(8,128)S(1)}, f32[480,128]{1,0:T(8,128)S(1)}) custom-call(s32[3]{0:T(128)S(1)} %pad_add_fusion.place, bf16[2,2,384,320]{3,2,1,0:T(8,128)(2,1)S(1)} %shard_map.96.rows, bf16[2,3,320,640]{3,2,1,0:T(8,128)(2,1)S(1)} %copy-done.1, bf16[2,1,320,640]{3,2,1,0:T(8,128)(2,1)S(1)} %bitcast.32, ...), custom_call_target="tpu_custom_call" | custom-call | tf_op jit(solution)/shard_map/pallas_call | solution.py:452
  72.5 2.6 %collective-permute-start.10 = (bf16[960,128]{1,0:T(8,128)(2,1)S(1)}, bf16[960,128]{1,0:T(8,128)(2,1)S(1)}, u32[]{:S(2)}, u32[]{:S(2)}) collective-permute-start(bf16[960,128]{1,0:T(8,128)(2,1)S(1)} %get-tuple-element.62), channel_id=1, source_target_pairs={{0,8},{4,12},{8,0},{12,4},{16,24},{20,28},{24,16},{28,20},{1,9},{5... | collective-permute-start | bytes 737288 | tf_op jit(solution)/shard_map/ppermute | solution.py:398
  75.0 8.8 %collective-permute-done.10.taken = bf16[960,128]{1,0:T(8,128)(2,1)S(1)} collective-permute-done((bf16[960,128]{1,0:T(8,128)(2,1)S(1)}, bf16[960,128]{1,0:T(8,128)(2,1)S(1)}, u32[]{:S(2)}, u32[]{:S(2)}) %collective-permute-start.10) | collective-permute-done | bytes 245792 | tf_op jit(solution)/shard_map/ppermute | solution.py:398
  83.9 5.0 %collective-permute-done.12.taken = bf16[1536,128]{1,0:T(8,128)(2,1)S(1)} collective-permute-done((bf16[1536,128]{1,0:T(8,128)(2,1)S(1)}, bf16[1536,128]{1,0:T(8,128)(2,1)S(1)}, u32[]{:S(2)}, u32[]{:S(2)}) %collective-permute-start.12) | collective-permute-done | bytes 393248 | tf_op jit(solution)/shard_map/ppermute | solution.py:398
  88.8 0.8 shard_map.102.own
  89.6 1.2 collective-permute-start.13
  90.9 2.9 %collective-permute-start.11 = (bf16[480,128]{1,0:T(8,128)(2,1)S(1)}, bf16[480,128]{1,0:T(8,128)(2,1)S(1)}, u32[]{:S(2)}, u32[]{:S(2)}) collective-permute-start(bf16[480,128]{1,0:T(8,128)(2,1)S(1)} %get-tuple-element.65), channel_id=1, source_target_pairs={{0,16},{4,20},{8,24},{12,28},{16,0},{20,4},{24,8},{28,12},{1,17},{... | collective-permute-start | bytes 368648 | tf_op jit(solution)/shard_map/ppermute | solution.py:398
  93.9 0.9 collective-permute-start.17
  94.7 6.1 %collective-permute-done.11.taken = bf16[480,128]{1,0:T(8,128)(2,1)S(1)} collective-permute-done((bf16[480,128]{1,0:T(8,128)(2,1)S(1)}, bf16[480,128]{1,0:T(8,128)(2,1)S(1)}, u32[]{:S(2)}, u32[]{:S(2)}) %collective-permute-start.11) | collective-permute-done | bytes 122912 | tf_op jit(solution)/shard_map/ppermute | solution.py:398
  100.9 0.9 collective-permute-done.13.partner
  101.7 1.4 %shard_map.103 = bf16[480,128]{1,0:T(8,128)(2,1)S(1)} custom-call(s32[3]{0:T(128)S(1)} %pad_add_fusion.place, f32[480,128]{1,0:T(8,128)S(1)} %get-tuple-element.64.total, bf16[480,128]{1,0:T(8,128)(2,1)S(1)} %collective-permute-done.11.taken, f32[5,128]{1,0:T(8,128)S(1)} %bitcast.35, bf16[1536,128]{1,0:T(8,128)(2,1)S(1)} %shard_map.102.own, ...), custom_call_target="tpu_custom_call" | custom-call | tf_op jit(solution)/shard_map/pallas_call | solution.py:492
  103.2 3.3 %collective-permute-start.14 = (bf16[480,128]{1,0:T(8,128)(2,1)S(1)}, bf16[480,128]{1,0:T(8,128)(2,1)S(1)}, u32[]{:S(2)}, u32[]{:S(2)}) collective-permute-start(bf16[480,128]{1,0:T(8,128)(2,1)S(1)} %shard_map.103), channel_id=1, source_target_pairs={{0,8},{4,12},{8,0},{12,4},{16,24},{20,28},{24,16},{28,20},{1,9},{5... | collective-permute-start | bytes 368648 | tf_op jit(solution)/shard_map/ppermute | solution.py:398
  106.5 2.4 %collective-permute-start.16 = (bf16[480,128]{1,0:T(8,128)(2,1)S(1)}, bf16[480,128]{1,0:T(8,128)(2,1)S(1)}, u32[]{:S(2)}, u32[]{:S(2)}) collective-permute-start(bf16[480,128]{1,0:T(8,128)(2,1)S(1)} %shard_map.103), channel_id=1, source_target_pairs={{0,24},{4,28},{8,16},{12,20},{16,8},{20,12},{24,0},{28,4},{1,25},{... | collective-permute-start | bytes 368648 | tf_op jit(solution)/shard_map/ppermute | solution.py:398
  109.6 0.7 collective-permute-done.14
  110.3 7.5 %collective-permute-done.15 = bf16[480,128]{1,0:T(8,128)(2,1)S(1)} collective-permute-done((bf16[480,128]{1,0:T(8,128)(2,1)S(1)}, bf16[480,128]{1,0:T(8,128)(2,1)S(1)}, u32[]{:S(2)}, u32[]{:S(2)}) %collective-permute-start.15) | collective-permute-done | bytes 122912 | tf_op jit(solution)/shard_map/ppermute | solution.py:398
  118.1 1.3 broadcast_select_fusion
  119.8 0.7 fusion.1
  120.5 0.7 fusion
  121.5 1.9 %collective-permute-done.19.taken = bf16[2,4,2,24,640]{4,3,2,1,0:T(8,128)(2,1)S(1)} collective-permute-done((bf16[2,4,2,24,640]{4,3,2,1,0:T(8,128)(2,1)S(1)}, bf16[2,4,2,24,640]{4,3,2,1,0:T(8,128)(2,1)S(1)}, u32[]{:S(2)}, u32[]{:S(2)}) %collective-permute-start.19) | collective-permute-done | bytes 491552 | tf_op jit(solution)/shard_map/ppermute | solution.py:401
  123.5 1.6 %collective-permute-start.20 = (bf16[4,24,640]{2,1,0:T(8,128)(2,1)S(1)}, bf16[4,24,640]{2,1,0:T(8,128)(2,1)S(1)}, u32[]{:S(2)}, u32[]{:S(2)}) collective-permute-start(bf16[4,24,640]{2,1,0:T(8,128)(2,1)S(1)} %get-tuple-element.76), channel_id=1, source_target_pairs={{0,2},{1,3},{2,0},{3,1},{4,6},{5,7},{6,4},{7,5},{8,10},{9,11},{10,... | collective-permute-start | bytes 368648 | tf_op jit(solution)/shard_map/ppermute | solution.py:401
  125.1 3.8 %collective-permute-done.20.taken = bf16[4,24,640]{2,1,0:T(8,128)(2,1)S(1)} collective-permute-done((bf16[4,24,640]{2,1,0:T(8,128)(2,1)S(1)}, bf16[4,24,640]{2,1,0:T(8,128)(2,1)S(1)}, u32[]{:S(2)}, u32[]{:S(2)}) %collective-permute-start.20) | collective-permute-done | bytes 122912 | tf_op jit(solution)/shard_map/ppermute | solution.py:401
  128.9 2.1 %collective-permute-start.21 = (bf16[24,640]{1,0:T(8,128)(2,1)S(1)}, bf16[24,640]{1,0:T(8,128)(2,1)S(1)}, u32[]{:S(2)}, u32[]{:S(2)}) collective-permute-start(bf16[24,640]{1,0:T(8,128)(2,1)S(1)} %get-tuple-element.78), channel_id=1, source_target_pairs={{0,8},{4,12},{8,0},{12,4},{16,24},{20,28},{24,16},{28,20},{1,9},{5... | collective-permute-start | bytes 92168 | tf_op jit(solution)/shard_map/ppermute | solution.py:398
  131.0 1.1 collective-permute-start.22
  132.1 1.3 collective-permute-start.23
  133.4 2.5 %collective-permute-done.22.refs_2_ = bf16[24,640]{1,0:T(8,128)(2,1)S(1)} collective-permute-done((bf16[24,640]{1,0:T(8,128)(2,1)S(1)}, bf16[24,640]{1,0:T(8,128)(2,1)S(1)}, u32[]{:S(2)}, u32[]{:S(2)}) %collective-permute-start.22) | collective-permute-done | bytes 30752 | tf_op jit(solution)/shard_map/ppermute | solution.py:398
  136.0 1.9 %collective-permute-done.23.refs_3_ = bf16[24,640]{1,0:T(8,128)(2,1)S(1)} collective-permute-done((bf16[24,640]{1,0:T(8,128)(2,1)S(1)}, bf16[24,640]{1,0:T(8,128)(2,1)S(1)}, u32[]{:S(2)}, u32[]{:S(2)}) %collective-permute-start.23) | collective-permute-done | bytes 30752 | tf_op jit(solution)/shard_map/ppermute | solution.py:398
  137.8 1.2 shard_map.108
  (58 shorter events, 2.8 us)
Async XLA Ops:
  0.0 1.7 %copy-start = (bf16[2,3,320,640]{3,2,1,0:T(8,128)(2,1)S(1)}, bf16[2,3,320,640]{3,2,1,0:T(8,128)(2,1)}, u32[]{:S(2)}) copy-start(bf16[2,3,320,640]{3,2,1,0:T(8,128)(2,1)} %weights.7) | copy-start | bytes 7372804
  1.7 3.3 %copy-start.4 = (s32[24,2560]{1,0:T(8,128)S(1)}, s32[24,2560]{1,0:T(8,128)}, u32[]{:S(2)}) copy-start(s32[24,2560]{1,0:T(8,128)} %in_bits.1) | copy-start | bytes 737284
  1.9 40.6 %collective-permute-start.6 = (bf16[2,2,320,640]{3,2,1,0:T(8,128)(2,1)S(1)}, bf16[2,2,320,640]{3,2,1,0:T(8,128)(2,1)S(1)}, u32[]{:S(2)}, u32[]{:S(2)}) collective-permute-start(bf16[2,2,320,640]{3,2,1,0:T(8,128)(2,1)S(1)} %shard_map.91), channel_id=1, source_target_pairs={{0,4},{4,0},{8,12},{12,8},{16,20},{20,16},{24,28},{28,24},{1,5},{5... | collective-permute-start | bytes 4915208 | tf_op jit(solution)/shard_map/ppermute | solution.py:395
  5.0 1.1 copy-start.3
  6.1 0.9 copy-start.6
  7.0 34.4 %copy-start.2 = (s32[96,2560]{1,0:T(8,128)S(1)}, s32[96,2560]{1,0:T(8,128)}, u32[]{:S(2)}) copy-start(s32[96,2560]{1,0:T(8,128)} %out_bits) | copy-start | bytes 2949124
  7.7 33.7 %copy-start.1 = (bf16[2,3,320,640]{3,2,1,0:T(8,128)(2,1)S(1)}, bf16[2,3,320,640]{3,2,1,0:T(8,128)(2,1)}, u32[]{:S(2)}) copy-start(bf16[2,3,320,640]{3,2,1,0:T(8,128)(2,1)} %weights.7) | copy-start | bytes 7372804
  7.7 33.7 %copy-start.5 = (s32[96,640]{1,0:T(8,128)S(1)}, s32[96,640]{1,0:T(8,128)}, u32[]{:S(2)}) copy-start(s32[96,640]{1,0:T(8,128)} %mix_bits.1) | copy-start | bytes 737284
  7.7 22.9 %collective-permute-start.1 = (bf16[14,24,640]{2,1,0:T(8,128)(2,1)S(1)}, bf16[14,24,640]{2,1,0:T(8,128)(2,1)S(1)}, u32[]{:S(2)}, u32[]{:S(2)}) collective-permute-start(bf16[14,24,640]{2,1,0:T(8,128)(2,1)S(1)} %get-tuple-element.46.signs_0), channel_id=1, source_target_pairs={{0,16},{4,20},{8,24},{12,28},{16,0},{20,4},{24,8},{28,12},{1,17},{... | collective-permute-start | bytes 1290248 | tf_op jit(solution)/shard_map/ppermute | solution.py:398
  10.4 21.4 %collective-permute-start = (bf16[14,24,640]{2,1,0:T(8,128)(2,1)S(1)}, bf16[14,24,640]{2,1,0:T(8,128)(2,1)S(1)}, u32[]{:S(2)}, u32[]{:S(2)}) collective-permute-start(bf16[14,24,640]{2,1,0:T(8,128)(2,1)S(1)} %get-tuple-element.45), channel_id=1, source_target_pairs={{0,8},{4,12},{8,0},{12,4},{16,24},{20,28},{24,16},{28,20},{1,9},{5... | collective-permute-start | bytes 1290248 | tf_op jit(solution)/shard_map/ppermute | solution.py:398
  12.0 19.8 %collective-permute-start.2 = (bf16[2,24,640]{2,1,0:T(8,128)(2,1)S(1)}, bf16[2,24,640]{2,1,0:T(8,128)(2,1)S(1)}, u32[]{:S(2)}, u32[]{:S(2)}) collective-permute-start(bf16[2,24,640]{2,1,0:T(8,128)(2,1)S(1)} %get-tuple-element.47), channel_id=1, source_target_pairs={{0,24},{4,28},{8,16},{12,20},{16,8},{20,12},{24,0},{28,4},{1,25},{... | collective-permute-start | bytes 184328 | tf_op jit(solution)/shard_map/ppermute | solution.py:398
  31.8 9.7 %collective-permute-start.4 = (bf16[12,24,640]{2,1,0:T(8,128)(2,1)S(1)}, bf16[12,24,640]{2,1,0:T(8,128)(2,1)S(1)}, u32[]{:S(2)}, u32[]{:S(2)}) collective-permute-start(bf16[12,24,640]{2,1,0:T(8,128)(2,1)S(1)} %shard_map.95), channel_id=1, source_target_pairs={{0,8},{4,12},{8,0},{12,4},{16,24},{20,28},{24,16},{28,20},{1,9},{5... | collective-permute-start | bytes 1105928 | tf_op jit(solution)/shard_map/ppermute | solution.py:398
  32.7 7.6 %collective-permute-start.3 = (bf16[4,2,24,640]{3,2,1,0:T(8,128)(2,1)S(1)}, bf16[4,2,24,640]{3,2,1,0:T(8,128)(2,1)S(1)}, u32[]{:S(2)}, u32[]{:S(2)}) collective-permute-start(bf16[4,2,24,640]{3,2,1,0:T(8,128)(2,1)S(1)} %shard_map.93.own), channel_id=1, source_target_pairs={{0,2},{1,3},{2,0},{3,1},{4,6},{5,7},{6,4},{7,5},{8,10},{9,11},{10,... | collective-permute-start | bytes 737288 | tf_op jit(solution)/shard_map/ppermute | solution.py:401
  41.4 2.0 %collective-permute-start.5 = (bf16[2,4,2,24,640]{4,3,2,1,0:T(8,128)(2,1)S(1)}, bf16[2,4,2,24,640]{4,3,2,1,0:T(8,128)(2,1)S(1)}, u32[]{:S(2)}, u32[]{:S(2)}) collective-permute-start(bf16[2,4,2,24,640]{4,3,2,1,0:T(8,128)(2,1)S(1)} %shard_map.94.own), channel_id=1, source_target_pairs={{0,1},{1,0},{2,3},{3,2},{4,5},{5,4},{6,7},{7,6},{8,9},{9,8},{10,11... | collective-permute-start | bytes 1474568 | tf_op jit(solution)/shard_map/ppermute | solution.py:401
  42.6 28.0 %collective-permute-start.9 = (bf16[2,320,640]{2,1,0:T(8,128)(2,1)S(1)}, bf16[2,320,640]{2,1,0:T(8,128)(2,1)S(1)}, u32[]{:S(2)}, u32[]{:S(2)}) collective-permute-start(bf16[2,320,640]{2,1,0:T(8,128)(2,1)S(1)} %get-tuple-element.59), channel_id=1, source_target_pairs={{0,4},{4,0},{8,12},{12,8},{16,20},{20,16},{24,28},{28,24},{1,5},{5... | collective-permute-start | bytes 2457608 | tf_op jit(solution)/shard_map/ppermute | solution.py:395
  48.1 20.8 %collective-permute-start.7 = (bf16[2304,128]{1,0:T(8,128)(2,1)S(1)}, bf16[2304,128]{1,0:T(8,128)(2,1)S(1)}, u32[]{:S(2)}, u32[]{:S(2)}) collective-permute-start(bf16[2304,128]{1,0:T(8,128)(2,1)S(1)} %get-tuple-element.52), channel_id=1, source_target_pairs={{0,8},{4,12},{8,0},{12,4},{16,24},{20,28},{24,16},{28,20},{1,9},{5... | collective-permute-start | bytes 1769480 | tf_op jit(solution)/shard_map/ppermute | solution.py:398
  49.9 20.6 %collective-permute-start.8 = (bf16[8,24,640]{2,1,0:T(8,128)(2,1)S(1)}, bf16[8,24,640]{2,1,0:T(8,128)(2,1)S(1)}, u32[]{:S(2)}, u32[]{:S(2)}) collective-permute-start(bf16[8,24,640]{2,1,0:T(8,128)(2,1)S(1)} %get-tuple-element.56), channel_id=1, source_target_pairs={{0,16},{4,20},{8,24},{12,28},{16,0},{20,4},{24,8},{28,12},{1,17},{... | collective-permute-start | bytes 737288 | tf_op jit(solution)/shard_map/ppermute | solution.py:398
  69.0 19.8 %collective-permute-start.12 = (bf16[1536,128]{1,0:T(8,128)(2,1)S(1)}, bf16[1536,128]{1,0:T(8,128)(2,1)S(1)}, u32[]{:S(2)}, u32[]{:S(2)}) collective-permute-start(bf16[1536,128]{1,0:T(8,128)(2,1)S(1)} %get-tuple-element.66), channel_id=1, source_target_pairs={{0,16},{4,20},{8,24},{12,28},{16,0},{20,4},{24,8},{28,12},{1,17},{... | collective-permute-start | bytes 1179656 | tf_op jit(solution)/shard_map/ppermute | solution.py:398
  70.5 18.3 %copy-start.7 = (f32[640]{0:T(1024)S(1)}, f32[640]{0:T(1024)}, u32[]{:S(2)}) copy-start(f32[640]{0:T(1024)} %param.14) | copy-start | bytes 7684
  72.5 29.3 %copy-start.8 = (f32[640]{0:T(1024)S(1)}, f32[640]{0:T(1024)}, u32[]{:S(2)}) copy-start(f32[640]{0:T(1024)} %param.13) | copy-start | bytes 7684
  72.5 11.3 %collective-permute-start.10 = (bf16[960,128]{1,0:T(8,128)(2,1)S(1)}, bf16[960,128]{1,0:T(8,128)(2,1)S(1)}, u32[]{:S(2)}, u32[]{:S(2)}) collective-permute-start(bf16[960,128]{1,0:T(8,128)(2,1)S(1)} %get-tuple-element.62), channel_id=1, source_target_pairs={{0,8},{4,12},{8,0},{12,4},{16,24},{20,28},{24,16},{28,20},{1,9},{5... | collective-permute-start | bytes 737288 | tf_op jit(solution)/shard_map/ppermute | solution.py:398
  89.6 12.1 %collective-permute-start.13 = (bf16[1536,128]{1,0:T(8,128)(2,1)S(1)}, bf16[1536,128]{1,0:T(8,128)(2,1)S(1)}, u32[]{:S(2)}, u32[]{:S(2)}) collective-permute-start(bf16[1536,128]{1,0:T(8,128)(2,1)S(1)} %shard_map.102.own), channel_id=1, source_target_pairs={{0,4},{4,0},{8,12},{12,8},{16,20},{20,16},{24,28},{28,24},{1,5},{5... | collective-permute-start | bytes 1179656 | tf_op jit(solution)/shard_map/ppermute | solution.py:395
  90.9 18.1 %collective-permute-start.18 = (bf16[12,24,640]{2,1,0:T(8,128)(2,1)S(1)}, bf16[12,24,640]{2,1,0:T(8,128)(2,1)S(1)}, u32[]{:S(2)}, u32[]{:S(2)}) collective-permute-start(bf16[12,24,640]{2,1,0:T(8,128)(2,1)S(1)} %shard_map.104), channel_id=1, source_target_pairs={{0,8},{4,12},{8,0},{12,4},{16,24},{20,28},{24,16},{28,20},{1,9},{5... | collective-permute-start | bytes 1105928 | tf_op jit(solution)/shard_map/ppermute | solution.py:398
  90.9 9.9 %collective-permute-start.11 = (bf16[480,128]{1,0:T(8,128)(2,1)S(1)}, bf16[480,128]{1,0:T(8,128)(2,1)S(1)}, u32[]{:S(2)}, u32[]{:S(2)}) collective-permute-start(bf16[480,128]{1,0:T(8,128)(2,1)S(1)} %get-tuple-element.65), channel_id=1, source_target_pairs={{0,16},{4,20},{8,24},{12,28},{16,0},{20,4},{24,8},{28,12},{1,17},{... | collective-permute-start | bytes 368648 | tf_op jit(solution)/shard_map/ppermute | solution.py:398
  93.9 24.2 %collective-permute-start.17 = (bf16[2,320,640]{2,1,0:T(8,128)(2,1)}, bf16[2,320,640]{2,1,0:T(8,128)(2,1)S(1)}, u32[]{:S(2)}, u32[]{:S(2)}) collective-permute-start(bf16[2,320,640]{2,1,0:T(8,128)(2,1)} %bitcast.8), channel_id=1, source_target_pairs={{0,4},{4,0},{8,12},{12,8},{16,20},{20,16},{24,28},{28,24},{1,5},{5... | collective-permute-start | bytes 2457608 | tf_op jit(solution)/shard_map/ppermute | solution.py:395
  103.2 7.1 %collective-permute-start.14 = (bf16[480,128]{1,0:T(8,128)(2,1)S(1)}, bf16[480,128]{1,0:T(8,128)(2,1)S(1)}, u32[]{:S(2)}, u32[]{:S(2)}) collective-permute-start(bf16[480,128]{1,0:T(8,128)(2,1)S(1)} %shard_map.103), channel_id=1, source_target_pairs={{0,8},{4,12},{8,0},{12,4},{16,24},{20,28},{24,16},{28,20},{1,9},{5... | collective-permute-start | bytes 368648 | tf_op jit(solution)/shard_map/ppermute | solution.py:398
  106.5 11.2 %collective-permute-start.15 = (bf16[480,128]{1,0:T(8,128)(2,1)S(1)}, bf16[480,128]{1,0:T(8,128)(2,1)S(1)}, u32[]{:S(2)}, u32[]{:S(2)}) collective-permute-start(bf16[480,128]{1,0:T(8,128)(2,1)S(1)} %shard_map.103), channel_id=1, source_target_pairs={{0,16},{4,20},{8,24},{12,28},{16,0},{20,4},{24,8},{28,12},{1,17},{... | collective-permute-start | bytes 368648 | tf_op jit(solution)/shard_map/ppermute | solution.py:398
  106.5 11.3 %collective-permute-start.16 = (bf16[480,128]{1,0:T(8,128)(2,1)S(1)}, bf16[480,128]{1,0:T(8,128)(2,1)S(1)}, u32[]{:S(2)}, u32[]{:S(2)}) collective-permute-start(bf16[480,128]{1,0:T(8,128)(2,1)S(1)} %shard_map.103), channel_id=1, source_target_pairs={{0,24},{4,28},{8,16},{12,20},{16,8},{20,12},{24,0},{28,4},{1,25},{... | collective-permute-start | bytes 368648 | tf_op jit(solution)/shard_map/ppermute | solution.py:398
  121.4 1.9 %collective-permute-start.19 = (bf16[2,4,2,24,640]{4,3,2,1,0:T(8,128)(2,1)S(1)}, bf16[2,4,2,24,640]{4,3,2,1,0:T(8,128)(2,1)S(1)}, u32[]{:S(2)}, u32[]{:S(2)}) collective-permute-start(bf16[2,4,2,24,640]{4,3,2,1,0:T(8,128)(2,1)S(1)} %get-tuple-element.83), channel_id=1, source_target_pairs={{0,1},{1,0},{2,3},{3,2},{4,5},{5,4},{6,7},{7,6},{8,9},{9,8},{10,11... | collective-permute-start | bytes 1474568 | tf_op jit(solution)/shard_map/ppermute | solution.py:401
  123.5 5.4 %collective-permute-start.20 = (bf16[4,24,640]{2,1,0:T(8,128)(2,1)S(1)}, bf16[4,24,640]{2,1,0:T(8,128)(2,1)S(1)}, u32[]{:S(2)}, u32[]{:S(2)}) collective-permute-start(bf16[4,24,640]{2,1,0:T(8,128)(2,1)S(1)} %get-tuple-element.76), channel_id=1, source_target_pairs={{0,2},{1,3},{2,0},{3,1},{4,6},{5,7},{6,4},{7,5},{8,10},{9,11},{10,... | collective-permute-start | bytes 368648 | tf_op jit(solution)/shard_map/ppermute | solution.py:401
  128.9 4.5 %collective-permute-start.21 = (bf16[24,640]{1,0:T(8,128)(2,1)S(1)}, bf16[24,640]{1,0:T(8,128)(2,1)S(1)}, u32[]{:S(2)}, u32[]{:S(2)}) collective-permute-start(bf16[24,640]{1,0:T(8,128)(2,1)S(1)} %get-tuple-element.78), channel_id=1, source_target_pairs={{0,8},{4,12},{8,0},{12,4},{16,24},{20,28},{24,16},{28,20},{1,9},{5... | collective-permute-start | bytes 92168 | tf_op jit(solution)/shard_map/ppermute | solution.py:398
  131.0 5.0 %collective-permute-start.22 = (bf16[24,640]{1,0:T(8,128)(2,1)S(1)}, bf16[24,640]{1,0:T(8,128)(2,1)S(1)}, u32[]{:S(2)}, u32[]{:S(2)}) collective-permute-start(bf16[24,640]{1,0:T(8,128)(2,1)S(1)} %get-tuple-element.79), channel_id=1, source_target_pairs={{0,16},{4,20},{8,24},{12,28},{16,0},{20,4},{24,8},{28,12},{1,17},{... | collective-permute-start | bytes 92168 | tf_op jit(solution)/shard_map/ppermute | solution.py:398
  132.1 5.7 %collective-permute-start.23 = (bf16[24,640]{1,0:T(8,128)(2,1)S(1)}, bf16[24,640]{1,0:T(8,128)(2,1)S(1)}, u32[]{:S(2)}, u32[]{:S(2)}) collective-permute-start(bf16[24,640]{1,0:T(8,128)(2,1)S(1)} %get-tuple-element.80), channel_id=1, source_target_pairs={{0,24},{4,28},{8,16},{12,20},{16,8},{20,12},{24,0},{28,4},{1,25},{... | collective-permute-start | bytes 92168 | tf_op jit(solution)/shard_map/ppermute | solution.py:398

commit v5 on v2

--- a/solution.py
+++ b/solution.py
@@ -421,20 +421,6 @@
         [shape(count, own_rows, 2 * slab) for count in counts],
         [VMEM] * depth, [SMEM] + [VMEM] * 3,
     )(place, after(tokens, early), in_bits, sign_bits)
-    got = [blocks[0]] + [swap_z(blocks[k], k) for k in steps if k]
-
-    def pair(first, second):
-        return call(pair_kernel, shape(2, *first.shape), VMEM, [VMEM] * 2)(first, second)
-
-    held_shape = (depth, 2, own_rows, 2 * slab)
-    held = call(stack_kernel, shape(*held_shape), VMEM, [VMEM] * depth)(*got)
-    forward = call(forward_kernel, shape(3 * team, own_rows, columns), VMEM, [VMEM])(got[2])
-    signs = (blocks[2], got[1], got[2], swap_z(after(forward, held), 1))
-    held = pair(held, swap_u(held, 2))
-    rows = call(rows_kernel, shape(2, half, 2 * slab), VMEM, [VMEM] * 2)(
-        held, swap_u(after(held, signs[3]), 1)
-    )
-
     query_weights, late_own, late_near, late_far = call(
         functools.partial(late_signs_kernel, team),
         [shape(2, slab, columns)]
@@ -443,6 +429,21 @@
         [SMEM] + [VMEM] * 2 + [ANY],
         [pltpu.SemaphoreType.DMA((2,))],
     )(place, after(out_bits, blocks[0]), mix_bits, qkv_weights)
+    blocks = [*blocks[:3], after(blocks[3], query_weights)]
+    got = [blocks[0]] + [swap_z(blocks[k], k) for k in steps if k]
+
+    def pair(first, second):
+        return call(pair_kernel, shape(2, *first.shape), VMEM, [VMEM] * 2)(first, second)
+
+    held_shape = (depth, 2, own_rows, 2 * slab)
+    held = call(stack_kernel, shape(*held_shape), VMEM, [VMEM] * depth)(*got)
+    forward = call(forward_kernel, shape(3 * team, own_rows, columns), VMEM, [VMEM])(got[2])
+    signs = (blocks[2], got[1], got[2], swap_z(after(forward, held), 1))
+    held = pair(held, swap_u(held, 2))
+    rows = call(rows_kernel, shape(2, half, 2 * slab), VMEM, [VMEM] * 2)(
+        held, swap_u(after(held, signs[3]), 1)
+    )
+
     late_far = swap_z(after(late_far, held), 2)
     partner_query = swap_x(after(query_weights, partner_early, forward))
     out_t = jnp.transpose(out_weights, (0, 2, 1))

time: 137 us -> 138 us (level)
  local copies, waits for them, and re-layouts: 3.89 us -> 6.69 us
    unnamed x21 -> x23, local copies, waits for them, and re-layouts: 3.77 us -> 6.56 us
    ppermute x16, waiting for transfers between devices: 54.7 us -> 52.9 us  [swap_z(): lax.ppermute(value, 'blk', [(i, i ^ 2 * step) for i in range(groups)])]
    ppermute x4, starting transfers between devices: 6.33 us -> 4.77 us  [swap_x(): return lax.ppermute(value, 'blk', [(i, i ^ 1) for i in range(groups)])]
  transfers between devices with their start and end apart: 24 -> 24, of which waited for: 15 -> 16; matrix products, arithmetic and copies ran while one was open for 1% -> 2% of each run, Pallas kernels for 9% -> 8%
where the time goes in v5:
time: 138 us
  waiting for transfers between devices  76.3 us (55%)
  starting transfers between devices  36.6 us (27%)
  Pallas kernels  14.3 us (10%)
  local copies, waits for them, and re-layouts  6.69 us (5%)
  other arithmetic  2.37 us (2%)
    ppermute x16, waiting for transfers between devices, swap_z(): lax.ppermute(value, 'blk', [(i, i ^ 2 * step) for i in range(groups)])  52.9 us
    ppermute x16, starting transfers between devices, swap_z(): lax.ppermute(value, 'blk', [(i, i ^ 2 * step) for i in range(groups)])  28.6 us
    ppermute x4, waiting for transfers between devices, swap_u(): return lax.ppermute(value, 'uly', [(i, i ^ bit) for i in range(team)])  13.1 us
    ppermute x4, waiting for transfers between devices, swap_x(): return lax.ppermute(value, 'blk', [(i, i ^ 1) for i in range(groups)])  10.4 us
    pallas_call x2, Pallas kernels, project(): call(functools.partial(project_kernel, parts, size), [shape(counts[0], HE...  6.76 us
    unnamed x23, local copies, waits for them, and re-layouts  6.56 us
    ppermute x4, starting transfers between devices, swap_x(): return lax.ppermute(value, 'blk', [(i, i ^ 1) for i in range(groups)])  4.77 us
    ppermute x4, starting transfers between devices, swap_u(): return lax.ppermute(value, 'uly', [(i, i ^ bit) for i in range(team)])  3.18 us
  transfers between devices with their start and end apart: 24, of which 16 were waited for; matrix products, arithmetic and copies ran while one was open for 2% of the time, Pallas kernels for 8%

profile of v5, /device:TPU:0, one launch (start us, length us, event | category | flops | bytes accessed | tf_op | source)
XLA Modules:
  0.0 137.9 jit_solution(8413072688181572719)
XLA Ops:
  0.0 1.7 %copy-done = bf16[2,3,320,640]{3,2,1,0:T(8,128)(2,1)S(1)} copy-done((bf16[2,3,320,640]{3,2,1,0:T(8,128)(2,1)S(1)}, bf16[2,3,320,640]{3,2,1,0:T(8,128)(2,1)}, u32[]{:S(2)}) %copy-start) | copy-done | bytes 2457624
  1.7 1.2 shard_map.91
  2.9 3.0 %collective-permute-start.6 = (bf16[2,2,320,640]{3,2,1,0:T(8,128)(2,1)}, bf16[2,2,320,640]{3,2,1,0:T(8,128)(2,1)}, u32[]{:S(2)}, u32[]{:S(2)}) collective-permute-start(bf16[2,2,320,640]{3,2,1,0:T(8,128)(2,1)} %shard_map.91), channel_id=1, source_target_pairs={{0,4},{4,0},{8,12},{12,8},{16,20},{20,16},{24,28},{28,24},{1,5},{5... | collective-permute-start | bytes 4915208 | tf_op jit(solution)/shard_map/ppermute | solution.py:400
  6.0 1.1 copy-done.3
  7.1 0.9 copy-done.6
  8.1 0.9 copy-done.8
  9.0 0.7 shard_map.92
  9.6 2.7 %collective-permute-start.1 = (bf16[14,24,640]{2,1,0:T(8,128)(2,1)S(1)}, bf16[14,24,640]{2,1,0:T(8,128)(2,1)S(1)}, u32[]{:S(2)}, u32[]{:S(2)}) collective-permute-start(bf16[14,24,640]{2,1,0:T(8,128)(2,1)S(1)} %get-tuple-element.48.signs_0), channel_id=1, source_target_pairs={{0,16},{4,20},{8,24},{12,28},{16,0},{20,4},{24,8},{28,12},{1,17},{... | collective-permute-start | bytes 1290248 | tf_op jit(solution)/shard_map/ppermute | solution.py:403
  12.3 1.6 %collective-permute-start = (bf16[14,24,640]{2,1,0:T(8,128)(2,1)S(1)}, bf16[14,24,640]{2,1,0:T(8,128)(2,1)S(1)}, u32[]{:S(2)}, u32[]{:S(2)}) collective-permute-start(bf16[14,24,640]{2,1,0:T(8,128)(2,1)S(1)} %get-tuple-element.47), channel_id=1, source_target_pairs={{0,8},{4,12},{8,0},{12,4},{16,24},{20,28},{24,16},{28,20},{1,9},{5... | collective-permute-start | bytes 1290248 | tf_op jit(solution)/shard_map/ppermute | solution.py:403
  13.9 0.9 copy-done.7
  14.8 1.1 shard_map.93
  16.2 16.3 %collective-permute-done.1.refs_2_.taken.signs_2 = bf16[14,24,640]{2,1,0:T(8,128)(2,1)S(1)} collective-permute-done((bf16[14,24,640]{2,1,0:T(8,128)(2,1)S(1)}, bf16[14,24,640]{2,1,0:T(8,128)(2,1)S(1)}, u32[]{:S(2)}, u32[]{:S(2)}) %collective-permute-start.1) | collective-permute-done | bytes 430112 | tf_op jit(solution)/shard_map/ppermute | solution.py:403
  32.6 1.1 collective-permute-done.2.refs_3_
  33.7 0.9 collective-permute-start.4
  34.6 1.5 %collective-permute-start.3 = (bf16[4,2,24,640]{3,2,1,0:T(8,128)(2,1)S(1)}, bf16[4,2,24,640]{3,2,1,0:T(8,128)(2,1)S(1)}, u32[]{:S(2)}, u32[]{:S(2)}) collective-permute-start(bf16[4,2,24,640]{3,2,1,0:T(8,128)(2,1)S(1)} %shard_map.94.own), channel_id=1, source_target_pairs={{0,2},{1,3},{2,0},{3,1},{4,6},{5,7},{6,4},{7,5},{8,10},{9,11},{10,... | collective-permute-start | bytes 737288 | tf_op jit(solution)/shard_map/ppermute | solution.py:406
  36.1 6.1 %collective-permute-done.3.taken = bf16[4,2,24,640]{3,2,1,0:T(8,128)(2,1)S(1)} collective-permute-done((bf16[4,2,24,640]{3,2,1,0:T(8,128)(2,1)S(1)}, bf16[4,2,24,640]{3,2,1,0:T(8,128)(2,1)S(1)}, u32[]{:S(2)}, u32[]{:S(2)}) %collective-permute-start.3) | collective-permute-done | bytes 245792 | tf_op jit(solution)/shard_map/ppermute | solution.py:406
  42.2 1.1 collective-permute-done.4.signs_3
  43.9 1.3 collective-permute-done.5.taken
  45.3 4.3 %shard_map.98 = (bf16[2304,128]{1,0:T(8,128)(2,1)S(1)}, f32[1536,128]{1,0:T(8,128)S(1)}, f32[768,128]{1,0:T(8,128)S(1)}) custom-call(s32[3]{0:T(128)S(1)} %pad_add_fusion.place, bf16[2,384,640]{2,1,0:T(8,128)(2,1)S(1)} %shard_map.97.rows, bf16[2,3,320,640]{3,2,1,0:T(8,128)(2,1)S(1)} %copy-done.1, bf16[2,2,320,640]{3,2,1,0:T(8,128)(2,1)} %collective-permute-done.6.partner, ...), custom_call_target="tpu_custom_call" | custom-call | tf_op jit(solution)/shard_map/pallas_call | solution.py:458
  49.6 1.8 %collective-permute-start.9 = (bf16[2304,128]{1,0:T(8,128)(2,1)S(1)}, bf16[2304,128]{1,0:T(8,128)(2,1)S(1)}, u32[]{:S(2)}, u32[]{:S(2)}) collective-permute-start(bf16[2304,128]{1,0:T(8,128)(2,1)S(1)} %get-tuple-element.55), channel_id=1, source_target_pairs={{0,8},{4,12},{8,0},{12,4},{16,24},{20,28},{24,16},{28,20},{1,9},{5... | collective-permute-start | bytes 1769480 | tf_op jit(solution)/shard_map/ppermute | solution.py:403
  51.4 2.3 %collective-permute-start.10 = (bf16[8,24,640]{2,1,0:T(8,128)(2,1)S(1)}, bf16[8,24,640]{2,1,0:T(8,128)(2,1)S(1)}, u32[]{:S(2)}, u32[]{:S(2)}) collective-permute-start(bf16[8,24,640]{2,1,0:T(8,128)(2,1)S(1)} %get-tuple-element.64), channel_id=1, source_target_pairs={{0,16},{4,20},{8,24},{12,28},{16,0},{20,4},{24,8},{28,12},{1,17},{... | collective-permute-start | bytes 737288 | tf_op jit(solution)/shard_map/ppermute | solution.py:403
  53.7 10.3 %collective-permute-done.7 = bf16[2,320,640]{2,1,0:T(8,128)(2,1)S(1)} collective-permute-done((bf16[2,320,640]{2,1,0:T(8,128)(2,1)S(1)}, bf16[2,320,640]{2,1,0:T(8,128)(2,1)S(1)}, u32[]{:S(2)}, u32[]{:S(2)}) %collective-permute-start.7) | collective-permute-done | bytes 819232 | tf_op jit(solution)/shard_map/ppermute | solution.py:400
  64.0 2.5 %shard_map.99 = (bf16[960,128]{1,0:T(8,128)(2,1)S(1)}, f32[480,128]{1,0:T(8,128)S(1)}, f32[480,128]{1,0:T(8,128)S(1)}) custom-call(s32[3]{0:T(128)S(1)} %pad_add_fusion.place, bf16[2,384,640]{2,1,0:T(8,128)(2,1)S(1)} %shard_map.97.rows, bf16[2,3,320,640]{3,2,1,0:T(8,128)(2,1)S(1)} %copy-done.1, bf16[2,1,320,640]{3,2,1,0:T(8,128)(2,1)S(1)} %bitcast.32, ...), custom_call_target="tpu_custom_call" | custom-call | tf_op jit(solution)/shard_map/pallas_call | solution.py:458
  66.6 3.0 %collective-permute-done.10.far = bf16[8,24,640]{2,1,0:T(8,128)(2,1)S(1)} collective-permute-done((bf16[8,24,640]{2,1,0:T(8,128)(2,1)S(1)}, bf16[8,24,640]{2,1,0:T(8,128)(2,1)S(1)}, u32[]{:S(2)}, u32[]{:S(2)}) %collective-permute-start.10) | collective-permute-done | bytes 245792 | tf_op jit(solution)/shard_map/ppermute | solution.py:403
  69.5 0.7 collective-permute-done.9.taken
  70.4 2.7 %collective-permute-start.12 = (bf16[1536,128]{1,0:T(8,128)(2,1)S(1)}, bf16[1536,128]{1,0:T(8,128)(2,1)S(1)}, u32[]{:S(2)}, u32[]{:S(2)}) collective-permute-start(bf16[1536,128]{1,0:T(8,128)(2,1)S(1)} %get-tuple-element.70), channel_id=1, source_target_pairs={{0,16},{4,20},{8,24},{12,28},{16,0},{20,4},{24,8},{28,12},{1,17},{... | collective-permute-start | bytes 1179656 | tf_op jit(solution)/shard_map/ppermute | solution.py:403
  73.1 1.4 %collective-permute-start.8 = (bf16[960,128]{1,0:T(8,128)(2,1)S(1)}, bf16[960,128]{1,0:T(8,128)(2,1)S(1)}, u32[]{:S(2)}, u32[]{:S(2)}) collective-permute-start(bf16[960,128]{1,0:T(8,128)(2,1)S(1)} %get-tuple-element.60), channel_id=1, source_target_pairs={{0,8},{4,12},{8,0},{12,4},{16,24},{20,28},{24,16},{28,20},{1,9},{5... | collective-permute-start | bytes 737288 | tf_op jit(solution)/shard_map/ppermute | solution.py:403
  75.1 11.2 %collective-permute-done.8.taken = bf16[960,128]{1,0:T(8,128)(2,1)S(1)} collective-permute-done((bf16[960,128]{1,0:T(8,128)(2,1)S(1)}, bf16[960,128]{1,0:T(8,128)(2,1)S(1)}, u32[]{:S(2)}, u32[]{:S(2)}) %collective-permute-start.8) | collective-permute-done | bytes 245792 | tf_op jit(solution)/shard_map/ppermute | solution.py:403
  86.3 4.0 %collective-permute-done.12.taken = bf16[1536,128]{1,0:T(8,128)(2,1)S(1)} collective-permute-done((bf16[1536,128]{1,0:T(8,128)(2,1)S(1)}, bf16[1536,128]{1,0:T(8,128)(2,1)S(1)}, u32[]{:S(2)}, u32[]{:S(2)}) %collective-permute-start.12) | collective-permute-done | bytes 393248 | tf_op jit(solution)/shard_map/ppermute | solution.py:403
  90.3 0.8 shard_map.102.own
  92.3 3.4 %collective-permute-start.11 = (bf16[480,128]{1,0:T(8,128)(2,1)S(1)}, bf16[480,128]{1,0:T(8,128)(2,1)S(1)}, u32[]{:S(2)}, u32[]{:S(2)}) collective-permute-start(bf16[480,128]{1,0:T(8,128)(2,1)S(1)} %get-tuple-element.69), channel_id=1, source_target_pairs={{0,16},{4,20},{8,24},{12,28},{16,0},{20,4},{24,8},{28,12},{1,17},{... | collective-permute-start | bytes 368648 | tf_op jit(solution)/shard_map/ppermute | solution.py:403
  95.7 7.0 %collective-permute-done.11.taken = bf16[480,128]{1,0:T(8,128)(2,1)S(1)} collective-permute-done((bf16[480,128]{1,0:T(8,128)(2,1)S(1)}, bf16[480,128]{1,0:T(8,128)(2,1)S(1)}, u32[]{:S(2)}, u32[]{:S(2)}) %collective-permute-start.11) | collective-permute-done | bytes 122912 | tf_op jit(solution)/shard_map/ppermute | solution.py:403
  102.6 1.4 %shard_map.103 = bf16[480,128]{1,0:T(8,128)(2,1)S(1)} custom-call(s32[3]{0:T(128)S(1)} %pad_add_fusion.place, f32[480,128]{1,0:T(8,128)S(1)} %get-tuple-element.68.total, bf16[480,128]{1,0:T(8,128)(2,1)S(1)} %collective-permute-done.11.taken, f32[5,128]{1,0:T(8,128)S(1)} %bitcast.35, bf16[1536,128]{1,0:T(8,128)(2,1)S(1)} %shard_map.102.own, ...), custom_call_target="tpu_custom_call" | custom-call | tf_op jit(solution)/shard_map/pallas_call | solution.py:500
  104.0 4.2 %collective-permute-start.14 = (bf16[480,128]{1,0:T(8,128)(2,1)S(1)}, bf16[480,128]{1,0:T(8,128)(2,1)S(1)}, u32[]{:S(2)}, u32[]{:S(2)}) collective-permute-start(bf16[480,128]{1,0:T(8,128)(2,1)S(1)} %shard_map.103), channel_id=1, source_target_pairs={{0,8},{4,12},{8,0},{12,4},{16,24},{20,28},{24,16},{28,20},{1,9},{5... | collective-permute-start | bytes 368648 | tf_op jit(solution)/shard_map/ppermute | solution.py:403
  108.2 2.4 %collective-permute-start.16 = (bf16[480,128]{1,0:T(8,128)(2,1)S(1)}, bf16[480,128]{1,0:T(8,128)(2,1)S(1)}, u32[]{:S(2)}, u32[]{:S(2)}) collective-permute-start(bf16[480,128]{1,0:T(8,128)(2,1)S(1)} %shard_map.103), channel_id=1, source_target_pairs={{0,24},{4,28},{8,16},{12,20},{16,8},{20,12},{24,0},{28,4},{1,25},{... | collective-permute-start | bytes 368648 | tf_op jit(solution)/shard_map/ppermute | solution.py:403
  110.7 0.9 copy-done.5
  112.3 1.5 %broadcast_select_fusion = (bf16[2,320,640]{2,1,0:T(8,128)(2,1)S(1)}, bf16[2,320,640]{2,1,0:T(8,128)(2,1)S(1)}) fusion(bf16[2,320,640]{2,1,0:T(8,128)(2,1)} %collective-permute-done.17, pred[]{:T(512)S(6)} %eq.6, bf16[2,640,320]{1,2,0:T(8,128)(2,1)} %param.15), kind=kLoop, calls=%fused_computation.15 | loop fusion | flops 819200 | bytes 3276801 | tf_op jit(solution)/shard_map/jit(_where)/select_n | solution.py:526
  114.3 5.1 %collective-permute-done.15 = bf16[480,128]{1,0:T(8,128)(2,1)S(1)} collective-permute-done((bf16[480,128]{1,0:T(8,128)(2,1)S(1)}, bf16[480,128]{1,0:T(8,128)(2,1)S(1)}, u32[]{:S(2)}, u32[]{:S(2)}) %collective-permute-start.15) | collective-permute-done | bytes 122912 | tf_op jit(solution)/shard_map/ppermute | solution.py:403
  119.7 0.7 fusion.1
  120.4 0.7 fusion
  121.4 1.9 %collective-permute-done.19.taken = bf16[2,4,2,24,640]{4,3,2,1,0:T(8,128)(2,1)S(1)} collective-permute-done((bf16[2,4,2,24,640]{4,3,2,1,0:T(8,128)(2,1)S(1)}, bf16[2,4,2,24,640]{4,3,2,1,0:T(8,128)(2,1)S(1)}, u32[]{:S(2)}, u32[]{:S(2)}) %collective-permute-start.19) | collective-permute-done | bytes 491552 | tf_op jit(solution)/shard_map/ppermute | solution.py:406
  123.4 1.6 %collective-permute-start.20 = (bf16[4,24,640]{2,1,0:T(8,128)(2,1)S(1)}, bf16[4,24,640]{2,1,0:T(8,128)(2,1)S(1)}, u32[]{:S(2)}, u32[]{:S(2)}) collective-permute-start(bf16[4,24,640]{2,1,0:T(8,128)(2,1)S(1)} %get-tuple-element.80), channel_id=1, source_target_pairs={{0,2},{1,3},{2,0},{3,1},{4,6},{5,7},{6,4},{7,5},{8,10},{9,11},{10,... | collective-permute-start | bytes 368648 | tf_op jit(solution)/shard_map/ppermute | solution.py:406
  125.0 3.8 %collective-permute-done.20.taken = bf16[4,24,640]{2,1,0:T(8,128)(2,1)S(1)} collective-permute-done((bf16[4,24,640]{2,1,0:T(8,128)(2,1)S(1)}, bf16[4,24,640]{2,1,0:T(8,128)(2,1)S(1)}, u32[]{:S(2)}, u32[]{:S(2)}) %collective-permute-start.20) | collective-permute-done | bytes 122912 | tf_op jit(solution)/shard_map/ppermute | solution.py:406
  128.9 2.0 %collective-permute-start.21 = (bf16[24,640]{1,0:T(8,128)(2,1)S(1)}, bf16[24,640]{1,0:T(8,128)(2,1)S(1)}, u32[]{:S(2)}, u32[]{:S(2)}) collective-permute-start(bf16[24,640]{1,0:T(8,128)(2,1)S(1)} %get-tuple-element.82), channel_id=1, source_target_pairs={{0,8},{4,12},{8,0},{12,4},{16,24},{20,28},{24,16},{28,20},{1,9},{5... | collective-permute-start | bytes 92168 | tf_op jit(solution)/shard_map/ppermute | solution.py:403
  131.0 2.3 %collective-permute-start.23 = (bf16[24,640]{1,0:T(8,128)(2,1)S(1)}, bf16[24,640]{1,0:T(8,128)(2,1)S(1)}, u32[]{:S(2)}, u32[]{:S(2)}) collective-permute-start(bf16[24,640]{1,0:T(8,128)(2,1)S(1)} %get-tuple-element.84), channel_id=1, source_target_pairs={{0,24},{4,28},{8,16},{12,20},{16,8},{20,12},{24,0},{28,4},{1,25},{... | collective-permute-start | bytes 92168 | tf_op jit(solution)/shard_map/ppermute | solution.py:403
  133.4 2.3 %collective-permute-done.22.refs_2_ = bf16[24,640]{1,0:T(8,128)(2,1)S(1)} collective-permute-done((bf16[24,640]{1,0:T(8,128)(2,1)S(1)}, bf16[24,640]{1,0:T(8,128)(2,1)S(1)}, u32[]{:S(2)}, u32[]{:S(2)}) %collective-permute-start.22) | collective-permute-done | bytes 30752 | tf_op jit(solution)/shard_map/ppermute | solution.py:403
  135.7 1.0 collective-permute-done.23.refs_3_
  136.7 1.2 shard_map.108
  (62 shorter events, 5.0 us)
Async XLA Ops:
  0.0 1.7 %copy-start = (bf16[2,3,320,640]{3,2,1,0:T(8,128)(2,1)S(1)}, bf16[2,3,320,640]{3,2,1,0:T(8,128)(2,1)}, u32[]{:S(2)}) copy-start(bf16[2,3,320,640]{3,2,1,0:T(8,128)(2,1)} %weights.7) | copy-start | bytes 7372804
  1.7 12.2 %copy-start.1 = (bf16[2,3,320,640]{3,2,1,0:T(8,128)(2,1)S(1)}, bf16[2,3,320,640]{3,2,1,0:T(8,128)(2,1)}, u32[]{:S(2)}) copy-start(bf16[2,3,320,640]{3,2,1,0:T(8,128)(2,1)} %weights.7) | copy-start | bytes 7372804
  1.7 12.2 %copy-start.2 = (s32[96,2560]{1,0:T(8,128)S(1)}, s32[96,2560]{1,0:T(8,128)}, u32[]{:S(2)}) copy-start(s32[96,2560]{1,0:T(8,128)} %out_bits) | copy-start | bytes 2949124
  2.9 40.5 %collective-permute-start.6 = (bf16[2,2,320,640]{3,2,1,0:T(8,128)(2,1)}, bf16[2,2,320,640]{3,2,1,0:T(8,128)(2,1)}, u32[]{:S(2)}, u32[]{:S(2)}) collective-permute-start(bf16[2,2,320,640]{3,2,1,0:T(8,128)(2,1)} %shard_map.91), channel_id=1, source_target_pairs={{0,4},{4,0},{8,12},{12,8},{16,20},{20,16},{24,28},{28,24},{1,5},{5... | collective-permute-start | bytes 4915208 | tf_op jit(solution)/shard_map/ppermute | solution.py:400
  6.0 1.1 copy-start.3
  7.1 0.9 copy-start.6
  8.1 0.9 copy-start.8
  9.6 22.9 %collective-permute-start.1 = (bf16[14,24,640]{2,1,0:T(8,128)(2,1)S(1)}, bf16[14,24,640]{2,1,0:T(8,128)(2,1)S(1)}, u32[]{:S(2)}, u32[]{:S(2)}) collective-permute-start(bf16[14,24,640]{2,1,0:T(8,128)(2,1)S(1)} %get-tuple-element.48.signs_0), channel_id=1, source_target_pairs={{0,16},{4,20},{8,24},{12,28},{16,0},{20,4},{24,8},{28,12},{1,17},{... | collective-permute-start | bytes 1290248 | tf_op jit(solution)/shard_map/ppermute | solution.py:403
  12.3 21.4 %collective-permute-start = (bf16[14,24,640]{2,1,0:T(8,128)(2,1)S(1)}, bf16[14,24,640]{2,1,0:T(8,128)(2,1)S(1)}, u32[]{:S(2)}, u32[]{:S(2)}) collective-permute-start(bf16[14,24,640]{2,1,0:T(8,128)(2,1)S(1)} %get-tuple-element.47), channel_id=1, source_target_pairs={{0,8},{4,12},{8,0},{12,4},{16,24},{20,28},{24,16},{28,20},{1,9},{5... | collective-permute-start | bytes 1290248 | tf_op jit(solution)/shard_map/ppermute | solution.py:403
  13.9 0.9 copy-start.7
  15.9 75.8 %copy-start.4 = (bf16[6,24,640]{2,1,0:T(8,128)(2,1)}, bf16[6,24,640]{2,1,0:T(8,128)(2,1)S(1)}, u32[]{:S(2)}) copy-start(bf16[6,24,640]{2,1,0:T(8,128)(2,1)S(1)} %get-tuple-element.75.near) | copy-start | bytes 552964
  15.9 17.8 %collective-permute-start.2 = (bf16[2,24,640]{2,1,0:T(8,128)(2,1)S(1)}, bf16[2,24,640]{2,1,0:T(8,128)(2,1)S(1)}, u32[]{:S(2)}, u32[]{:S(2)}) collective-permute-start(bf16[2,24,640]{2,1,0:T(8,128)(2,1)S(1)} %get-tuple-element.52), channel_id=1, source_target_pairs={{0,24},{4,28},{8,16},{12,20},{16,8},{20,12},{24,0},{28,4},{1,25},{... | collective-permute-start | bytes 184328 | tf_op jit(solution)/shard_map/ppermute | solution.py:403
  33.7 9.7 %collective-permute-start.4 = (bf16[12,24,640]{2,1,0:T(8,128)(2,1)S(1)}, bf16[12,24,640]{2,1,0:T(8,128)(2,1)S(1)}, u32[]{:S(2)}, u32[]{:S(2)}) collective-permute-start(bf16[12,24,640]{2,1,0:T(8,128)(2,1)S(1)} %shard_map.96), channel_id=1, source_target_pairs={{0,8},{4,12},{8,0},{12,4},{16,24},{20,28},{24,16},{28,20},{1,9},{5... | collective-permute-start | bytes 1105928 | tf_op jit(solution)/shard_map/ppermute | solution.py:403
  34.6 7.6 %collective-permute-start.3 = (bf16[4,2,24,640]{3,2,1,0:T(8,128)(2,1)S(1)}, bf16[4,2,24,640]{3,2,1,0:T(8,128)(2,1)S(1)}, u32[]{:S(2)}, u32[]{:S(2)}) collective-permute-start(bf16[4,2,24,640]{3,2,1,0:T(8,128)(2,1)S(1)} %shard_map.94.own), channel_id=1, source_target_pairs={{0,2},{1,3},{2,0},{3,1},{4,6},{5,7},{6,4},{7,5},{8,10},{9,11},{10,... | collective-permute-start | bytes 737288 | tf_op jit(solution)/shard_map/ppermute | solution.py:406
  43.4 1.9 %collective-permute-start.5 = (bf16[2,4,2,24,640]{4,3,2,1,0:T(8,128)(2,1)S(1)}, bf16[2,4,2,24,640]{4,3,2,1,0:T(8,128)(2,1)S(1)}, u32[]{:S(2)}, u32[]{:S(2)}) collective-permute-start(bf16[2,4,2,24,640]{4,3,2,1,0:T(8,128)(2,1)S(1)} %shard_map.95.own), channel_id=1, source_target_pairs={{0,1},{1,0},{2,3},{3,2},{4,5},{5,4},{6,7},{7,6},{8,9},{9,8},{10,11... | collective-permute-start | bytes 1474568 | tf_op jit(solution)/shard_map/ppermute | solution.py:406
  43.4 20.7 %collective-permute-start.7 = (bf16[2,320,640]{2,1,0:T(8,128)(2,1)S(1)}, bf16[2,320,640]{2,1,0:T(8,128)(2,1)S(1)}, u32[]{:S(2)}, u32[]{:S(2)}) collective-permute-start(bf16[2,320,640]{2,1,0:T(8,128)(2,1)S(1)} %get-tuple-element.57), channel_id=1, source_target_pairs={{0,4},{4,0},{8,12},{12,8},{16,20},{20,16},{24,28},{28,24},{1,5},{5... | collective-permute-start | bytes 2457608 | tf_op jit(solution)/shard_map/ppermute | solution.py:400
  49.6 20.7 %collective-permute-start.9 = (bf16[2304,128]{1,0:T(8,128)(2,1)S(1)}, bf16[2304,128]{1,0:T(8,128)(2,1)S(1)}, u32[]{:S(2)}, u32[]{:S(2)}) collective-permute-start(bf16[2304,128]{1,0:T(8,128)(2,1)S(1)} %get-tuple-element.55), channel_id=1, source_target_pairs={{0,8},{4,12},{8,0},{12,4},{16,24},{20,28},{24,16},{28,20},{1,9},{5... | collective-permute-start | bytes 1769480 | tf_op jit(solution)/shard_map/ppermute | solution.py:403
  51.4 18.2 %collective-permute-start.10 = (bf16[8,24,640]{2,1,0:T(8,128)(2,1)S(1)}, bf16[8,24,640]{2,1,0:T(8,128)(2,1)S(1)}, u32[]{:S(2)}, u32[]{:S(2)}) collective-permute-start(bf16[8,24,640]{2,1,0:T(8,128)(2,1)S(1)} %get-tuple-element.64), channel_id=1, source_target_pairs={{0,16},{4,20},{8,24},{12,28},{16,0},{20,4},{24,8},{28,12},{1,17},{... | collective-permute-start | bytes 737288 | tf_op jit(solution)/shard_map/ppermute | solution.py:403
  66.5 23.8 %copy-start.9 = (f32[640]{0:T(1024)S(1)}, f32[640]{0:T(1024)}, u32[]{:S(2)}) copy-start(f32[640]{0:T(1024)} %param.14) | copy-start | bytes 7684
  70.4 32.2 %copy-start.10 = (f32[640]{0:T(1024)S(1)}, f32[640]{0:T(1024)}, u32[]{:S(2)}) copy-start(f32[640]{0:T(1024)} %param.13) | copy-start | bytes 7684
  70.4 20.0 %collective-permute-start.12 = (bf16[1536,128]{1,0:T(8,128)(2,1)S(1)}, bf16[1536,128]{1,0:T(8,128)(2,1)S(1)}, u32[]{:S(2)}, u32[]{:S(2)}) collective-permute-start(bf16[1536,128]{1,0:T(8,128)(2,1)S(1)} %get-tuple-element.70), channel_id=1, source_target_pairs={{0,16},{4,20},{8,24},{12,28},{16,0},{20,4},{24,8},{28,12},{1,17},{... | collective-permute-start | bytes 1179656 | tf_op jit(solution)/shard_map/ppermute | solution.py:403
  73.1 13.2 %collective-permute-start.8 = (bf16[960,128]{1,0:T(8,128)(2,1)S(1)}, bf16[960,128]{1,0:T(8,128)(2,1)S(1)}, u32[]{:S(2)}, u32[]{:S(2)}) collective-permute-start(bf16[960,128]{1,0:T(8,128)(2,1)S(1)} %get-tuple-element.60), channel_id=1, source_target_pairs={{0,8},{4,12},{8,0},{12,4},{16,24},{20,28},{24,16},{28,20},{1,9},{5... | collective-permute-start | bytes 737288 | tf_op jit(solution)/shard_map/ppermute | solution.py:403
  74.5 37.8 %collective-permute-start.17 = (bf16[2,320,640]{2,1,0:T(8,128)(2,1)}, bf16[2,320,640]{2,1,0:T(8,128)(2,1)}, u32[]{:S(2)}, u32[]{:S(2)}) collective-permute-start(bf16[2,320,640]{2,1,0:T(8,128)(2,1)} %bitcast.8), channel_id=1, source_target_pairs={{0,4},{4,0},{8,12},{12,8},{16,20},{20,16},{24,28},{28,24},{1,5},{5... | collective-permute-start | bytes 2457608 | tf_op jit(solution)/shard_map/ppermute | solution.py:400
  91.1 11.5 %collective-permute-start.13 = (bf16[1536,128]{1,0:T(8,128)(2,1)S(1)}, bf16[1536,128]{1,0:T(8,128)(2,1)S(1)}, u32[]{:S(2)}, u32[]{:S(2)}) collective-permute-start(bf16[1536,128]{1,0:T(8,128)(2,1)S(1)} %shard_map.102.own), channel_id=1, source_target_pairs={{0,4},{4,0},{8,12},{12,8},{16,20},{20,16},{24,28},{28,24},{1,5},{5... | collective-permute-start | bytes 1179656 | tf_op jit(solution)/shard_map/ppermute | solution.py:400
  91.8 18.9 %collective-permute-start.18 = (bf16[12,24,640]{2,1,0:T(8,128)(2,1)S(1)}, bf16[12,24,640]{2,1,0:T(8,128)(2,1)S(1)}, u32[]{:S(2)}, u32[]{:S(2)}) collective-permute-start(bf16[12,24,640]{2,1,0:T(8,128)(2,1)S(1)} %shard_map.104), channel_id=1, source_target_pairs={{0,8},{4,12},{8,0},{12,4},{16,24},{20,28},{24,16},{28,20},{1,9},{5... | collective-permute-start | bytes 1105928 | tf_op jit(solution)/shard_map/ppermute | solution.py:403
  92.3 10.3 %collective-permute-start.11 = (bf16[480,128]{1,0:T(8,128)(2,1)S(1)}, bf16[480,128]{1,0:T(8,128)(2,1)S(1)}, u32[]{:S(2)}, u32[]{:S(2)}) collective-permute-start(bf16[480,128]{1,0:T(8,128)(2,1)S(1)} %get-tuple-element.69), channel_id=1, source_target_pairs={{0,16},{4,20},{8,24},{12,28},{16,0},{20,4},{24,8},{28,12},{1,17},{... | collective-permute-start | bytes 368648 | tf_op jit(solution)/shard_map/ppermute | solution.py:403
  104.0 10.2 %collective-permute-start.14 = (bf16[480,128]{1,0:T(8,128)(2,1)S(1)}, bf16[480,128]{1,0:T(8,128)(2,1)S(1)}, u32[]{:S(2)}, u32[]{:S(2)}) collective-permute-start(bf16[480,128]{1,0:T(8,128)(2,1)S(1)} %shard_map.103), channel_id=1, source_target_pairs={{0,8},{4,12},{8,0},{12,4},{16,24},{20,28},{24,16},{28,20},{1,9},{5... | collective-permute-start | bytes 368648 | tf_op jit(solution)/shard_map/ppermute | solution.py:403
  108.2 11.2 %collective-permute-start.15 = (bf16[480,128]{1,0:T(8,128)(2,1)S(1)}, bf16[480,128]{1,0:T(8,128)(2,1)S(1)}, u32[]{:S(2)}, u32[]{:S(2)}) collective-permute-start(bf16[480,128]{1,0:T(8,128)(2,1)S(1)} %shard_map.103), channel_id=1, source_target_pairs={{0,16},{4,20},{8,24},{12,28},{16,0},{20,4},{24,8},{28,12},{1,17},{... | collective-permute-start | bytes 368648 | tf_op jit(solution)/shard_map/ppermute | solution.py:403
  108.2 11.3 %collective-permute-start.16 = (bf16[480,128]{1,0:T(8,128)(2,1)S(1)}, bf16[480,128]{1,0:T(8,128)(2,1)S(1)}, u32[]{:S(2)}, u32[]{:S(2)}) collective-permute-start(bf16[480,128]{1,0:T(8,128)(2,1)S(1)} %shard_map.103), channel_id=1, source_target_pairs={{0,24},{4,28},{8,16},{12,20},{16,8},{20,12},{24,0},{28,4},{1,25},{... | collective-permute-start | bytes 368648 | tf_op jit(solution)/shard_map/ppermute | solution.py:403
  110.7 0.9 copy-start.5
  121.3 1.9 %collective-permute-start.19 = (bf16[2,4,2,24,640]{4,3,2,1,0:T(8,128)(2,1)S(1)}, bf16[2,4,2,24,640]{4,3,2,1,0:T(8,128)(2,1)S(1)}, u32[]{:S(2)}, u32[]{:S(2)}) collective-permute-start(bf16[2,4,2,24,640]{4,3,2,1,0:T(8,128)(2,1)S(1)} %get-tuple-element.87), channel_id=1, source_target_pairs={{0,1},{1,0},{2,3},{3,2},{4,5},{5,4},{6,7},{7,6},{8,9},{9,8},{10,11... | collective-permute-start | bytes 1474568 | tf_op jit(solution)/shard_map/ppermute | solution.py:406
  123.4 5.4 %collective-permute-start.20 = (bf16[4,24,640]{2,1,0:T(8,128)(2,1)S(1)}, bf16[4,24,640]{2,1,0:T(8,128)(2,1)S(1)}, u32[]{:S(2)}, u32[]{:S(2)}) collective-permute-start(bf16[4,24,640]{2,1,0:T(8,128)(2,1)S(1)} %get-tuple-element.80), channel_id=1, source_target_pairs={{0,2},{1,3},{2,0},{3,1},{4,6},{5,7},{6,4},{7,5},{8,10},{9,11},{10,... | collective-permute-start | bytes 368648 | tf_op jit(solution)/shard_map/ppermute | solution.py:406
  128.9 4.5 %collective-permute-start.21 = (bf16[24,640]{1,0:T(8,128)(2,1)S(1)}, bf16[24,640]{1,0:T(8,128)(2,1)S(1)}, u32[]{:S(2)}, u32[]{:S(2)}) collective-permute-start(bf16[24,640]{1,0:T(8,128)(2,1)S(1)} %get-tuple-element.82), channel_id=1, source_target_pairs={{0,8},{4,12},{8,0},{12,4},{16,24},{20,28},{24,16},{28,20},{1,9},{5... | collective-permute-start | bytes 92168 | tf_op jit(solution)/shard_map/ppermute | solution.py:403
  130.9 4.8 %collective-permute-start.22 = (bf16[24,640]{1,0:T(8,128)(2,1)S(1)}, bf16[24,640]{1,0:T(8,128)(2,1)S(1)}, u32[]{:S(2)}, u32[]{:S(2)}) collective-permute-start(bf16[24,640]{1,0:T(8,128)(2,1)S(1)} %get-tuple-element.83), channel_id=1, source_target_pairs={{0,16},{4,20},{8,24},{12,28},{16,0},{20,4},{24,8},{28,12},{1,17},{... | collective-permute-start | bytes 92168 | tf_op jit(solution)/shard_map/ppermute | solution.py:403
  131.0 5.7 %collective-permute-start.23 = (bf16[24,640]{1,0:T(8,128)(2,1)S(1)}, bf16[24,640]{1,0:T(8,128)(2,1)S(1)}, u32[]{:S(2)}, u32[]{:S(2)}) collective-permute-start(bf16[24,640]{1,0:T(8,128)(2,1)S(1)} %get-tuple-element.84), channel_id=1, source_target_pairs={{0,24},{4,28},{8,16},{12,20},{16,8},{20,12},{24,0},{28,4},{1,25},{... | collective-permute-start | bytes 92168 | tf_op jit(solution)/shard_map/ppermute | solution.py:403
